TPU v7x, 32 devices: a whole 2x2x4 slice. The times are simulated.
32 devices in a mesh: bunch: 8 (over y, x, core), tile: 4 (over z).
Axes of the slice: x: 2, y: 2, z: 4, core: 2. Of those that a mesh axis runs over, the one named last changes fastest.
Arguments:
- cell_index: int32 [2, 8, 2, 4096], P(None, 'bunch', None, 'tile'), may hold values from 0 to 255
- charges: bfloat16 [2, 8, 4096], P(None, 'bunch', 'tile'), may hold values from 0.5 to 2
- momenta: float32 [2, 8, 2, 4096], P(None, 'bunch', None, 'tile'), may hold values from -6 to 6
- fill_pattern: int32 [2, 8], P(None, 'bunch'), may hold values 0 or 1
- encounters: int32 [4, 2, 2, 8], P(None, None, None, 'bunch'), may hold values 0 or 1
- green_spectrum: float32 [256, 256], P(None, 'tile'), may hold values from 0.5 to 4
- stop_gain: float32 [4], replicated, may hold values from 0.5 to 2
- parasitic_gain: float32 [4], replicated, may hold values from 0.25 to 1
Outputs:
- kicked: float32 [2, 8, 2, 4096], P(None, 'bunch', None, 'tile')
All inputs are finite; a program needn't handle non-finite values. No bound on the sum of `fill_pattern` or of `encounters` on one device may be relied on, other than what follows from the above.
Results may differ from a plain program's by a relative error of at most 0.0037.
Values may be sent and summed in bfloat16 or wider, within the bound.
No kernel may reach another device: no remote copies, remote signals or barrier semaphores. Data moves between devices by JAX's collectives and lax.ppermute only.
A program may use at most 128 MiB of HBM per device.

v0:
```python
import functools
import math

import jax
import jax.numpy as jnp
import ml_dtypes
import numpy as np
from jax import lax
from jax.experimental import pallas as pl
from jax.experimental.pallas import tpu as pltpu
from jax.sharding import PartitionSpec as P

GRID = 256
HALF = GRID // 2
STOPS = 4
OFFSET_CELLS = 32
BANDS = GRID // OFFSET_CELLS
REACH = STOPS + 1
f32 = jnp.float32
bf16 = jnp.bfloat16


def split_table(table):
    high = table.astype(ml_dtypes.bfloat16)
    low = (table - high.astype(np.float64)).astype(ml_dtypes.bfloat16)
    return np.stack([high, low])


@functools.cache
def make_tables():
    cells = np.arange(GRID)
    wave = np.where(cells <= HALF, cells, cells - HALF)
    is_sin = cells > HALF
    angle = 2 * np.pi * ((cells[:, None] * wave[None, :]) % GRID) / GRID
    basis = np.where(is_sin[None, :], np.sin(angle), np.cos(angle))
    slope = -0.5 * (np.roll(basis, -1, 0) - np.roll(basis, 1, 0))
    order = OFFSET_CELLS * (cells % BANDS) + cells // BANDS
    here = (cells[None, :] == wave[:, None]).astype(np.float64)
    there = (cells[None, :] == (-wave[:, None]) % GRID).astype(np.float64)
    count = np.where((wave == 0) | (wave == HALF), 1.0, 2.0)[:, None] / GRID
    sign = np.where(is_sin, -1.0, 1.0)[:, None]
    even = 0.5 * (here + there) * count
    odd = 0.5 * (here - there) * count
    tables = np.stack(
        [
            split_table(basis.T),
            split_table(basis),
            split_table(slope.T),
            split_table(basis[order]),
            split_table(slope[order]),
        ]
    )
    mixers = np.stack([even, even, odd * sign, -odd * sign]).astype(ml_dtypes.bfloat16)
    return tables, mixers


def dot(a, b):
    return jnp.dot(a, b, preferred_element_type=f32)


def dot_nt(a, b):
    return lax.dot_general(a, b, (((1,), (1,)), ((), ())), preferred_element_type=f32)


def halves(x):
    high = x.astype(bf16)
    return high, (x - high.astype(f32)).astype(bf16)


def pack_kernel(cells, charges, fill, marks, gains, strengths, out, first, second):
    for beam in range(2):
        parts = [
            charges[beam].astype(f32) * fill[beam, 0].astype(f32),
            cells[beam, 0, 0:1, :].astype(f32),
            cells[beam, 0, 1:2, :].astype(f32),
        ]
        width = parts[0].shape[1] // 8
        weights = []
        for offset in range(1, REACH):
            stop = offset - 1
            mark = marks[stop, beam, 0, 0].astype(f32)
            weights.append(gains[stop] * strengths[stop] * mark)
        for offset in range(STOPS - 1):
            stop = offset + 1
            mark = marks[stop, beam, 1, 0].astype(f32)
            weights.append(gains[stop] * strengths[stop] * mark)
        weights.append(jnp.float32(0))
        own = first if beam == 0 else second
        for row, value in enumerate(parts):
            out[4 * beam + row : 4 * beam + row + 1, :] = value
            own[row : row + 1, :] = value
        for group, weight in enumerate(weights):
            value = jnp.full((1, width), weight, f32)
            out[4 * beam + 3 : 4 * beam + 4, group * width : (group + 1) * width] = value
            own[3:4, group * width : (group + 1) * width] = value


def field_kernel(tiles, index, *refs):
    packs = refs[:tiles]
    greens = refs[tiles : 2 * tiles]
    tables, mixers, out = refs[2 * tiles :]
    columns = greens[0].shape[1]
    gains = []
    for which in (0, 2):
        total = jnp.zeros((GRID, GRID), f32)
        for step in range(tiles):
            owner = lax.rem(index[0] - step + tiles, tiles)
            start = pl.multiple_of(owner * columns, columns)
            high, low = halves(greens[step][...])
            rest = greens[step][...] - high.astype(f32) - low.astype(f32)
            pieces = (high, low, rest.astype(bf16))
            left = mixers[which + 1]
            turned = sum(dot(left, piece) for piece in pieces)
            high, low = halves(turned)
            last = (turned - high.astype(f32) - low.astype(f32)).astype(bf16)
            columns_side = mixers[4 + which // 2, pl.ds(start, columns), :]
            for piece in (high, low, last):
                total = total + lax.dot_general(
                    columns_side, piece, (((0,), (1,)), ((), ())), preferred_element_type=f32
                )
        gains.append(total)
    alpha, beta = gains
    particles = packs[0].shape[1]
    cells = lax.broadcasted_iota(jnp.int32, (GRID, particles), 0).astype(f32)
    for beam in range(2):
        density = jnp.zeros((GRID, GRID), f32)
        for step in range(tiles):
            base = 4 * beam
            charge = packs[step][base : base + 1, :]
            rows = packs[step][base + 1 : base + 2, :]
            cols = packs[step][base + 2 : base + 3, :]
            row_hot = jnp.where(cells == rows, 1.0, 0.0).astype(bf16)
            col_hot = jnp.where(cells == cols, charge, 0.0).astype(bf16)
            density = density + dot_nt(col_hot, row_hot)
        high, low = halves(density)
        first = dot(tables[0, 0], high) + dot(tables[0, 0], low) + dot(tables[0, 1], high)
        high, low = halves(first)
        spectrum = dot(high, tables[1, 0]) + dot(low, tables[1, 0]) + dot(high, tables[1, 1])
        swapped = jnp.concatenate(
            [
                jnp.concatenate([spectrum[HALF:, HALF:], spectrum[HALF:, :HALF]], axis=1),
                jnp.concatenate([spectrum[:HALF, HALF:], spectrum[:HALF, :HALF]], axis=1),
            ],
            axis=0,
        )
        scaled = alpha * spectrum + beta * swapped
        high, low = halves(scaled)
        for axis, (inner, outer) in enumerate(((2, 3), (0, 4))):
            part = (
                dot(high, tables[inner, 0])
                + dot(low, tables[inner, 0])
                + dot(high, tables[inner, 1])
            )
            top, bottom = halves(part)
            field = (
                dot(tables[outer, 0], top) + dot(tables[outer, 0], bottom) + dot(tables[outer, 1], top)
            )
            out[beam, axis * GRID : (axis + 1) * GRID, :] = field.astype(bf16)


def kick_kernel(count, index, gains, *refs):
    fields = refs[0]
    queries = (refs[1 : 1 + REACH], refs[1 + REACH : 1 + 2 * REACH])
    out = refs[1 + 2 * REACH]
    particles = queries[0][0].shape[1]
    width = particles // 8
    here = index[0]
    block = 2 * width
    cells = lax.broadcasted_iota(jnp.int32, (GRID, block), 0).astype(f32)
    bands = lax.broadcasted_iota(jnp.int32, (BANDS, block), 0).astype(f32)
    for offset in reversed(range(REACH)):
        for beam in range(2):
            sign = 1 if beam == 0 else -1
            target = lax.rem(here - sign * offset + count, count)
            source = queries[beam][offset]
            middle = gains[offset] if offset < STOPS else None
            up = source[3:4, (offset - 1) * width : offset * width] if offset else None
            down = source[3:4, (offset + 4) * width : (offset + 5) * width] if offset < STOPS - 1 else None
            for start in range(0, particles, block):
                rows = source[1:2, start : start + block]
                cols = source[2:3, start : start + block]
                band = jnp.floor(cols * (1.0 / OFFSET_CELLS))
                inside = cols - band * OFFSET_CELLS
                hot = jnp.where(cells == rows, 1.0, 0.0).astype(bf16)
                values = dot(fields[1 - beam], hot)
                picked = [jnp.zeros((BANDS, block), f32) for _ in range(2)]
                for place in range(OFFSET_CELLS):
                    hit = jnp.broadcast_to(inside == place, (BANDS, block))
                    for axis in range(2):
                        at = axis * GRID + place * BANDS
                        picked[axis] = jnp.where(hit, values[at : at + BANDS, :], picked[axis])
                weight = jnp.zeros((BANDS, block), f32)
                if middle is not None:
                    weight = jnp.where(bands == band, middle, weight)
                if up is not None:
                    weight = jnp.where(bands == band - 1, jnp.concatenate([up, up], axis=1), weight)
                if down is not None:
                    weight = jnp.where(bands == band + 1, jnp.concatenate([down, down], axis=1), weight)
                for axis in range(2):
                    kick = jnp.sum(weight * picked[axis], axis=0, keepdims=True)
                    out[target, 2 * beam + axis : 2 * beam + axis + 1, start : start + block] = kick


def final_kernel(count, index, received, momenta, out):
    here = index[0]
    for beam in range(2):
        sign = 1 if beam == 0 else -1
        for axis in range(2):
            total = None
            for offset in range(REACH):
                source = lax.rem(here + sign * offset + count, count)
                part = received[source, 2 * beam + axis : 2 * beam + axis + 1, :]
                total = part if total is None else total + part
            out[beam, 0, axis : axis + 1, :] = momenta[beam, 0, axis : axis + 1, :] + total.astype(
                bf16
            ).astype(f32)


SMEM = pl.BlockSpec(memory_space=pltpu.SMEM)
VMEM = pl.BlockSpec(memory_space=pltpu.VMEM)
LIMIT = pltpu.CompilerParams(vmem_limit_bytes=48 * 1024 * 1024)


def shifted(value, axis, steps):
    count = lax.axis_size(axis)
    return lax.ppermute(value, axis, [(i, (i + steps) % count) for i in range(count)])


def body(cell_index, charges, momenta, fill_pattern, encounters, green_spectrum, stop_gain, parasitic_gain):
    particles = cell_index.shape[3]
    tiles = lax.axis_size("tile")
    count = lax.axis_size("bunch")
    tables, mixers = make_tables()
    mixers = np.concatenate([mixers, np.stack([mixers[0].T, mixers[2].T])])
    bunch = lax.axis_index("bunch").astype(jnp.int32).reshape(1)
    tile = lax.axis_index("tile").astype(jnp.int32).reshape(1)
    pack, first, second = pl.pallas_call(
        pack_kernel,
        out_shape=(
            jax.ShapeDtypeStruct((8, particles), f32),
            jax.ShapeDtypeStruct((4, particles), f32),
            jax.ShapeDtypeStruct((4, particles), f32),
        ),
        in_specs=[VMEM, VMEM, SMEM, SMEM, SMEM, SMEM],
        out_specs=(VMEM, VMEM, VMEM),
    )(cell_index, charges, fill_pattern, encounters, stop_gain, parasitic_gain)
    packs = [pack] + [shifted(pack, "tile", step) for step in range(1, tiles)]
    greens = [green_spectrum] + [shifted(green_spectrum, "tile", step) for step in range(1, tiles)]
    from_first = [first] + [shifted(first, "bunch", offset) for offset in range(1, REACH)]
    from_second = [second] + [shifted(second, "bunch", -offset) for offset in range(1, REACH)]
    fields = pl.pallas_call(
        functools.partial(field_kernel, tiles),
        out_shape=jax.ShapeDtypeStruct((2, 2 * GRID, GRID), bf16),
        in_specs=[SMEM] + [VMEM] * (2 * tiles + 2),
        out_specs=VMEM,
        compiler_params=LIMIT,
    )(tile, *packs, *greens, jnp.asarray(tables), jnp.asarray(mixers))
    kicks = pl.pallas_call(
        functools.partial(kick_kernel, count),
        out_shape=jax.ShapeDtypeStruct((count, 4, particles), f32),
        in_specs=[SMEM, SMEM] + [VMEM] * (1 + 2 * REACH),
        out_specs=VMEM,
        compiler_params=LIMIT,
    )(bunch, stop_gain, fields, *from_first, *from_second)
    received = lax.all_to_all(kicks, "bunch", split_axis=0, concat_axis=0, tiled=True)
    return pl.pallas_call(
        functools.partial(final_kernel, count),
        out_shape=jax.ShapeDtypeStruct(momenta.shape, f32),
        in_specs=[SMEM, VMEM, VMEM],
        out_specs=VMEM,
    )(bunch, received, momenta)


def solution(mesh):
    in_specs = (
        P(None, "bunch", None, "tile"),
        P(None, "bunch", "tile"),
        P(None, "bunch", None, "tile"),
        P(None, "bunch"),
        P(None, None, None, "bunch"),
        P(None, "tile"),
        P(),
        P(),
    )
    out_specs = P(None, "bunch", None, "tile")
    return jax.shard_map(body, mesh=mesh, in_specs=in_specs, out_specs=out_specs, check_vma=False)
```

profile of v0, /device:TPU:0, one launch (start us, length us, event | category | flops | bytes accessed | tf_op | source)
XLA Modules:
  0.0 59.0 jit_solution(14204502263716977391)
XLA Ops:
  0.0 1.3 %copy.11.charges = bf16[2,1,1024]{2,1,0:T(2,128)(2,1)} copy(bf16[2,1,1024]{2,0,1:T(2,128)(2,1)} %param.11) | data formatting | bytes 8192 | tf_op args[1]
  1.3 1.4 %copy.13.marks = s32[4,2,2,1]{3,2,1,0:T(2,128)} copy(s32[4,2,2,1]{0,3,2,1:T(1,128)} %param.14) | data formatting | bytes 128 | tf_op args[4]
  2.7 1.3 %copy.12.fill = s32[2,1]{1,0:T(2,128)} copy(s32[2,1]{0,1:T(1,128)} %param.13) | data formatting | bytes 16 | tf_op args[3]
  4.0 1.6 %shard_map.100 = (f32[8,1024]{1,0:T(8,128)}, f32[4,1024]{1,0:T(4,128)}, f32[4,1024]{1,0:T(4,128)}) custom-call(s32[2,1,2,1024]{3,2,1,0:T(2,128)} %cells.1, bf16[2,1,1024]{2,1,0:T(2,128)(2,1)} %copy.11.charges, s32[2,1]{1,0:T(2,128)} %copy.12.fill, s32[4,2,2,1]{3,2,1,0:T(2,128)} %copy.13.marks, f32[4]{0:T(128)} %gains.3, f32[4]{0:T(128)} %strengths.1), custom_call_target="tpu_custom_call" | custom-call | tf_op jit(solution)/shard_map/pallas_call | solution.py:237
  5.6 3.3 %collective-permute-start.10 = (f32[4,1024]{1,0:T(4,128)}, f32[4,1024]{1,0:T(4,128)S(1)}, u32[]{:S(2)}, u32[]{:S(2)}) collective-permute-start(f32[4,1024]{1,0:T(4,128)} %get-tuple-element.10.refs_6_), channel_id=1, source_target_pairs={{0,28},{4,0},{8,4},{12,8},{16,12},{20,16},{24,20},{28,24},{1,29},{... | collective-permute-start | bytes 49160 | tf_op jit(solution)/shard_map/ppermute | solution.py:226
  8.9 0.6 collective-permute-start.11
  9.5 1.6 %collective-permute-start = (f32[8,1024]{1,0:T(8,128)}, f32[8,1024]{1,0:T(8,128)S(1)}, u32[]{:S(2)}, u32[]{:S(2)}) collective-permute-start(f32[8,1024]{1,0:T(8,128)} %get-tuple-element.8.refs_0_), channel_id=1, source_target_pairs={{0,1},{1,2},{2,3},{3,0},{4,5},{5,6},{6,7},{7,4},{8,9},{9,10},{10,1... | collective-permute-start | bytes 98312 | tf_op jit(solution)/shard_map/ppermute | solution.py:226
  11.1 0.9 %copy.17.refs_4_ = f32[256,64]{1,0:T(8,128)S(1)} copy(f32[256,64]{0,1:T(8,128)} %param.15) | data formatting | bytes 131072 | tf_op args[5]
  12.0 1.6 %collective-permute-start.3 = (f32[256,64]{1,0:T(8,128)S(1)}, f32[256,64]{1,0:T(8,128)S(1)}, u32[]{:S(2)}, u32[]{:S(2)}) collective-permute-start(f32[256,64]{1,0:T(8,128)S(1)} %copy.17.refs_4_), channel_id=1, source_target_pairs={{0,1},{1,2},{2,3},{3,0},{4,5},{5,6},{6,7},{7,4},{8,9},{9,10},{10,1... | collective-permute-start | bytes 196616 | tf_op jit(solution)/shard_map/ppermute | solution.py:226
  13.6 1.2 %collective-permute-start.4 = (f32[256,64]{1,0:T(8,128)S(1)}, f32[256,64]{1,0:T(8,128)S(1)}, u32[]{:S(2)}, u32[]{:S(2)}) collective-permute-start(f32[256,64]{1,0:T(8,128)S(1)} %copy.17.refs_4_), channel_id=1, source_target_pairs={{0,2},{1,3},{2,0},{3,1},{4,6},{5,7},{6,4},{7,5},{8,10},{9,11},{10,... | collective-permute-start | bytes 196616 | tf_op jit(solution)/shard_map/ppermute | solution.py:226
  14.9 0.0 collective-permute-done.10.refs_7_
  14.9 2.7 %collective-permute-start.5 = (f32[256,64]{1,0:T(8,128)S(1)}, f32[256,64]{1,0:T(8,128)S(1)}, u32[]{:S(2)}, u32[]{:S(2)}) collective-permute-start(f32[256,64]{1,0:T(8,128)S(1)} %copy.17.refs_4_), channel_id=1, source_target_pairs={{0,3},{1,0},{2,1},{3,2},{4,7},{5,4},{6,5},{7,6},{8,11},{9,8},{10,9... | collective-permute-start | bytes 196616 | tf_op jit(solution)/shard_map/ppermute | solution.py:226
  17.6 0.0 collective-permute-done.11.refs_8_
  17.6 0.0 collective-permute-start.12
  17.6 3.4 %collective-permute-done.12.refs_9_ = f32[4,1024]{1,0:T(4,128)S(1)} collective-permute-done((f32[4,1024]{1,0:T(4,128)}, f32[4,1024]{1,0:T(4,128)S(1)}, u32[]{:S(2)}, u32[]{:S(2)}) %collective-permute-start.12) | collective-permute-done | bytes 16416 | tf_op jit(solution)/shard_map/ppermute | solution.py:226
  20.9 0.3 collective-permute-start.1
  21.3 0.0 collective-permute-done.refs_1_
  21.3 1.3 %collective-permute-start.2 = (f32[8,1024]{1,0:T(8,128)}, f32[8,1024]{1,0:T(8,128)S(1)}, u32[]{:S(2)}, u32[]{:S(2)}) collective-permute-start(f32[8,1024]{1,0:T(8,128)} %get-tuple-element.8.refs_0_), channel_id=1, source_target_pairs={{0,3},{1,0},{2,1},{3,2},{4,7},{5,4},{6,5},{7,6},{8,11},{9,8},{10,9... | collective-permute-start | bytes 98312 | tf_op jit(solution)/shard_map/ppermute | solution.py:226
  22.6 6.5 %collective-permute-done.1.refs_2_ = f32[8,1024]{1,0:T(8,128)S(1)} collective-permute-done((f32[8,1024]{1,0:T(8,128)}, f32[8,1024]{1,0:T(8,128)S(1)}, u32[]{:S(2)}, u32[]{:S(2)}) %collective-permute-start.1) | collective-permute-done | bytes 32800 | tf_op jit(solution)/shard_map/ppermute | solution.py:226
  29.1 0.5 collective-permute-start.13
  29.6 0.0 collective-permute-done.2.refs_3_
  29.6 0.0 collective-permute-start.6
  29.6 0.0 collective-permute-done.3.refs_5_
  29.6 0.6 %collective-permute-start.7 = (f32[4,1024]{1,0:T(4,128)}, f32[4,1024]{1,0:T(4,128)S(1)}, u32[]{:S(2)}, u32[]{:S(2)}) collective-permute-start(f32[4,1024]{1,0:T(4,128)} %get-tuple-element.9.refs_1_), channel_id=1, source_target_pairs={{0,8},{4,12},{8,16},{12,20},{16,24},{20,28},{24,0},{28,4},{1,9},{5... | collective-permute-start | bytes 49160 | tf_op jit(solution)/shard_map/ppermute | solution.py:226
  30.3 0.0 collective-permute-done.4.refs_6_
  30.3 2.1 %collective-permute-start.8 = (f32[4,1024]{1,0:T(4,128)}, f32[4,1024]{1,0:T(4,128)S(1)}, u32[]{:S(2)}, u32[]{:S(2)}) collective-permute-start(f32[4,1024]{1,0:T(4,128)} %get-tuple-element.9.refs_1_), channel_id=1, source_target_pairs={{0,12},{4,16},{8,20},{12,24},{16,28},{20,0},{24,4},{28,8},{1,13},{... | collective-permute-start | bytes 49160 | tf_op jit(solution)/shard_map/ppermute | solution.py:226
  32.4 0.0 collective-permute-done.5.refs_7_
  32.4 0.8 %collective-permute-start.9 = (f32[4,1024]{1,0:T(4,128)}, f32[4,1024]{1,0:T(4,128)S(1)}, u32[]{:S(2)}, u32[]{:S(2)}) collective-permute-start(f32[4,1024]{1,0:T(4,128)} %get-tuple-element.9.refs_1_), channel_id=1, source_target_pairs={{0,16},{4,20},{8,24},{12,28},{16,0},{20,4},{24,8},{28,12},{1,17},{... | collective-permute-start | bytes 49160 | tf_op jit(solution)/shard_map/ppermute | solution.py:226
  33.2 0.0 copy-start
  33.2 1.3 %copy-done = bf16[5,2,256,256]{3,2,1,0:T(8,128)(2,1)S(1)} copy-done((bf16[5,2,256,256]{3,2,1,0:T(8,128)(2,1)S(1)}, bf16[5,2,256,256]{3,2,1,0:T(8,128)(2,1)}, u32[]{:S(2)}) %copy-start) | copy-done | bytes 1310744
  34.5 0.0 copy-start.1
  34.5 1.1 %copy-done.1 = bf16[6,256,256]{2,1,0:T(8,128)(2,1)S(1)} copy-done((bf16[6,256,256]{2,1,0:T(8,128)(2,1)S(1)}, bf16[6,256,256]{2,1,0:T(8,128)(2,1)}, u32[]{:S(2)}) %copy-start.1) | copy-done | bytes 786456
  35.6 0.0 copy-start.2
  35.6 0.8 %copy-done.2 = f32[8,1024]{1,0:T(8,128)S(1)} copy-done((f32[8,1024]{1,0:T(8,128)S(1)}, f32[8,1024]{1,0:T(8,128)}, u32[]{:S(2)}) %copy-start.2) | copy-done | bytes 32792
  36.4 0.0 copy-start.3
  36.4 0.0 copy-start.4
  36.4 0.0 copy-start.5
  36.4 7.2 %shard_map.101.refs_0_ = bf16[2,512,256]{2,1,0:T(8,128)(2,1)S(1)} custom-call(s32[1]{0:T(128)} %bitcast.1.index, f32[8,1024]{1,0:T(8,128)S(1)} %copy-done.2, f32[8,1024]{1,0:T(8,128)S(1)} %collective-permute-done.refs_1_, f32[8,1024]{1,0:T(8,128)S(1)} %collective-permute-done.1.refs_2_, f32[8,1024]{1,0:T(8,128)S(1)} %collective-permute-done.2.refs_3_, ...), custom_call_target="tpu_custom_call" | custom-call | tf_op jit(solution)/shard_map/pallas_call | solution.py:251
  43.6 0.0 collective-permute-done.13.refs_10_
  43.6 0.0 collective-permute-done.6.refs_2_
  43.6 0.0 collective-permute-done.7.refs_3_
  43.6 0.0 collective-permute-done.8.refs_4_
  43.7 0.0 collective-permute-done.9.refs_5_
  43.7 0.0 copy-done.3
  43.7 0.0 copy-done.4
  43.7 0.0 copy-done.5
  43.7 4.7 %shard_map.102 = f32[8,4,1024]{2,1,0:T(4,128)S(1)} custom-call(s32[1]{0:T(128)} %bitcast.index, f32[4]{0:T(128)S(1)} %copy-done.5, bf16[2,512,256]{2,1,0:T(8,128)(2,1)S(1)} %shard_map.101.refs_0_, f32[4,1024]{1,0:T(4,128)S(1)} %copy-done.3, f32[4,1024]{1,0:T(4,128)S(1)} %collective-permute-done.6.refs_2_, f32[4,1024]{1,0:T(4,128)S(1)} %collective-permute-done.7.refs_3_, ...), custom_call_target="tpu_custom_call" | custom-call | tf_op jit(solution)/shard_map/pallas_call | solution.py:258
  48.4 9.1 %all_to_all.5.received = f32[8,4,1024]{2,1,0:T(4,128)} all-to-all(f32[8,4,1024]{2,1,0:T(4,128)S(1)} %shard_map.102), channel_id=1, replica_groups=mesh['bunch'=8,'tile'=4] {'bunch'}, dimensions={0} | all-to-all | bytes 262144 | tf_op jit(solution)/shard_map/all_to_all | solution.py:265
  57.5 1.5 %shard_map.103 = f32[2,1,2,1024]{3,2,1,0:T(2,128)} custom-call(s32[1]{0:T(128)} %bitcast.index, f32[8,4,1024]{2,1,0:T(4,128)} %all_to_all.5.received, f32[2,1,2,1024]{3,2,1,0:T(2,128)} %momenta.1), custom_call_target="tpu_custom_call" | custom-call | tf_op jit(solution)/shard_map/pallas_call | solution.py:266
Async XLA Ops:
  5.6 9.3 %collective-permute-start.10 = (f32[4,1024]{1,0:T(4,128)}, f32[4,1024]{1,0:T(4,128)S(1)}, u32[]{:S(2)}, u32[]{:S(2)}) collective-permute-start(f32[4,1024]{1,0:T(4,128)} %get-tuple-element.10.refs_6_), channel_id=1, source_target_pairs={{0,28},{4,0},{8,4},{12,8},{16,12},{20,16},{24,20},{28,24},{1,29},{... | collective-permute-start | bytes 49160 | tf_op jit(solution)/shard_map/ppermute | solution.py:226
  8.9 8.6 %collective-permute-start.11 = (f32[4,1024]{1,0:T(4,128)}, f32[4,1024]{1,0:T(4,128)S(1)}, u32[]{:S(2)}, u32[]{:S(2)}) collective-permute-start(f32[4,1024]{1,0:T(4,128)} %get-tuple-element.10.refs_6_), channel_id=1, source_target_pairs={{0,24},{4,28},{8,0},{12,4},{16,8},{20,12},{24,16},{28,20},{1,25},{... | collective-permute-start | bytes 49160 | tf_op jit(solution)/shard_map/ppermute | solution.py:226
  9.5 11.8 %collective-permute-start = (f32[8,1024]{1,0:T(8,128)}, f32[8,1024]{1,0:T(8,128)S(1)}, u32[]{:S(2)}, u32[]{:S(2)}) collective-permute-start(f32[8,1024]{1,0:T(8,128)} %get-tuple-element.8.refs_0_), channel_id=1, source_target_pairs={{0,1},{1,2},{2,3},{3,0},{4,5},{5,6},{6,7},{7,4},{8,9},{9,10},{10,1... | collective-permute-start | bytes 98312 | tf_op jit(solution)/shard_map/ppermute | solution.py:226
  12.0 17.6 %collective-permute-start.3 = (f32[256,64]{1,0:T(8,128)S(1)}, f32[256,64]{1,0:T(8,128)S(1)}, u32[]{:S(2)}, u32[]{:S(2)}) collective-permute-start(f32[256,64]{1,0:T(8,128)S(1)} %copy.17.refs_4_), channel_id=1, source_target_pairs={{0,1},{1,2},{2,3},{3,0},{4,5},{5,6},{6,7},{7,4},{8,9},{9,10},{10,1... | collective-permute-start | bytes 196616 | tf_op jit(solution)/shard_map/ppermute | solution.py:226
  13.6 16.7 %collective-permute-start.4 = (f32[256,64]{1,0:T(8,128)S(1)}, f32[256,64]{1,0:T(8,128)S(1)}, u32[]{:S(2)}, u32[]{:S(2)}) collective-permute-start(f32[256,64]{1,0:T(8,128)S(1)} %copy.17.refs_4_), channel_id=1, source_target_pairs={{0,2},{1,3},{2,0},{3,1},{4,6},{5,7},{6,4},{7,5},{8,10},{9,11},{10,... | collective-permute-start | bytes 196616 | tf_op jit(solution)/shard_map/ppermute | solution.py:226
  14.9 17.5 %collective-permute-start.5 = (f32[256,64]{1,0:T(8,128)S(1)}, f32[256,64]{1,0:T(8,128)S(1)}, u32[]{:S(2)}, u32[]{:S(2)}) collective-permute-start(f32[256,64]{1,0:T(8,128)S(1)} %copy.17.refs_4_), channel_id=1, source_target_pairs={{0,3},{1,0},{2,1},{3,2},{4,7},{5,4},{6,5},{7,6},{8,11},{9,8},{10,9... | collective-permute-start | bytes 196616 | tf_op jit(solution)/shard_map/ppermute | solution.py:226
  17.6 3.4 %collective-permute-start.12 = (f32[4,1024]{1,0:T(4,128)}, f32[4,1024]{1,0:T(4,128)S(1)}, u32[]{:S(2)}, u32[]{:S(2)}) collective-permute-start(f32[4,1024]{1,0:T(4,128)} %get-tuple-element.10.refs_6_), channel_id=1, source_target_pairs={{0,20},{4,24},{8,28},{12,0},{16,4},{20,8},{24,12},{28,16},{1,21},{... | collective-permute-start | bytes 49160 | tf_op jit(solution)/shard_map/ppermute | solution.py:226
  20.9 8.2 %collective-permute-start.1 = (f32[8,1024]{1,0:T(8,128)}, f32[8,1024]{1,0:T(8,128)S(1)}, u32[]{:S(2)}, u32[]{:S(2)}) collective-permute-start(f32[8,1024]{1,0:T(8,128)} %get-tuple-element.8.refs_0_), channel_id=1, source_target_pairs={{0,2},{1,3},{2,0},{3,1},{4,6},{5,7},{6,4},{7,5},{8,10},{9,11},{10,... | collective-permute-start | bytes 98312 | tf_op jit(solution)/shard_map/ppermute | solution.py:226
  21.3 8.3 %collective-permute-start.2 = (f32[8,1024]{1,0:T(8,128)}, f32[8,1024]{1,0:T(8,128)S(1)}, u32[]{:S(2)}, u32[]{:S(2)}) collective-permute-start(f32[8,1024]{1,0:T(8,128)} %get-tuple-element.8.refs_0_), channel_id=1, source_target_pairs={{0,3},{1,0},{2,1},{3,2},{4,7},{5,4},{6,5},{7,6},{8,11},{9,8},{10,9... | collective-permute-start | bytes 98312 | tf_op jit(solution)/shard_map/ppermute | solution.py:226
  29.1 14.5 %collective-permute-start.13 = (f32[4,1024]{1,0:T(4,128)}, f32[4,1024]{1,0:T(4,128)S(1)}, u32[]{:S(2)}, u32[]{:S(2)}) collective-permute-start(f32[4,1024]{1,0:T(4,128)} %get-tuple-element.10.refs_6_), channel_id=1, source_target_pairs={{0,16},{4,20},{8,24},{12,28},{16,0},{20,4},{24,8},{28,12},{1,17},{... | collective-permute-start | bytes 49160 | tf_op jit(solution)/shard_map/ppermute | solution.py:226
  29.6 14.0 %collective-permute-start.6 = (f32[4,1024]{1,0:T(4,128)}, f32[4,1024]{1,0:T(4,128)S(1)}, u32[]{:S(2)}, u32[]{:S(2)}) collective-permute-start(f32[4,1024]{1,0:T(4,128)} %get-tuple-element.9.refs_1_), channel_id=1, source_target_pairs={{0,4},{4,8},{8,12},{12,16},{16,20},{20,24},{24,28},{28,0},{1,5},{5... | collective-permute-start | bytes 49160 | tf_op jit(solution)/shard_map/ppermute | solution.py:226
  29.6 14.0 %collective-permute-start.7 = (f32[4,1024]{1,0:T(4,128)}, f32[4,1024]{1,0:T(4,128)S(1)}, u32[]{:S(2)}, u32[]{:S(2)}) collective-permute-start(f32[4,1024]{1,0:T(4,128)} %get-tuple-element.9.refs_1_), channel_id=1, source_target_pairs={{0,8},{4,12},{8,16},{12,20},{16,24},{20,28},{24,0},{28,4},{1,9},{5... | collective-permute-start | bytes 49160 | tf_op jit(solution)/shard_map/ppermute | solution.py:226
  30.3 13.4 %collective-permute-start.8 = (f32[4,1024]{1,0:T(4,128)}, f32[4,1024]{1,0:T(4,128)S(1)}, u32[]{:S(2)}, u32[]{:S(2)}) collective-permute-start(f32[4,1024]{1,0:T(4,128)} %get-tuple-element.9.refs_1_), channel_id=1, source_target_pairs={{0,12},{4,16},{8,20},{12,24},{16,28},{20,0},{24,4},{28,8},{1,13},{... | collective-permute-start | bytes 49160 | tf_op jit(solution)/shard_map/ppermute | solution.py:226
  32.4 11.3 %collective-permute-start.9 = (f32[4,1024]{1,0:T(4,128)}, f32[4,1024]{1,0:T(4,128)S(1)}, u32[]{:S(2)}, u32[]{:S(2)}) collective-permute-start(f32[4,1024]{1,0:T(4,128)} %get-tuple-element.9.refs_1_), channel_id=1, source_target_pairs={{0,16},{4,20},{8,24},{12,28},{16,0},{20,4},{24,8},{28,12},{1,17},{... | collective-permute-start | bytes 49160 | tf_op jit(solution)/shard_map/ppermute | solution.py:226
  33.2 1.3 %copy-start = (bf16[5,2,256,256]{3,2,1,0:T(8,128)(2,1)S(1)}, bf16[5,2,256,256]{3,2,1,0:T(8,128)(2,1)}, u32[]{:S(2)}) copy-start(bf16[5,2,256,256]{3,2,1,0:T(8,128)(2,1)} %constant.13.clone.refs_8_) | copy-start | bytes 3932164
  34.5 1.1 %copy-start.1 = (bf16[6,256,256]{2,1,0:T(8,128)(2,1)S(1)}, bf16[6,256,256]{2,1,0:T(8,128)(2,1)}, u32[]{:S(2)}) copy-start(bf16[6,256,256]{2,1,0:T(8,128)(2,1)} %constant.14.clone.refs_9_) | copy-start | bytes 2359300
  35.6 0.8 %copy-start.2 = (f32[8,1024]{1,0:T(8,128)S(1)}, f32[8,1024]{1,0:T(8,128)}, u32[]{:S(2)}) copy-start(f32[8,1024]{1,0:T(8,128)} %get-tuple-element.8.refs_0_) | copy-start | bytes 98308
  36.4 7.3 %copy-start.3 = (f32[4,1024]{1,0:T(4,128)S(1)}, f32[4,1024]{1,0:T(4,128)}, u32[]{:S(2)}) copy-start(f32[4,1024]{1,0:T(4,128)} %get-tuple-element.9.refs_1_) | copy-start | bytes 49156
  36.4 7.3 %copy-start.4 = (f32[4,1024]{1,0:T(4,128)S(1)}, f32[4,1024]{1,0:T(4,128)}, u32[]{:S(2)}) copy-start(f32[4,1024]{1,0:T(4,128)} %get-tuple-element.10.refs_6_) | copy-start | bytes 49156
  36.4 7.3 %copy-start.5 = (f32[4]{0:T(128)S(1)}, f32[4]{0:T(128)}, u32[]{:S(2)}) copy-start(f32[4]{0:T(128)} %gains.3) | copy-start | bytes 52
where the time goes:
time: 59.5 us; the launch traced here: 59 us
  starting transfers between devices  16.8 us (28%)
  Pallas kernels  15.1 us (25%)
  waiting for transfers between devices  9.89 us (17%)
  blocking collectives  9.1 us (15%)
  local copies, waits for them, and re-layouts  8.13 us (14%)
    ppermute x14, starting transfers between devices, shifted(): lax.ppermute(value, axis, [(i, (i + steps) % count) for i in range(count)])  16.8 us
    ppermute x14, waiting for transfers between devices, shifted(): lax.ppermute(value, axis, [(i, (i + steps) % count) for i in range(count)])  9.89 us
    all_to_all x1, blocking collectives, body(): lax.all_to_all(kicks, 'bunch', split_axis=0, concat_axis=0, tiled=True)  9.1 us
    unnamed x16, local copies, waits for them, and re-layouts  8.13 us
    pallas_call x1, Pallas kernels, body(): pl.pallas_call(functools.partial(field_kernel, tiles), out_shape=jax.Shap...  7.23 us
    pallas_call x1, Pallas kernels, body(): pl.pallas_call(functools.partial(kick_kernel, count), out_shape=jax.Shape...  4.7 us
    pallas_call x1, Pallas kernels, body(): pl.pallas_call(pack_kernel, out_shape=(jax.ShapeDtypeStruct((8, particles...  1.59 us
    pallas_call x1, Pallas kernels, body(): pl.pallas_call(functools.partial(final_kernel, count), out_shape=jax.Shap...  1.55 us
  transfers between devices with their start and end apart: 14, of which 2 were waited for; matrix products, arithmetic and copies ran while one was open for 2% of the time, Pallas kernels for 12%

commit v1 on v0

v1 whole, which is shorter than its diff:
```python
import functools
import math

import jax
import jax.numpy as jnp
import ml_dtypes
import numpy as np
from jax import lax
from jax.experimental import pallas as pl
from jax.experimental.pallas import tpu as pltpu
from jax.sharding import PartitionSpec as P

GRID = 256
HALF = GRID // 2
STOPS = 4
OFFSET_CELLS = 32
BANDS = GRID // OFFSET_CELLS
REACH = STOPS + 1
f32 = jnp.float32
bf16 = jnp.bfloat16


def split_table(table):
    high = table.astype(ml_dtypes.bfloat16)
    low = (table - high.astype(np.float64)).astype(ml_dtypes.bfloat16)
    return np.stack([high, low])


@functools.cache
def make_tables():
    cells = np.arange(GRID)
    wave = np.where(cells <= HALF, cells, cells - HALF)
    is_sin = cells > HALF
    angle = 2 * np.pi * ((cells[:, None] * wave[None, :]) % GRID) / GRID
    basis = np.where(is_sin[None, :], np.sin(angle), np.cos(angle))
    slope = -0.5 * (np.roll(basis, -1, 0) - np.roll(basis, 1, 0))
    order = OFFSET_CELLS * (cells % BANDS) + cells // BANDS
    here = (cells[None, :] == wave[:, None]).astype(np.float64)
    there = (cells[None, :] == (-wave[:, None]) % GRID).astype(np.float64)
    count = np.where((wave == 0) | (wave == HALF), 1.0, 2.0)[:, None] / GRID
    sign = np.where(is_sin, -1.0, 1.0)[:, None]
    even = 0.5 * (here + there) * count
    odd = 0.5 * (here - there) * count
    tables = np.stack(
        [
            split_table(basis.T),
            split_table(basis),
            split_table(slope.T),
            split_table(basis[order]),
            split_table(slope[order]),
        ]
    )
    mixers = np.stack([even, even.T, odd * sign, -(odd * sign).T]).astype(ml_dtypes.bfloat16)
    return np.concatenate([tables.reshape(-1, GRID, GRID), mixers])


def dot(a, b):
    return jnp.dot(a, b, preferred_element_type=f32)


def dot_nt(a, b):
    return lax.dot_general(a, b, (((1,), (1,)), ((), ())), preferred_element_type=f32)


def halves(x):
    high = x.astype(bf16)
    return high, (x - high.astype(f32)).astype(bf16)


def product(a, b):
    return dot(a[0], b[0]) + dot(a[0], b[1]) + dot(a[1], b[0])


def pack_kernel(cells, charges, fill, marks, green, out, copies, thin):
    particles = charges.shape[1]
    width = particles // 8
    for beam in range(2):
        rows = [
            charges[beam : beam + 1, :].astype(f32) * fill[0, beam].astype(f32),
            cells[beam, 0, 0:1, :].astype(f32),
            cells[beam, 0, 1:2, :].astype(f32),
        ]
        group = lax.broadcasted_iota(jnp.int32, (1, particles), 1) // width
        mark = jnp.zeros((1, particles), f32)
        for offset in range(1, REACH):
            mark = jnp.where(group == offset - 1, marks[beam, 0, 0, offset - 1].astype(f32), mark)
        for offset in range(STOPS - 1):
            mark = jnp.where(group == STOPS + offset, marks[beam, 1, 0, offset + 1].astype(f32), mark)
        rows.append(mark)
        for row, value in enumerate(rows):
            out[4 * beam + row : 4 * beam + row + 1, :] = value.astype(bf16)
    for copy in range(copies.shape[0]):
        copies[copy] = out[...]
    thin[...] = green[...].astype(bf16)


def field_kernel(tiles, index, *refs):
    packs = refs[1:tiles]
    greens = refs[tiles + 1 : 2 * tiles]
    far, out, near, own, gathered, arrived = refs[2 * tiles :]
    columns = greens[0].shape[0]
    places = [
        pl.ds(pl.multiple_of(relative(index[0], step, tiles) * columns, columns), columns)
        for step in range(tiles)
    ]
    fetch = [
        pltpu.make_async_copy(refs[0], own, arrived.at[0]),
        pltpu.make_async_copy(refs[tiles], gathered.at[places[0], :], arrived.at[1]),
        pltpu.make_async_copy(far, near, arrived.at[2]),
    ]
    for copy in fetch:
        copy.start()
    for step in range(1, tiles):
        gathered[places[step], :] = greens[step - 1][...]
    particles = packs[0].shape[1]
    cells = lax.broadcasted_iota(jnp.int32, (GRID, particles), 0).astype(f32)
    densities = [jnp.zeros((GRID, GRID), f32) for _ in range(2)]
    for pack in (*packs, own):
        if pack is own:
            fetch[0].wait()
        for beam in range(2):
            base = 4 * beam
            charge = pack[base : base + 1, :].astype(f32)
            rows = pack[base + 1 : base + 2, :].astype(f32)
            cols = pack[base + 2 : base + 3, :].astype(f32)
            row_hot = jnp.where(cells == rows, 1.0, 0.0).astype(bf16)
            col_hot = jnp.where(cells == cols, charge, 0.0).astype(bf16)
            densities[beam] = densities[beam] + dot_nt(col_hot, row_hot)
    densities = [halves(density) for density in densities]
    fetch[1].wait()
    fetch[2].wait()
    tables = [(near[2 * which], near[2 * which + 1]) for which in range(5)]
    mixers = [near[10 + which] for which in range(4)]
    alpha, beta = (
        dot(mixers[side], turned[0]) + dot(mixers[side], turned[1])
        for side, turned in (
            (side, halves(dot(gathered[...], mixers[side + 1]))) for side in (0, 2)
        )
    )
    for beam in range(2):
        first = halves(product(tables[0], densities[beam]))
        spectrum = product(first, tables[1])
        swapped = jnp.concatenate(
            [
                jnp.concatenate([spectrum[HALF:, HALF:], spectrum[HALF:, :HALF]], axis=1),
                jnp.concatenate([spectrum[:HALF, HALF:], spectrum[:HALF, :HALF]], axis=1),
            ],
            axis=0,
        )
        scaled = halves(alpha * spectrum + beta * swapped)
        for axis, (inner, outer) in enumerate(((2, 3), (0, 4))):
            part = halves(product(scaled, tables[inner]))
            field = product(tables[outer], part)
            out[beam, axis * GRID : (axis + 1) * GRID, :] = field.astype(bf16)


def kick_kernel(count, index, gains, strengths, fields, queries, out):
    particles = queries.shape[2]
    width = particles // 8
    here = index[0]
    block = 2 * width
    cells = lax.broadcasted_iota(jnp.int32, (GRID, block), 0).astype(f32)
    bands = lax.broadcasted_iota(jnp.int32, (BANDS, block), 0).astype(f32)
    for offset in reversed(range(REACH)):
        for beam in range(2):
            sign = 1 if beam == 0 else -1
            target = lax.rem(here - sign * offset + count, count)
            source = queries.at[target]
            base = 4 * beam

            def weight_of(stop, group):
                mark = source[base + 3 : base + 4, group * width : (group + 1) * width].astype(f32)
                mark = mark * (gains[stop] * strengths[stop])
                return jnp.concatenate([mark, mark], axis=1)

            middle = gains[offset] if offset < STOPS else None
            up = weight_of(offset - 1, offset - 1) if offset else None
            down = weight_of(offset + 1, STOPS + offset) if offset < STOPS - 1 else None
            for start in range(0, particles, block):
                rows = source[base + 1 : base + 2, start : start + block].astype(f32)
                cols = source[base + 2 : base + 3, start : start + block].astype(f32)
                band = jnp.floor(cols * (1.0 / OFFSET_CELLS))
                inside = cols - band * OFFSET_CELLS
                hot = jnp.where(cells == rows, 1.0, 0.0).astype(bf16)
                values = dot(fields[1 - beam], hot)
                picked = [jnp.zeros((BANDS, block), f32) for _ in range(2)]
                for place in range(OFFSET_CELLS):
                    hit = jnp.broadcast_to(inside == place, (BANDS, block))
                    for axis in range(2):
                        at = axis * GRID + place * BANDS
                        picked[axis] = jnp.where(hit, values[at : at + BANDS, :], picked[axis])
                weight = jnp.zeros((BANDS, block), f32)
                if middle is not None:
                    weight = jnp.where(bands == band, middle, weight)
                if up is not None:
                    weight = jnp.where(bands == band - 1, up, weight)
                if down is not None:
                    weight = jnp.where(bands == band + 1, down, weight)
                for axis in range(2):
                    kick = jnp.sum(weight * picked[axis], axis=0, keepdims=True)
                    out[target, 2 * beam + axis : 2 * beam + axis + 1, start : start + block] = kick


def final_kernel(count, index, received, momenta, out):
    here = index[0]
    for beam in range(2):
        sign = 1 if beam == 0 else -1
        for axis in range(2):
            total = None
            for offset in range(REACH):
                source = lax.rem(here + sign * offset + count, count)
                part = received[source, 2 * beam + axis : 2 * beam + axis + 1, :]
                total = part if total is None else total + part
            out[beam, 0, axis : axis + 1, :] = momenta[beam, 0, axis : axis + 1, :] + total.astype(
                bf16
            ).astype(f32)


SMEM = pl.BlockSpec(memory_space=pltpu.SMEM)
VMEM = pl.BlockSpec(memory_space=pltpu.VMEM)
FAR = pl.BlockSpec(memory_space=pltpu.HBM)
LIMIT = pltpu.CompilerParams(vmem_limit_bytes=48 * 1024 * 1024)
SMALL = pltpu.CompilerParams(vmem_limit_bytes=16 * 1024 * 1024)


def kept_far(value):
    return pltpu.with_memory_space_constraint(value, pltpu.HBM)


def is_power_of_two(count):
    return count & (count - 1) == 0


def relative(index, step, count):
    if is_power_of_two(count):
        return jnp.bitwise_xor(index, step)
    return lax.rem(index - step + count, count)


def exchanged(value, axis, step):
    count = lax.axis_size(axis)
    if is_power_of_two(count):
        pairs = [(i, i ^ step) for i in range(count)]
    else:
        pairs = [(i, (i + step) % count) for i in range(count)]
    return lax.ppermute(value, axis, pairs)


def body(cell_index, charges, momenta, fill_pattern, encounters, green_spectrum, stop_gain, parasitic_gain):
    particles = cell_index.shape[3]
    tiles = lax.axis_size("tile")
    count = lax.axis_size("bunch")
    tables = make_tables()
    bunch = lax.axis_index("bunch").astype(jnp.int32).reshape(1)
    tile = lax.axis_index("tile").astype(jnp.int32).reshape(1)
    columns = green_spectrum.shape[1]
    pack, copies, thin = pl.pallas_call(
        pack_kernel,
        out_shape=(
            jax.ShapeDtypeStruct((8, particles), bf16),
            jax.ShapeDtypeStruct((count, 8, particles), bf16),
            jax.ShapeDtypeStruct((columns, GRID), bf16),
        ),
        in_specs=[VMEM, VMEM, SMEM, SMEM, VMEM],
        out_specs=(VMEM, VMEM, VMEM),
        compiler_params=SMALL,
    )(
        kept_far(cell_index),
        kept_far(charges.reshape(2, particles)),
        kept_far(fill_pattern.T),
        kept_far(jnp.transpose(encounters, (1, 2, 3, 0))),
        kept_far(green_spectrum.T),
    )
    packs = [pack] + [exchanged(pack, "tile", step) for step in range(1, tiles)]
    greens = [thin] + [exchanged(thin, "tile", step) for step in range(1, tiles)]
    queries = lax.all_to_all(copies, "bunch", split_axis=0, concat_axis=0, tiled=True)
    fields = pl.pallas_call(
        functools.partial(field_kernel, tiles),
        out_shape=jax.ShapeDtypeStruct((2, 2 * GRID, GRID), bf16),
        in_specs=[SMEM] + ([FAR] + [VMEM] * (tiles - 1)) * 2 + [FAR],
        out_specs=VMEM,
        scratch_shapes=[
            pltpu.VMEM(tables.shape, bf16),
            pltpu.VMEM(pack.shape, bf16),
            pltpu.VMEM((GRID, GRID), bf16),
            pltpu.SemaphoreType.DMA((3,)),
        ],
        compiler_params=LIMIT,
    )(tile, *packs, *greens, kept_far(jnp.asarray(tables)))
    kicks = pl.pallas_call(
        functools.partial(kick_kernel, count),
        out_shape=jax.ShapeDtypeStruct((count, 4, particles), f32),
        in_specs=[SMEM, SMEM, SMEM, VMEM, VMEM],
        out_specs=VMEM,
        compiler_params=LIMIT,
    )(bunch, stop_gain, parasitic_gain, fields, queries)
    received = lax.all_to_all(kicks, "bunch", split_axis=0, concat_axis=0, tiled=True)
    return pl.pallas_call(
        functools.partial(final_kernel, count),
        out_shape=jax.ShapeDtypeStruct(momenta.shape, f32),
        in_specs=[SMEM, VMEM, VMEM],
        out_specs=VMEM,
        compiler_params=SMALL,
    )(bunch, received, momenta)


def solution(mesh):
    in_specs = (
        P(None, "bunch", None, "tile"),
        P(None, "bunch", "tile"),
        P(None, "bunch", None, "tile"),
        P(None, "bunch"),
        P(None, None, None, "bunch"),
        P(None, "tile"),
        P(),
        P(),
    )
    out_specs = P(None, "bunch", None, "tile")
    return jax.shard_map(body, mesh=mesh, in_specs=in_specs, out_specs=out_specs, check_vma=False)
```

time: 59.5 us -> 39.8 us (0.67)
  local copies, waits for them, and re-layouts: 8.13 us -> 0.01 us
  waiting for transfers between devices: 9.89 us -> 3.86 us
  Pallas kernels: 15.1 us -> 12.1 us
  starting transfers between devices: 16.8 us -> 14 us
    unnamed x16 -> x6, local copies, waits for them, and re-layouts: 8.13 us -> 0.01 us
    ppermute x14 -> x6, starting transfers between devices: 16.8 us -> 8.84 us  [exchanged(): return lax.ppermute(value, axis, pairs)]
    ppermute x14 -> x6, waiting for transfers between devices: 9.89 us -> 3.86 us  [exchanged(): return lax.ppermute(value, axis, pairs)]
    all_to_all x0 -> x1, starting transfers between devices: none -> 5.17 us  [body(): lax.all_to_all(copies, 'bunch', split_axis=0, concat_axis=0, tiled=True)]
    pallas_call x1, Pallas kernels: 7.23 us -> 5.2 us  [body(): pl.pallas_call(functools.partial(field_kernel, tiles), out_shape=jax.Shap...]
    pallas_call x1, Pallas kernels: 1.55 us -> 0.64 us  [body(): pl.pallas_call(functools.partial(final_kernel, count), out_shape=jax.Shap...]
  transfers between devices with their start and end apart: 14 -> 7, of which waited for: 2 -> 1; matrix products, arithmetic and copies ran while one was open for 2% -> 0% of each run, Pallas kernels for 12% -> 13%
where the time goes in v1:
time: 39.8 us; the launch traced here: 39.5 us
  starting transfers between devices  14 us (35%)
  Pallas kernels  12.1 us (30%)
  blocking collectives  9.46 us (24%)
  waiting for transfers between devices  3.86 us (10%)
    all_to_all x1, blocking collectives, body(): lax.all_to_all(kicks, 'bunch', split_axis=0, concat_axis=0, tiled=True)  9.46 us
    ppermute x6, starting transfers between devices, exchanged(): return lax.ppermute(value, axis, pairs)  8.84 us
    pallas_call x1, Pallas kernels, body(): pl.pallas_call(functools.partial(field_kernel, tiles), out_shape=jax.Shap...  5.2 us
    all_to_all x1, starting transfers between devices, body(): lax.all_to_all(copies, 'bunch', split_axis=0, concat_axis=0, tiled=True)  5.17 us
    pallas_call x1, Pallas kernels, body(): pl.pallas_call(functools.partial(kick_kernel, count), out_shape=jax.Shape...  4.66 us
    ppermute x6, waiting for transfers between devices, exchanged(): return lax.ppermute(value, axis, pairs)  3.86 us
    pallas_call x1, Pallas kernels, body(): pl.pallas_call(pack_kernel, out_shape=(jax.ShapeDtypeStruct((8, particles...  1.6 us
  transfers between devices with their start and end apart: 7, of which 1 were waited for; matrix products, arithmetic and copies ran while one was open for 0% of the time, Pallas kernels for 13%

profile of v1, /device:TPU:0, one launch (start us, length us, event | category | flops | bytes accessed | tf_op | source)
XLA Modules:
  0.0 39.5 jit_solution(1589524136721531897)
XLA Ops:
  0.0 0.0 copy-start.2
  0.0 0.0 copy-start.1
  0.0 1.6 %shard_map.91 = (bf16[8,1024]{1,0:T(8,128)(2,1)S(1)}, bf16[8,8,1024]{2,1,0:T(8,128)(2,1)}, bf16[64,256]{1,0:T(8,128)(2,1)S(1)}) custom-call(s32[2,1,2,1024]{3,2,1,0:T(2,128)} %cells.1, bf16[2,1024]{1,0:T(2,128)(2,1)} %bitcast.7, s32[1,2]{1,0:T(1,128)} %bitcast.9, s32[2,2,1,4]{3,2,1,0:T(1,128)} %bitcast.8, f32[64,256]{1,0:T(8,128)} %bitcast.6), custom_call_target="tpu_custom_call" | custom-call | tf_op jit(solution)/shard_map/pallas_call | solution.py:257
  1.6 5.2 %all-to-all-start = ((bf16[8,8,1024]{2,1,0:T(8,128)(2,1)}), bf16[8,8,1024]{2,1,0:T(8,128)(2,1)S(1)}, u32[]{:S(2)}, u32[]{:S(2)}) async-start(bf16[8,8,1024]{2,1,0:T(8,128)(2,1)} %get-tuple-element.10), calls=%async_computation | async-start | bytes 262144 | tf_op jit(solution)/shard_map/all_to_all | solution.py:276
  6.8 0.0 copy-start
  6.8 3.7 %collective-permute-start.2 = (bf16[8,1024]{1,0:T(8,128)(2,1)S(1)}, bf16[8,1024]{1,0:T(8,128)(2,1)S(1)}, u32[]{:S(2)}, u32[]{:S(2)}) collective-permute-start(bf16[8,1024]{1,0:T(8,128)(2,1)S(1)} %get-tuple-element.8.refs_0_), channel_id=1, source_target_pairs={{0,3},{1,2},{2,1},{3,0},{4,7},{5,6},{6,5},{7,4},{8,11},{9,10},{10,... | collective-permute-start | bytes 49160 | tf_op jit(solution)/shard_map/ppermute | solution.py:246
  10.4 0.2 collective-permute-start.5
  10.7 0.8 %collective-permute-start.4 = (bf16[64,256]{1,0:T(8,128)(2,1)S(1)}, bf16[64,256]{1,0:T(8,128)(2,1)S(1)}, u32[]{:S(2)}, u32[]{:S(2)}) collective-permute-start(bf16[64,256]{1,0:T(8,128)(2,1)S(1)} %get-tuple-element.9.refs_4_), channel_id=1, source_target_pairs={{0,2},{1,3},{2,0},{3,1},{4,6},{5,7},{6,4},{7,5},{8,10},{9,11},{10,... | collective-permute-start | bytes 98312 | tf_op jit(solution)/shard_map/ppermute | solution.py:246
  11.5 3.4 %collective-permute-start.3 = (bf16[64,256]{1,0:T(8,128)(2,1)S(1)}, bf16[64,256]{1,0:T(8,128)(2,1)S(1)}, u32[]{:S(2)}, u32[]{:S(2)}) collective-permute-start(bf16[64,256]{1,0:T(8,128)(2,1)S(1)} %get-tuple-element.9.refs_4_), channel_id=1, source_target_pairs={{0,1},{1,0},{2,3},{3,2},{4,5},{5,4},{6,7},{7,6},{8,9},{9,8},{10,11... | collective-permute-start | bytes 98312 | tf_op jit(solution)/shard_map/ppermute | solution.py:246
  14.8 0.0 collective-permute-start.1
  14.8 0.0 collective-permute-done.2.refs_3_
  14.8 0.8 %collective-permute-start = (bf16[8,1024]{1,0:T(8,128)(2,1)S(1)}, bf16[8,1024]{1,0:T(8,128)(2,1)S(1)}, u32[]{:S(2)}, u32[]{:S(2)}) collective-permute-start(bf16[8,1024]{1,0:T(8,128)(2,1)S(1)} %get-tuple-element.8.refs_0_), channel_id=1, source_target_pairs={{0,1},{1,0},{2,3},{3,2},{4,5},{5,4},{6,7},{7,6},{8,9},{9,8},{10,11... | collective-permute-start | bytes 49160 | tf_op jit(solution)/shard_map/ppermute | solution.py:246
  15.6 3.8 %collective-permute-done.1.refs_2_ = bf16[8,1024]{1,0:T(8,128)(2,1)S(1)} collective-permute-done((bf16[8,1024]{1,0:T(8,128)(2,1)S(1)}, bf16[8,1024]{1,0:T(8,128)(2,1)S(1)}, u32[]{:S(2)}, u32[]{:S(2)}) %collective-permute-start.1) | collective-permute-done | bytes 16416 | tf_op jit(solution)/shard_map/ppermute | solution.py:246
  19.5 0.0 collective-permute-done.refs_1_
  19.5 0.0 collective-permute-done.5.refs_7_
  19.5 0.0 collective-permute-done.4.refs_6_
  19.5 0.0 collective-permute-done.3.refs_5_
  19.5 5.2 %shard_map.92.fields = bf16[2,512,256]{2,1,0:T(8,128)(2,1)S(1)} custom-call(s32[1]{0:T(128)} %bitcast.1.index, bf16[8,1024]{1,0:T(8,128)(2,1)S(1)} %get-tuple-element.8.refs_0_, bf16[8,1024]{1,0:T(8,128)(2,1)S(1)} %collective-permute-done.refs_1_, bf16[8,1024]{1,0:T(8,128)(2,1)S(1)} %collective-permute-done.1.refs_2_, ...), custom_call_target="tpu_custom_call" | custom-call | tf_op jit(solution)/shard_map/pallas_call | solution.py:277
  24.7 0.0 all-to-all-done.queries
  24.7 0.0 copy-done.2
  24.7 0.0 copy-done.1
  24.7 4.7 %shard_map.93 = f32[8,4,1024]{2,1,0:T(4,128)S(1)} custom-call(s32[1]{0:T(128)} %bitcast.index, f32[4]{0:T(128)S(1)} %copy-done.1, f32[4]{0:T(128)S(1)} %copy-done.2, bf16[2,512,256]{2,1,0:T(8,128)(2,1)S(1)} %shard_map.92.fields, bf16[8,8,1024]{2,1,0:T(8,128)(2,1)S(1)} %all-to-all-done.queries), custom_call_target="tpu_custom_call" | custom-call | tf_op jit(solution)/shard_map/pallas_call | solution.py:290
  29.4 9.5 %all_to_all.10.received = f32[8,4,1024]{2,1,0:T(4,128)S(1)} all-to-all(f32[8,4,1024]{2,1,0:T(4,128)S(1)} %shard_map.93), channel_id=1, replica_groups=mesh['bunch'=8,'tile'=4] {'bunch'}, dimensions={0} | all-to-all | bytes 262144 | tf_op jit(solution)/shard_map/all_to_all | solution.py:297
  38.9 0.0 copy-done
  38.9 0.6 %shard_map.94 = f32[2,1,2,1024]{3,2,1,0:T(2,128)} custom-call(s32[1]{0:T(128)} %bitcast.index, f32[8,4,1024]{2,1,0:T(4,128)S(1)} %all_to_all.10.received, f32[2,1,2,1024]{3,2,1,0:T(2,128)S(1)} %copy-done), custom_call_target="tpu_custom_call" | custom-call | tf_op jit(solution)/shard_map/pallas_call | solution.py:298
Async XLA Ops:
  0.0 24.7 %copy-start.2 = (f32[4]{0:T(128)S(1)}, f32[4]{0:T(128)}, u32[]{:S(2)}) copy-start(f32[4]{0:T(128)} %strengths.1) | copy-start | bytes 52
  0.0 24.7 %copy-start.1 = (f32[4]{0:T(128)S(1)}, f32[4]{0:T(128)}, u32[]{:S(2)}) copy-start(f32[4]{0:T(128)} %gains.1) | copy-start | bytes 52
  1.6 23.1 %all-to-all-start = ((bf16[8,8,1024]{2,1,0:T(8,128)(2,1)}), bf16[8,8,1024]{2,1,0:T(8,128)(2,1)S(1)}, u32[]{:S(2)}, u32[]{:S(2)}) async-start(bf16[8,8,1024]{2,1,0:T(8,128)(2,1)} %get-tuple-element.10), calls=%async_computation | async-start | bytes 262144 | tf_op jit(solution)/shard_map/all_to_all | solution.py:276
  6.8 32.1 %copy-start = (f32[2,1,2,1024]{3,2,1,0:T(2,128)S(1)}, f32[2,1,2,1024]{3,2,1,0:T(2,128)}, u32[]{:S(2)}) copy-start(f32[2,1,2,1024]{3,2,1,0:T(2,128)} %momenta.1) | copy-start | bytes 49156
  6.8 8.1 %collective-permute-start.2 = (bf16[8,1024]{1,0:T(8,128)(2,1)S(1)}, bf16[8,1024]{1,0:T(8,128)(2,1)S(1)}, u32[]{:S(2)}, u32[]{:S(2)}) collective-permute-start(bf16[8,1024]{1,0:T(8,128)(2,1)S(1)} %get-tuple-element.8.refs_0_), channel_id=1, source_target_pairs={{0,3},{1,2},{2,1},{3,0},{4,7},{5,6},{6,5},{7,4},{8,11},{9,10},{10,... | collective-permute-start | bytes 49160 | tf_op jit(solution)/shard_map/ppermute | solution.py:246
  10.4 9.0 %collective-permute-start.5 = (bf16[64,256]{1,0:T(8,128)(2,1)S(1)}, bf16[64,256]{1,0:T(8,128)(2,1)S(1)}, u32[]{:S(2)}, u32[]{:S(2)}) collective-permute-start(bf16[64,256]{1,0:T(8,128)(2,1)S(1)} %get-tuple-element.9.refs_4_), channel_id=1, source_target_pairs={{0,3},{1,2},{2,1},{3,0},{4,7},{5,6},{6,5},{7,4},{8,11},{9,10},{10,... | collective-permute-start | bytes 98312 | tf_op jit(solution)/shard_map/ppermute | solution.py:246
  10.7 8.8 %collective-permute-start.4 = (bf16[64,256]{1,0:T(8,128)(2,1)S(1)}, bf16[64,256]{1,0:T(8,128)(2,1)S(1)}, u32[]{:S(2)}, u32[]{:S(2)}) collective-permute-start(bf16[64,256]{1,0:T(8,128)(2,1)S(1)} %get-tuple-element.9.refs_4_), channel_id=1, source_target_pairs={{0,2},{1,3},{2,0},{3,1},{4,6},{5,7},{6,4},{7,5},{8,10},{9,11},{10,... | collective-permute-start | bytes 98312 | tf_op jit(solution)/shard_map/ppermute | solution.py:246
  11.5 8.0 %collective-permute-start.3 = (bf16[64,256]{1,0:T(8,128)(2,1)S(1)}, bf16[64,256]{1,0:T(8,128)(2,1)S(1)}, u32[]{:S(2)}, u32[]{:S(2)}) collective-permute-start(bf16[64,256]{1,0:T(8,128)(2,1)S(1)} %get-tuple-element.9.refs_4_), channel_id=1, source_target_pairs={{0,1},{1,0},{2,3},{3,2},{4,5},{5,4},{6,7},{7,6},{8,9},{9,8},{10,11... | collective-permute-start | bytes 98312 | tf_op jit(solution)/shard_map/ppermute | solution.py:246
  14.8 4.6 %collective-permute-start.1 = (bf16[8,1024]{1,0:T(8,128)(2,1)S(1)}, bf16[8,1024]{1,0:T(8,128)(2,1)S(1)}, u32[]{:S(2)}, u32[]{:S(2)}) collective-permute-start(bf16[8,1024]{1,0:T(8,128)(2,1)S(1)} %get-tuple-element.8.refs_0_), channel_id=1, source_target_pairs={{0,2},{1,3},{2,0},{3,1},{4,6},{5,7},{6,4},{7,5},{8,10},{9,11},{10,... | collective-permute-start | bytes 49160 | tf_op jit(solution)/shard_map/ppermute | solution.py:246
  14.8 4.6 %collective-permute-start = (bf16[8,1024]{1,0:T(8,128)(2,1)S(1)}, bf16[8,1024]{1,0:T(8,128)(2,1)S(1)}, u32[]{:S(2)}, u32[]{:S(2)}) collective-permute-start(bf16[8,1024]{1,0:T(8,128)(2,1)S(1)} %get-tuple-element.8.refs_0_), channel_id=1, source_target_pairs={{0,1},{1,0},{2,3},{3,2},{4,5},{5,4},{6,7},{7,6},{8,9},{9,8},{10,11... | collective-permute-start | bytes 49160 | tf_op jit(solution)/shard_map/ppermute | solution.py:246

commit v2 on v1

--- a/solution.py
+++ b/solution.py
@@ -71,7 +71,7 @@
     return dot(a[0], b[0]) + dot(a[0], b[1]) + dot(a[1], b[0])
 
 
-def pack_kernel(cells, charges, fill, marks, green, out, copies, thin):
+def pack_kernel(cells, charges, fill, marks, green, out, copies, message):
     particles = charges.shape[1]
     width = particles // 8
     for beam in range(2):
@@ -91,44 +91,39 @@
             out[4 * beam + row : 4 * beam + row + 1, :] = value.astype(bf16)
     for copy in range(copies.shape[0]):
         copies[copy] = out[...]
-    thin[...] = green[...].astype(bf16)
+    lists = 8 * particles // GRID
+    for part in range(particles // GRID):
+        message[8 * part : 8 * part + 8, :] = out[:, part * GRID : (part + 1) * GRID]
+    message[lists:, :] = green[...].astype(bf16)
 
 
 def field_kernel(tiles, index, *refs):
-    packs = refs[1:tiles]
-    greens = refs[tiles + 1 : 2 * tiles]
-    far, out, near, own, gathered, arrived = refs[2 * tiles :]
-    columns = greens[0].shape[0]
-    places = [
-        pl.ds(pl.multiple_of(relative(index[0], step, tiles) * columns, columns), columns)
-        for step in range(tiles)
-    ]
-    fetch = [
-        pltpu.make_async_copy(refs[0], own, arrived.at[0]),
-        pltpu.make_async_copy(refs[tiles], gathered.at[places[0], :], arrived.at[1]),
-        pltpu.make_async_copy(far, near, arrived.at[2]),
-    ]
-    for copy in fetch:
-        copy.start()
-    for step in range(1, tiles):
-        gathered[places[step], :] = greens[step - 1][...]
-    particles = packs[0].shape[1]
-    cells = lax.broadcasted_iota(jnp.int32, (GRID, particles), 0).astype(f32)
+    messages = refs[:tiles]
+    far, out, near, gathered, arrived = refs[tiles:]
+    fetch = pltpu.make_async_copy(far, near, arrived)
+    fetch.start()
+    lists = messages[0].shape[0] - GRID // tiles
+    columns = GRID // tiles
+    for step in range(tiles):
+        start = pl.multiple_of(relative(index[0], step, tiles) * columns, columns)
+        gathered[pl.ds(start, columns), :] = messages[step][lists:, :]
+    cells = lax.broadcasted_iota(jnp.int32, (GRID, GRID), 0).astype(f32)
     densities = [jnp.zeros((GRID, GRID), f32) for _ in range(2)]
-    for pack in (*packs, own):
-        if pack is own:
-            fetch[0].wait()
+    for message in messages:
         for beam in range(2):
-            base = 4 * beam
-            charge = pack[base : base + 1, :].astype(f32)
-            rows = pack[base + 1 : base + 2, :].astype(f32)
-            cols = pack[base + 2 : base + 3, :].astype(f32)
-            row_hot = jnp.where(cells == rows, 1.0, 0.0).astype(bf16)
-            col_hot = jnp.where(cells == cols, charge, 0.0).astype(bf16)
-            densities[beam] = densities[beam] + dot_nt(col_hot, row_hot)
+            row_hots, col_hots = [], []
+            for part in range(lists // 8):
+                base = 8 * part + 4 * beam
+                charge = message[base : base + 1, :].astype(f32)
+                rows = message[base + 1 : base + 2, :].astype(f32)
+                cols = message[base + 2 : base + 3, :].astype(f32)
+                row_hots.append(jnp.where(cells == rows, 1.0, 0.0).astype(bf16))
+                col_hots.append(jnp.where(cells == cols, charge, 0.0).astype(bf16))
+            densities[beam] = densities[beam] + dot_nt(
+                jnp.concatenate(col_hots, axis=1), jnp.concatenate(row_hots, axis=1)
+            )
     densities = [halves(density) for density in densities]
-    fetch[1].wait()
-    fetch[2].wait()
+    fetch.wait()
     tables = [(near[2 * which], near[2 * which + 1]) for which in range(5)]
     mixers = [near[10 + which] for which in range(4)]
     alpha, beta = (
@@ -254,12 +249,12 @@
     bunch = lax.axis_index("bunch").astype(jnp.int32).reshape(1)
     tile = lax.axis_index("tile").astype(jnp.int32).reshape(1)
     columns = green_spectrum.shape[1]
-    pack, copies, thin = pl.pallas_call(
+    pack, copies, message = pl.pallas_call(
         pack_kernel,
         out_shape=(
             jax.ShapeDtypeStruct((8, particles), bf16),
             jax.ShapeDtypeStruct((count, 8, particles), bf16),
-            jax.ShapeDtypeStruct((columns, GRID), bf16),
+            jax.ShapeDtypeStruct((8 * particles // GRID + columns, GRID), bf16),
         ),
         in_specs=[VMEM, VMEM, SMEM, SMEM, VMEM],
         out_specs=(VMEM, VMEM, VMEM),
@@ -271,22 +266,21 @@
         kept_far(jnp.transpose(encounters, (1, 2, 3, 0))),
         kept_far(green_spectrum.T),
     )
-    packs = [pack] + [exchanged(pack, "tile", step) for step in range(1, tiles)]
-    greens = [thin] + [exchanged(thin, "tile", step) for step in range(1, tiles)]
+    messages = [message] + [exchanged(message, "tile", step) for step in range(1, tiles)]
     queries = lax.all_to_all(copies, "bunch", split_axis=0, concat_axis=0, tiled=True)
     fields = pl.pallas_call(
         functools.partial(field_kernel, tiles),
         out_shape=jax.ShapeDtypeStruct((2, 2 * GRID, GRID), bf16),
-        in_specs=[SMEM] + ([FAR] + [VMEM] * (tiles - 1)) * 2 + [FAR],
+        in_specs=[SMEM] + [VMEM] * tiles + [FAR],
         out_specs=VMEM,
         scratch_shapes=[
             pltpu.VMEM(tables.shape, bf16),
-            pltpu.VMEM(pack.shape, bf16),
             pltpu.VMEM((GRID, GRID), bf16),
-            pltpu.SemaphoreType.DMA((3,)),
+            pltpu.SemaphoreType.DMA,
         ],
         compiler_params=LIMIT,
-    )(tile, *packs, *greens, kept_far(jnp.asarray(tables)))
+        cost_estimate=pl.CostEstimate(flops=3000000000, bytes_accessed=1000000, transcendentals=0),
+    )(tile, *messages, kept_far(jnp.asarray(tables)))
     kicks = pl.pallas_call(
         functools.partial(kick_kernel, count),
         out_shape=jax.ShapeDtypeStruct((count, 4, particles), f32),

time: 39.8 us -> 31.9 us (0.80)
  starting transfers between devices: 14 us -> 9.56 us
  waiting for transfers between devices: 3.86 us -> 0.48 us
    ppermute x6 -> x3, waiting for transfers between devices: 3.86 us -> 0.48 us  [exchanged(): return lax.ppermute(value, axis, pairs)]
    ppermute x6 -> x3, starting transfers between devices: 8.84 us -> 5.62 us  [exchanged(): return lax.ppermute(value, axis, pairs)]
    all_to_all x1, starting transfers between devices: 5.17 us -> 3.94 us  [body(): lax.all_to_all(copies, 'bunch', split_axis=0, concat_axis=0, tiled=True)]
  transfers between devices with their start and end apart: 7 -> 4, of which waited for: 1 -> 1; matrix products, arithmetic and copies ran while one was open for 0% -> 0% of each run, Pallas kernels for 13% -> 17%
where the time goes in v2:
time: 31.9 us; the launch traced here: 31.6 us
  Pallas kernels  12.4 us (39%)
  starting transfers between devices  9.56 us (30%)
  blocking collectives  9.09 us (28%)
  waiting for transfers between devices  0.48 us (2%)
    all_to_all x1, blocking collectives, body(): lax.all_to_all(kicks, 'bunch', split_axis=0, concat_axis=0, tiled=True)  9.09 us
    ppermute x3, starting transfers between devices, exchanged(): return lax.ppermute(value, axis, pairs)  5.62 us
    pallas_call x1, Pallas kernels, body(): pl.pallas_call(functools.partial(field_kernel, tiles), out_shape=jax.Shap...  5.46 us
    pallas_call x1, Pallas kernels, body(): pl.pallas_call(functools.partial(kick_kernel, count), out_shape=jax.Shape...  4.68 us
    all_to_all x1, starting transfers between devices, body(): lax.all_to_all(copies, 'bunch', split_axis=0, concat_axis=0, tiled=True)  3.94 us
    pallas_call x1, Pallas kernels, body(): pl.pallas_call(pack_kernel, out_shape=(jax.ShapeDtypeStruct((8, particles...  1.59 us
    pallas_call x1, Pallas kernels, body(): pl.pallas_call(functools.partial(final_kernel, count), out_shape=jax.Shap...  0.64 us
  transfers between devices with their start and end apart: 4, of which 1 were waited for; matrix products, arithmetic and copies ran while one was open for 0% of the time, Pallas kernels for 17%

profile of v2, /device:TPU:0, one launch (start us, length us, event | category | flops | bytes accessed | tf_op | source)
XLA Modules:
  0.0 31.6 jit_solution(8975409909684463921)
XLA Ops:
  0.0 1.6 %shard_map.91 = (bf16[8,1024]{1,0:T(8,128)(2,1)}, bf16[8,8,1024]{2,1,0:T(8,128)(2,1)}, bf16[96,256]{1,0:T(8,128)(2,1)S(1)}) custom-call(s32[2,1,2,1024]{3,2,1,0:T(2,128)} %cells.1, bf16[2,1024]{1,0:T(2,128)(2,1)} %bitcast.7, s32[1,2]{1,0:T(1,128)} %bitcast.9, s32[2,2,1,4]{3,2,1,0:T(1,128)} %bitcast.8, f32[64,256]{1,0:T(8,128)} %bitcast.6), custom_call_target="tpu_custom_call" | custom-call | tf_op jit(solution)/shard_map/pallas_call | solution.py:252
  1.6 5.0 %collective-permute-start.2 = (bf16[96,256]{1,0:T(8,128)(2,1)S(1)}, bf16[96,256]{1,0:T(8,128)(2,1)S(1)}, u32[]{:S(2)}, u32[]{:S(2)}) collective-permute-start(bf16[96,256]{1,0:T(8,128)(2,1)S(1)} %get-tuple-element.7.refs_0_), channel_id=1, source_target_pairs={{0,3},{1,2},{2,1},{3,0},{4,7},{5,6},{6,5},{7,4},{8,11},{9,10},{10,... | collective-permute-start | bytes 147464 | tf_op jit(solution)/shard_map/ppermute | solution.py:241
  6.6 0.0 collective-permute-start.1
  6.6 0.6 %collective-permute-start = (bf16[96,256]{1,0:T(8,128)(2,1)S(1)}, bf16[96,256]{1,0:T(8,128)(2,1)S(1)}, u32[]{:S(2)}, u32[]{:S(2)}) collective-permute-start(bf16[96,256]{1,0:T(8,128)(2,1)S(1)} %get-tuple-element.7.refs_0_), channel_id=1, source_target_pairs={{0,1},{1,0},{2,3},{3,2},{4,5},{5,4},{6,7},{7,6},{8,9},{9,8},{10,11... | collective-permute-start | bytes 147464 | tf_op jit(solution)/shard_map/ppermute | solution.py:241
  7.2 3.9 %all-to-all-start = ((bf16[8,8,1024]{2,1,0:T(8,128)(2,1)}), bf16[8,8,1024]{2,1,0:T(8,128)(2,1)S(1)}, u32[]{:S(2)}, u32[]{:S(2)}) async-start(bf16[8,8,1024]{2,1,0:T(8,128)(2,1)} %get-tuple-element.8), calls=%async_computation | async-start | bytes 262144 | tf_op jit(solution)/shard_map/all_to_all | solution.py:270
  11.2 0.0 collective-permute-done.2.refs_3_
  11.2 0.5 %collective-permute-done.1.refs_2_ = bf16[96,256]{1,0:T(8,128)(2,1)S(1)} collective-permute-done((bf16[96,256]{1,0:T(8,128)(2,1)S(1)}, bf16[96,256]{1,0:T(8,128)(2,1)S(1)}, u32[]{:S(2)}, u32[]{:S(2)}) %collective-permute-start.1) | collective-permute-done | bytes 49184 | tf_op jit(solution)/shard_map/ppermute | solution.py:241
  11.6 0.0 collective-permute-done.refs_1_
  11.6 0.0 copy-start.1
  11.6 0.0 copy-start.2
  11.6 0.0 copy-start
  11.6 5.5 %shard_map.92.fields = bf16[2,512,256]{2,1,0:T(8,128)(2,1)S(1)} custom-call(s32[1]{0:T(128)} %bitcast.1.index, bf16[96,256]{1,0:T(8,128)(2,1)S(1)} %get-tuple-element.7.refs_0_, bf16[96,256]{1,0:T(8,128)(2,1)S(1)} %collective-permute-done.refs_1_, bf16[96,256]{1,0:T(8,128)(2,1)S(1)} %collective-permute-done.1.refs_2_, ...), custom_call_target="tpu_custom_call" | custom-call | flops 3000000000 | bytes 1000000 | tf_op jit(solution)/shard_map/pallas_call | solution.py:271
  17.1 0.0 all-to-all-done.queries
  17.1 0.0 copy-done.1
  17.1 0.0 copy-done.2
  17.1 4.7 %shard_map.93 = f32[8,4,1024]{2,1,0:T(4,128)S(1)} custom-call(s32[1]{0:T(128)} %bitcast.index, f32[4]{0:T(128)S(1)} %copy-done.1, f32[4]{0:T(128)S(1)} %copy-done.2, bf16[2,512,256]{2,1,0:T(8,128)(2,1)S(1)} %shard_map.92.fields, bf16[8,8,1024]{2,1,0:T(8,128)(2,1)S(1)} %all-to-all-done.queries), custom_call_target="tpu_custom_call" | custom-call | tf_op jit(solution)/shard_map/pallas_call | solution.py:284
  21.8 9.1 %all_to_all.10.received = f32[8,4,1024]{2,1,0:T(4,128)S(1)} all-to-all(f32[8,4,1024]{2,1,0:T(4,128)S(1)} %shard_map.93), channel_id=1, replica_groups=mesh['bunch'=8,'tile'=4] {'bunch'}, dimensions={0} | all-to-all | bytes 262144 | tf_op jit(solution)/shard_map/all_to_all | solution.py:291
  30.9 0.0 copy-done
  30.9 0.6 %shard_map.94 = f32[2,1,2,1024]{3,2,1,0:T(2,128)} custom-call(s32[1]{0:T(128)} %bitcast.index, f32[8,4,1024]{2,1,0:T(4,128)S(1)} %all_to_all.10.received, f32[2,1,2,1024]{3,2,1,0:T(2,128)S(1)} %copy-done), custom_call_target="tpu_custom_call" | custom-call | tf_op jit(solution)/shard_map/pallas_call | solution.py:292
Async XLA Ops:
  1.6 9.6 %collective-permute-start.2 = (bf16[96,256]{1,0:T(8,128)(2,1)S(1)}, bf16[96,256]{1,0:T(8,128)(2,1)S(1)}, u32[]{:S(2)}, u32[]{:S(2)}) collective-permute-start(bf16[96,256]{1,0:T(8,128)(2,1)S(1)} %get-tuple-element.7.refs_0_), channel_id=1, source_target_pairs={{0,3},{1,2},{2,1},{3,0},{4,7},{5,6},{6,5},{7,4},{8,11},{9,10},{10,... | collective-permute-start | bytes 147464 | tf_op jit(solution)/shard_map/ppermute | solution.py:241
  6.6 5.0 %collective-permute-start.1 = (bf16[96,256]{1,0:T(8,128)(2,1)S(1)}, bf16[96,256]{1,0:T(8,128)(2,1)S(1)}, u32[]{:S(2)}, u32[]{:S(2)}) collective-permute-start(bf16[96,256]{1,0:T(8,128)(2,1)S(1)} %get-tuple-element.7.refs_0_), channel_id=1, source_target_pairs={{0,2},{1,3},{2,0},{3,1},{4,6},{5,7},{6,4},{7,5},{8,10},{9,11},{10,... | collective-permute-start | bytes 147464 | tf_op jit(solution)/shard_map/ppermute | solution.py:241
  6.6 5.0 %collective-permute-start = (bf16[96,256]{1,0:T(8,128)(2,1)S(1)}, bf16[96,256]{1,0:T(8,128)(2,1)S(1)}, u32[]{:S(2)}, u32[]{:S(2)}) collective-permute-start(bf16[96,256]{1,0:T(8,128)(2,1)S(1)} %get-tuple-element.7.refs_0_), channel_id=1, source_target_pairs={{0,1},{1,0},{2,3},{3,2},{4,5},{5,4},{6,7},{7,6},{8,9},{9,8},{10,11... | collective-permute-start | bytes 147464 | tf_op jit(solution)/shard_map/ppermute | solution.py:241
  7.2 9.9 %all-to-all-start = ((bf16[8,8,1024]{2,1,0:T(8,128)(2,1)}), bf16[8,8,1024]{2,1,0:T(8,128)(2,1)S(1)}, u32[]{:S(2)}, u32[]{:S(2)}) async-start(bf16[8,8,1024]{2,1,0:T(8,128)(2,1)} %get-tuple-element.8), calls=%async_computation | async-start | bytes 262144 | tf_op jit(solution)/shard_map/all_to_all | solution.py:270
  11.6 5.5 %copy-start.1 = (f32[4]{0:T(128)S(1)}, f32[4]{0:T(128)}, u32[]{:S(2)}) copy-start(f32[4]{0:T(128)} %gains.1) | copy-start | bytes 52
  11.6 5.5 %copy-start.2 = (f32[4]{0:T(128)S(1)}, f32[4]{0:T(128)}, u32[]{:S(2)}) copy-start(f32[4]{0:T(128)} %strengths.1) | copy-start | bytes 52
  11.6 19.3 %copy-start = (f32[2,1,2,1024]{3,2,1,0:T(2,128)S(1)}, f32[2,1,2,1024]{3,2,1,0:T(2,128)}, u32[]{:S(2)}) copy-start(f32[2,1,2,1024]{3,2,1,0:T(2,128)} %momenta.1) | copy-start | bytes 49156

commit v3 on v2

--- a/solution.py
+++ b/solution.py
@@ -41,17 +41,10 @@
     sign = np.where(is_sin, -1.0, 1.0)[:, None]
     even = 0.5 * (here + there) * count
     odd = 0.5 * (here - there) * count
-    tables = np.stack(
-        [
-            split_table(basis.T),
-            split_table(basis),
-            split_table(slope.T),
-            split_table(basis[order]),
-            split_table(slope[order]),
-        ]
-    )
-    mixers = np.stack([even, even.T, odd * sign, -(odd * sign).T]).astype(ml_dtypes.bfloat16)
-    return np.concatenate([tables.reshape(-1, GRID, GRID), mixers])
+    mixers = np.stack([even, even.T, odd * sign, -(odd * sign).T])
+    tables = [basis.T, basis, slope.T, basis[order], slope[order]]
+    tables = [*(split_table(table) for table in tables), mixers]
+    return np.concatenate([table.astype(ml_dtypes.bfloat16) for table in tables])
 
 
 def dot(a, b):
@@ -67,8 +60,13 @@
     return high, (x - high.astype(f32)).astype(bf16)
 
 
-def product(a, b):
-    return dot(a[0], b[0]) + dot(a[0], b[1]) + dot(a[1], b[0])
+def wide(x, axis):
+    high, low = halves(x)
+    return jnp.concatenate([high, low, high], axis=axis)
+
+
+def long(table, axis):
+    return jnp.concatenate([table[0], table[0], table[1]], axis=axis)
 
 
 def pack_kernel(cells, charges, fill, marks, green, out, copies, message):
@@ -122,19 +120,19 @@
             densities[beam] = densities[beam] + dot_nt(
                 jnp.concatenate(col_hots, axis=1), jnp.concatenate(row_hots, axis=1)
             )
-    densities = [halves(density) for density in densities]
     fetch.wait()
-    tables = [(near[2 * which], near[2 * which + 1]) for which in range(5)]
-    mixers = [near[10 + which] for which in range(4)]
     alpha, beta = (
-        dot(mixers[side], turned[0]) + dot(mixers[side], turned[1])
+        dot(near[side], turned[0]) + dot(near[side], turned[1])
         for side, turned in (
-            (side, halves(dot(gathered[...], mixers[side + 1]))) for side in (0, 2)
+            (side, halves(dot(gathered[...], near[side + 1]))) for side in (10, 12)
         )
     )
+    first = dot(long(near[0:2], 1), wide(jnp.concatenate(densities, axis=1), 0))
+    first = jnp.concatenate([first[:, :GRID], first[:, GRID:]], axis=0)
+    spectra = dot(wide(first, 1), long(near[2:4], 0))
+    scaled = []
     for beam in range(2):
-        first = halves(product(tables[0], densities[beam]))
-        spectrum = product(first, tables[1])
+        spectrum = spectra[beam * GRID : (beam + 1) * GRID]
         swapped = jnp.concatenate(
             [
                 jnp.concatenate([spectrum[HALF:, HALF:], spectrum[HALF:, :HALF]], axis=1),
@@ -142,11 +140,17 @@
             ],
             axis=0,
         )
-        scaled = halves(alpha * spectrum + beta * swapped)
-        for axis, (inner, outer) in enumerate(((2, 3), (0, 4))):
-            part = halves(product(scaled, tables[inner]))
-            field = product(tables[outer], part)
-            out[beam, axis * GRID : (axis + 1) * GRID, :] = field.astype(bf16)
+        scaled.append(alpha * spectrum + beta * swapped)
+    scaled = wide(jnp.concatenate(scaled, axis=0), 1)
+    for axis, (inner, outer) in enumerate(((4, 6), (0, 8))):
+        part = dot(scaled, long(near[inner : inner + 2], 0)).astype(bf16)
+        part = jnp.concatenate([part[:GRID], part[GRID:]], axis=1)
+        table = jnp.concatenate([near[outer], near[outer + 1]], axis=1)
+        field = dot(table, jnp.concatenate([part, part], axis=0))
+        for beam in range(2):
+            out[beam, axis * GRID : (axis + 1) * GRID, :] = field[
+                :, beam * GRID : (beam + 1) * GRID
+            ].astype(bf16)
 
 
 def kick_kernel(count, index, gains, strengths, fields, queries, out):
@@ -175,12 +179,12 @@
                 rows = source[base + 1 : base + 2, start : start + block].astype(f32)
                 cols = source[base + 2 : base + 3, start : start + block].astype(f32)
                 band = jnp.floor(cols * (1.0 / OFFSET_CELLS))
-                inside = cols - band * OFFSET_CELLS
+                inside = jnp.broadcast_to(cols - band * OFFSET_CELLS, (BANDS, block))
                 hot = jnp.where(cells == rows, 1.0, 0.0).astype(bf16)
                 values = dot(fields[1 - beam], hot)
                 picked = [jnp.zeros((BANDS, block), f32) for _ in range(2)]
                 for place in range(OFFSET_CELLS):
-                    hit = jnp.broadcast_to(inside == place, (BANDS, block))
+                    hit = inside == place
                     for axis in range(2):
                         at = axis * GRID + place * BANDS
                         picked[axis] = jnp.where(hit, values[at : at + BANDS, :], picked[axis])

time: 31.9 us -> 30.3 us (0.950)
  Pallas kernels: 12.4 us -> 10.8 us
    pallas_call x1, Pallas kernels: 4.68 us -> 3.46 us  [body(): pl.pallas_call(functools.partial(kick_kernel, count), out_shape=jax.Shape...]
    pallas_call x1, Pallas kernels: 5.46 us -> 5.08 us  [body(): pl.pallas_call(functools.partial(field_kernel, tiles), out_shape=jax.Shap...]
where the time goes in v3:
time: 30.3 us; the launch traced here: 30 us
  Pallas kernels  10.8 us (36%)
  starting transfers between devices  9.56 us (32%)
  blocking collectives  9.09 us (30%)
  waiting for transfers between devices  0.48 us (2%)
    all_to_all x1, blocking collectives, body(): lax.all_to_all(kicks, 'bunch', split_axis=0, concat_axis=0, tiled=True)  9.09 us
    ppermute x3, starting transfers between devices, exchanged(): return lax.ppermute(value, axis, pairs)  5.62 us
    pallas_call x1, Pallas kernels, body(): pl.pallas_call(functools.partial(field_kernel, tiles), out_shape=jax.Shap...  5.08 us
    all_to_all x1, starting transfers between devices, body(): lax.all_to_all(copies, 'bunch', split_axis=0, concat_axis=0, tiled=True)  3.94 us
    pallas_call x1, Pallas kernels, body(): pl.pallas_call(functools.partial(kick_kernel, count), out_shape=jax.Shape...  3.46 us
    pallas_call x1, Pallas kernels, body(): pl.pallas_call(pack_kernel, out_shape=(jax.ShapeDtypeStruct((8, particles...  1.59 us
    pallas_call x1, Pallas kernels, body(): pl.pallas_call(functools.partial(final_kernel, count), out_shape=jax.Shap...  0.64 us
  transfers between devices with their start and end apart: 4, of which 1 were waited for; matrix products, arithmetic and copies ran while one was open for 0% of the time, Pallas kernels for 17%

profile of v3, /device:TPU:0, one launch (start us, length us, event | category | flops | bytes accessed | tf_op | source)
XLA Modules:
  0.0 30.0 jit_solution(14154900002208760066)
XLA Ops:
  0.0 1.6 %shard_map.91 = (bf16[8,1024]{1,0:T(8,128)(2,1)}, bf16[8,8,1024]{2,1,0:T(8,128)(2,1)}, bf16[96,256]{1,0:T(8,128)(2,1)S(1)}) custom-call(s32[2,1,2,1024]{3,2,1,0:T(2,128)} %cells.1, bf16[2,1024]{1,0:T(2,128)(2,1)} %bitcast.7, s32[1,2]{1,0:T(1,128)} %bitcast.9, s32[2,2,1,4]{3,2,1,0:T(1,128)} %bitcast.8, f32[64,256]{1,0:T(8,128)} %bitcast.6), custom_call_target="tpu_custom_call" | custom-call | tf_op jit(solution)/shard_map/pallas_call | solution.py:256
  1.6 5.0 %collective-permute-start.2 = (bf16[96,256]{1,0:T(8,128)(2,1)S(1)}, bf16[96,256]{1,0:T(8,128)(2,1)S(1)}, u32[]{:S(2)}, u32[]{:S(2)}) collective-permute-start(bf16[96,256]{1,0:T(8,128)(2,1)S(1)} %get-tuple-element.7.refs_0_), channel_id=1, source_target_pairs={{0,3},{1,2},{2,1},{3,0},{4,7},{5,6},{6,5},{7,4},{8,11},{9,10},{10,... | collective-permute-start | bytes 147464 | tf_op jit(solution)/shard_map/ppermute | solution.py:245
  6.6 0.0 collective-permute-start.1
  6.6 0.6 %collective-permute-start = (bf16[96,256]{1,0:T(8,128)(2,1)S(1)}, bf16[96,256]{1,0:T(8,128)(2,1)S(1)}, u32[]{:S(2)}, u32[]{:S(2)}) collective-permute-start(bf16[96,256]{1,0:T(8,128)(2,1)S(1)} %get-tuple-element.7.refs_0_), channel_id=1, source_target_pairs={{0,1},{1,0},{2,3},{3,2},{4,5},{5,4},{6,7},{7,6},{8,9},{9,8},{10,11... | collective-permute-start | bytes 147464 | tf_op jit(solution)/shard_map/ppermute | solution.py:245
  7.2 3.9 %all-to-all-start = ((bf16[8,8,1024]{2,1,0:T(8,128)(2,1)}), bf16[8,8,1024]{2,1,0:T(8,128)(2,1)S(1)}, u32[]{:S(2)}, u32[]{:S(2)}) async-start(bf16[8,8,1024]{2,1,0:T(8,128)(2,1)} %get-tuple-element.8), calls=%async_computation | async-start | bytes 262144 | tf_op jit(solution)/shard_map/all_to_all | solution.py:274
  11.2 0.0 collective-permute-done.2.refs_3_
  11.2 0.5 %collective-permute-done.1.refs_2_ = bf16[96,256]{1,0:T(8,128)(2,1)S(1)} collective-permute-done((bf16[96,256]{1,0:T(8,128)(2,1)S(1)}, bf16[96,256]{1,0:T(8,128)(2,1)S(1)}, u32[]{:S(2)}, u32[]{:S(2)}) %collective-permute-start.1) | collective-permute-done | bytes 49184 | tf_op jit(solution)/shard_map/ppermute | solution.py:245
  11.6 0.0 collective-permute-done.refs_1_
  11.6 0.0 copy-start.1
  11.6 0.0 copy-start.2
  11.6 0.0 copy-start
  11.6 5.1 %shard_map.92.fields = bf16[2,512,256]{2,1,0:T(8,128)(2,1)S(1)} custom-call(s32[1]{0:T(128)} %bitcast.1.index, bf16[96,256]{1,0:T(8,128)(2,1)S(1)} %get-tuple-element.7.refs_0_, bf16[96,256]{1,0:T(8,128)(2,1)S(1)} %collective-permute-done.refs_1_, bf16[96,256]{1,0:T(8,128)(2,1)S(1)} %collective-permute-done.1.refs_2_, ...), custom_call_target="tpu_custom_call" | custom-call | flops 3000000000 | bytes 1000000 | tf_op jit(solution)/shard_map/pallas_call | solution.py:275
  16.7 0.0 all-to-all-done.queries
  16.7 0.0 copy-done.1
  16.8 0.0 copy-done.2
  16.8 3.5 %shard_map.93 = f32[8,4,1024]{2,1,0:T(4,128)S(1)} custom-call(s32[1]{0:T(128)} %bitcast.index, f32[4]{0:T(128)S(1)} %copy-done.1, f32[4]{0:T(128)S(1)} %copy-done.2, bf16[2,512,256]{2,1,0:T(8,128)(2,1)S(1)} %shard_map.92.fields, bf16[8,8,1024]{2,1,0:T(8,128)(2,1)S(1)} %all-to-all-done.queries), custom_call_target="tpu_custom_call" | custom-call | tf_op jit(solution)/shard_map/pallas_call | solution.py:288
  20.2 9.1 %all_to_all.10.received = f32[8,4,1024]{2,1,0:T(4,128)S(1)} all-to-all(f32[8,4,1024]{2,1,0:T(4,128)S(1)} %shard_map.93), channel_id=1, replica_groups=mesh['bunch'=8,'tile'=4] {'bunch'}, dimensions={0} | all-to-all | bytes 262144 | tf_op jit(solution)/shard_map/all_to_all | solution.py:295
  29.3 0.0 copy-done
  29.3 0.6 %shard_map.94 = f32[2,1,2,1024]{3,2,1,0:T(2,128)} custom-call(s32[1]{0:T(128)} %bitcast.index, f32[8,4,1024]{2,1,0:T(4,128)S(1)} %all_to_all.10.received, f32[2,1,2,1024]{3,2,1,0:T(2,128)S(1)} %copy-done), custom_call_target="tpu_custom_call" | custom-call | tf_op jit(solution)/shard_map/pallas_call | solution.py:296
Async XLA Ops:
  1.6 9.6 %collective-permute-start.2 = (bf16[96,256]{1,0:T(8,128)(2,1)S(1)}, bf16[96,256]{1,0:T(8,128)(2,1)S(1)}, u32[]{:S(2)}, u32[]{:S(2)}) collective-permute-start(bf16[96,256]{1,0:T(8,128)(2,1)S(1)} %get-tuple-element.7.refs_0_), channel_id=1, source_target_pairs={{0,3},{1,2},{2,1},{3,0},{4,7},{5,6},{6,5},{7,4},{8,11},{9,10},{10,... | collective-permute-start | bytes 147464 | tf_op jit(solution)/shard_map/ppermute | solution.py:245
  6.6 5.0 %collective-permute-start.1 = (bf16[96,256]{1,0:T(8,128)(2,1)S(1)}, bf16[96,256]{1,0:T(8,128)(2,1)S(1)}, u32[]{:S(2)}, u32[]{:S(2)}) collective-permute-start(bf16[96,256]{1,0:T(8,128)(2,1)S(1)} %get-tuple-element.7.refs_0_), channel_id=1, source_target_pairs={{0,2},{1,3},{2,0},{3,1},{4,6},{5,7},{6,4},{7,5},{8,10},{9,11},{10,... | collective-permute-start | bytes 147464 | tf_op jit(solution)/shard_map/ppermute | solution.py:245
  6.6 5.0 %collective-permute-start = (bf16[96,256]{1,0:T(8,128)(2,1)S(1)}, bf16[96,256]{1,0:T(8,128)(2,1)S(1)}, u32[]{:S(2)}, u32[]{:S(2)}) collective-permute-start(bf16[96,256]{1,0:T(8,128)(2,1)S(1)} %get-tuple-element.7.refs_0_), channel_id=1, source_target_pairs={{0,1},{1,0},{2,3},{3,2},{4,5},{5,4},{6,7},{7,6},{8,9},{9,8},{10,11... | collective-permute-start | bytes 147464 | tf_op jit(solution)/shard_map/ppermute | solution.py:245
  7.2 9.5 %all-to-all-start = ((bf16[8,8,1024]{2,1,0:T(8,128)(2,1)}), bf16[8,8,1024]{2,1,0:T(8,128)(2,1)S(1)}, u32[]{:S(2)}, u32[]{:S(2)}) async-start(bf16[8,8,1024]{2,1,0:T(8,128)(2,1)} %get-tuple-element.8), calls=%async_computation | async-start | bytes 262144 | tf_op jit(solution)/shard_map/all_to_all | solution.py:274
  11.6 5.1 %copy-start.1 = (f32[4]{0:T(128)S(1)}, f32[4]{0:T(128)}, u32[]{:S(2)}) copy-start(f32[4]{0:T(128)} %gains.1) | copy-start | bytes 52
  11.6 5.1 %copy-start.2 = (f32[4]{0:T(128)S(1)}, f32[4]{0:T(128)}, u32[]{:S(2)}) copy-start(f32[4]{0:T(128)} %strengths.1) | copy-start | bytes 52
  11.6 17.7 %copy-start = (f32[2,1,2,1024]{3,2,1,0:T(2,128)S(1)}, f32[2,1,2,1024]{3,2,1,0:T(2,128)}, u32[]{:S(2)}) copy-start(f32[2,1,2,1024]{3,2,1,0:T(2,128)} %momenta.1) | copy-start | bytes 49156

commit v4 on v3

--- a/solution.py
+++ b/solution.py
@@ -97,7 +97,7 @@
 
 def field_kernel(tiles, index, *refs):
     messages = refs[:tiles]
-    far, out, near, gathered, arrived = refs[tiles:]
+    far, out, near, gathered, densities, arrived = refs[tiles:]
     fetch = pltpu.make_async_copy(far, near, arrived)
     fetch.start()
     lists = messages[0].shape[0] - GRID // tiles
@@ -105,21 +105,23 @@
     for step in range(tiles):
         start = pl.multiple_of(relative(index[0], step, tiles) * columns, columns)
         gathered[pl.ds(start, columns), :] = messages[step][lists:, :]
-    cells = lax.broadcasted_iota(jnp.int32, (GRID, GRID), 0).astype(f32)
-    densities = [jnp.zeros((GRID, GRID), f32) for _ in range(2)]
-    for message in messages:
+
+    @pl.when(index[0] >= 0)
+    def deposit():
+        cells = lax.broadcasted_iota(jnp.int32, (GRID, GRID), 0).astype(f32)
         for beam in range(2):
             row_hots, col_hots = [], []
-            for part in range(lists // 8):
-                base = 8 * part + 4 * beam
-                charge = message[base : base + 1, :].astype(f32)
-                rows = message[base + 1 : base + 2, :].astype(f32)
-                cols = message[base + 2 : base + 3, :].astype(f32)
-                row_hots.append(jnp.where(cells == rows, 1.0, 0.0).astype(bf16))
-                col_hots.append(jnp.where(cells == cols, charge, 0.0).astype(bf16))
-            densities[beam] = densities[beam] + dot_nt(
-                jnp.concatenate(col_hots, axis=1), jnp.concatenate(row_hots, axis=1)
-            )
+            for message in messages:
+                for part in range(lists // 8):
+                    base = 8 * part + 4 * beam
+                    charge = message[base : base + 1, :].astype(f32)
+                    rows = message[base + 1 : base + 2, :].astype(f32)
+                    cols = message[base + 2 : base + 3, :].astype(f32)
+                    row_hots.append(jnp.where(cells == rows, 1.0, 0.0).astype(bf16))
+                    col_hots.append(jnp.where(cells == cols, charge, 0.0).astype(bf16))
+            density = dot_nt(jnp.concatenate(col_hots, axis=1), jnp.concatenate(row_hots, axis=1))
+            densities[:, beam * GRID : (beam + 1) * GRID] = wide(density, 0)
+
     fetch.wait()
     alpha, beta = (
         dot(near[side], turned[0]) + dot(near[side], turned[1])
@@ -127,7 +129,7 @@
             (side, halves(dot(gathered[...], near[side + 1]))) for side in (10, 12)
         )
     )
-    first = dot(long(near[0:2], 1), wide(jnp.concatenate(densities, axis=1), 0))
+    first = dot(long(near[0:2], 1), densities[...])
     first = jnp.concatenate([first[:, :GRID], first[:, GRID:]], axis=0)
     spectra = dot(wide(first, 1), long(near[2:4], 0))
     scaled = []
@@ -280,6 +282,7 @@
         scratch_shapes=[
             pltpu.VMEM(tables.shape, bf16),
             pltpu.VMEM((GRID, GRID), bf16),
+            pltpu.VMEM((3 * GRID, 2 * GRID), bf16),
             pltpu.SemaphoreType.DMA,
         ],
         compiler_params=LIMIT,

time: 30.3 us -> 29.2 us (0.964)
  Pallas kernels: 10.8 us -> 9.72 us
  blocking collectives: 9.09 us -> 8.09 us
  waiting for transfers between devices: 0.48 us -> 1.48 us
    pallas_call x1, Pallas kernels: 5.08 us -> 4.03 us  [body(): pl.pallas_call(functools.partial(field_kernel, tiles), out_shape=jax.Shap...]
    all_to_all x1, waiting for transfers between devices: 0.01 us -> 1 us  [body(): lax.all_to_all(copies, 'bunch', split_axis=0, concat_axis=0, tiled=True)]
    all_to_all x1, blocking collectives: 9.09 us -> 8.09 us  [body(): lax.all_to_all(kicks, 'bunch', split_axis=0, concat_axis=0, tiled=True)]
  transfers between devices with their start and end apart: 4 -> 4, of which waited for: 1 -> 2; matrix products, arithmetic and copies ran while one was open for 0% -> 0% of each run, Pallas kernels for 17% -> 14%
where the time goes in v4:
time: 29.2 us; the launch traced here: 28.9 us
  Pallas kernels  9.72 us (33%)
  starting transfers between devices  9.56 us (33%)
  blocking collectives  8.09 us (28%)
  waiting for transfers between devices  1.48 us (5%)
    all_to_all x1, blocking collectives, body(): lax.all_to_all(kicks, 'bunch', split_axis=0, concat_axis=0, tiled=True)  8.09 us
    ppermute x3, starting transfers between devices, exchanged(): return lax.ppermute(value, axis, pairs)  5.62 us
    pallas_call x1, Pallas kernels, body(): pl.pallas_call(functools.partial(field_kernel, tiles), out_shape=jax.Shap...  4.03 us
    all_to_all x1, starting transfers between devices, body(): lax.all_to_all(copies, 'bunch', split_axis=0, concat_axis=0, tiled=True)  3.94 us
    pallas_call x1, Pallas kernels, body(): pl.pallas_call(functools.partial(kick_kernel, count), out_shape=jax.Shape...  3.46 us
    pallas_call x1, Pallas kernels, body(): pl.pallas_call(pack_kernel, out_shape=(jax.ShapeDtypeStruct((8, particles...  1.59 us
    all_to_all x1, waiting for transfers between devices, body(): lax.all_to_all(copies, 'bunch', split_axis=0, concat_axis=0, tiled=True)  1 us
    pallas_call x1, Pallas kernels, body(): pl.pallas_call(functools.partial(final_kernel, count), out_shape=jax.Shap...  0.64 us
  transfers between devices with their start and end apart: 4, of which 2 were waited for; matrix products, arithmetic and copies ran while one was open for 0% of the time, Pallas kernels for 14%

profile of v4, /device:TPU:0, one launch (start us, length us, event | category | flops | bytes accessed | tf_op | source)
XLA Modules:
  0.0 28.9 jit_solution(4298523851284280686)
XLA Ops:
  0.0 1.6 %shard_map.91 = (bf16[8,1024]{1,0:T(8,128)(2,1)}, bf16[8,8,1024]{2,1,0:T(8,128)(2,1)}, bf16[96,256]{1,0:T(8,128)(2,1)S(1)}) custom-call(s32[2,1,2,1024]{3,2,1,0:T(2,128)} %cells.1, bf16[2,1024]{1,0:T(2,128)(2,1)} %bitcast.7, s32[1,2]{1,0:T(1,128)} %bitcast.9, s32[2,2,1,4]{3,2,1,0:T(1,128)} %bitcast.8, f32[64,256]{1,0:T(8,128)} %bitcast.6), custom_call_target="tpu_custom_call" | custom-call | tf_op jit(solution)/shard_map/pallas_call | solution.py:258
  1.6 5.0 %collective-permute-start.2 = (bf16[96,256]{1,0:T(8,128)(2,1)S(1)}, bf16[96,256]{1,0:T(8,128)(2,1)S(1)}, u32[]{:S(2)}, u32[]{:S(2)}) collective-permute-start(bf16[96,256]{1,0:T(8,128)(2,1)S(1)} %get-tuple-element.7.refs_0_), channel_id=1, source_target_pairs={{0,3},{1,2},{2,1},{3,0},{4,7},{5,6},{6,5},{7,4},{8,11},{9,10},{10,... | collective-permute-start | bytes 147464 | tf_op jit(solution)/shard_map/ppermute | solution.py:247
  6.6 0.0 collective-permute-start.1
  6.6 0.6 %collective-permute-start = (bf16[96,256]{1,0:T(8,128)(2,1)S(1)}, bf16[96,256]{1,0:T(8,128)(2,1)S(1)}, u32[]{:S(2)}, u32[]{:S(2)}) collective-permute-start(bf16[96,256]{1,0:T(8,128)(2,1)S(1)} %get-tuple-element.7.refs_0_), channel_id=1, source_target_pairs={{0,1},{1,0},{2,3},{3,2},{4,5},{5,4},{6,7},{7,6},{8,9},{9,8},{10,11... | collective-permute-start | bytes 147464 | tf_op jit(solution)/shard_map/ppermute | solution.py:247
  7.2 3.9 %all-to-all-start = ((bf16[8,8,1024]{2,1,0:T(8,128)(2,1)}), bf16[8,8,1024]{2,1,0:T(8,128)(2,1)S(1)}, u32[]{:S(2)}, u32[]{:S(2)}) async-start(bf16[8,8,1024]{2,1,0:T(8,128)(2,1)} %get-tuple-element.8), calls=%async_computation | async-start | bytes 262144 | tf_op jit(solution)/shard_map/all_to_all | solution.py:276
  11.2 0.0 collective-permute-done.2.refs_3_
  11.2 0.5 %collective-permute-done.1.refs_2_ = bf16[96,256]{1,0:T(8,128)(2,1)S(1)} collective-permute-done((bf16[96,256]{1,0:T(8,128)(2,1)S(1)}, bf16[96,256]{1,0:T(8,128)(2,1)S(1)}, u32[]{:S(2)}, u32[]{:S(2)}) %collective-permute-start.1) | collective-permute-done | bytes 49184 | tf_op jit(solution)/shard_map/ppermute | solution.py:247
  11.6 0.0 collective-permute-done.refs_1_
  11.6 0.0 copy-start.1
  11.6 0.0 copy-start.2
  11.6 0.0 copy-start
  11.6 4.0 %shard_map.92.fields = bf16[2,512,256]{2,1,0:T(8,128)(2,1)S(1)} custom-call(s32[1]{0:T(128)} %bitcast.1.index, bf16[96,256]{1,0:T(8,128)(2,1)S(1)} %get-tuple-element.7.refs_0_, bf16[96,256]{1,0:T(8,128)(2,1)S(1)} %collective-permute-done.refs_1_, bf16[96,256]{1,0:T(8,128)(2,1)S(1)} %collective-permute-done.1.refs_2_, ...), custom_call_target="tpu_custom_call" | custom-call | flops 3000000000 | bytes 1000000 | tf_op jit(solution)/shard_map/pallas_call | solution.py:277
  15.7 1.0 %all-to-all-done.queries = bf16[8,8,1024]{2,1,0:T(8,128)(2,1)S(1)} async-done(((bf16[8,8,1024]{2,1,0:T(8,128)(2,1)}), bf16[8,8,1024]{2,1,0:T(8,128)(2,1)S(1)}, u32[]{:S(2)}, u32[]{:S(2)}) %all-to-all-start) | async-done | bytes 131104 | tf_op jit(solution)/shard_map/all_to_all | solution.py:276
  16.7 0.0 copy-done.1
  16.7 0.0 copy-done.2
  16.7 3.5 %shard_map.93 = f32[8,4,1024]{2,1,0:T(4,128)S(1)} custom-call(s32[1]{0:T(128)} %bitcast.index, f32[4]{0:T(128)S(1)} %copy-done.1, f32[4]{0:T(128)S(1)} %copy-done.2, bf16[2,512,256]{2,1,0:T(8,128)(2,1)S(1)} %shard_map.92.fields, bf16[8,8,1024]{2,1,0:T(8,128)(2,1)S(1)} %all-to-all-done.queries), custom_call_target="tpu_custom_call" | custom-call | tf_op jit(solution)/shard_map/pallas_call | solution.py:291
  20.2 8.1 %all_to_all.10.received = f32[8,4,1024]{2,1,0:T(4,128)S(1)} all-to-all(f32[8,4,1024]{2,1,0:T(4,128)S(1)} %shard_map.93), channel_id=1, replica_groups=mesh['bunch'=8,'tile'=4] {'bunch'}, dimensions={0} | all-to-all | bytes 262144 | tf_op jit(solution)/shard_map/all_to_all | solution.py:298
  28.2 0.0 copy-done
  28.3 0.6 %shard_map.94 = f32[2,1,2,1024]{3,2,1,0:T(2,128)} custom-call(s32[1]{0:T(128)} %bitcast.index, f32[8,4,1024]{2,1,0:T(4,128)S(1)} %all_to_all.10.received, f32[2,1,2,1024]{3,2,1,0:T(2,128)S(1)} %copy-done), custom_call_target="tpu_custom_call" | custom-call | tf_op jit(solution)/shard_map/pallas_call | solution.py:299
Async XLA Ops:
  1.6 9.6 %collective-permute-start.2 = (bf16[96,256]{1,0:T(8,128)(2,1)S(1)}, bf16[96,256]{1,0:T(8,128)(2,1)S(1)}, u32[]{:S(2)}, u32[]{:S(2)}) collective-permute-start(bf16[96,256]{1,0:T(8,128)(2,1)S(1)} %get-tuple-element.7.refs_0_), channel_id=1, source_target_pairs={{0,3},{1,2},{2,1},{3,0},{4,7},{5,6},{6,5},{7,4},{8,11},{9,10},{10,... | collective-permute-start | bytes 147464 | tf_op jit(solution)/shard_map/ppermute | solution.py:247
  6.6 5.0 %collective-permute-start.1 = (bf16[96,256]{1,0:T(8,128)(2,1)S(1)}, bf16[96,256]{1,0:T(8,128)(2,1)S(1)}, u32[]{:S(2)}, u32[]{:S(2)}) collective-permute-start(bf16[96,256]{1,0:T(8,128)(2,1)S(1)} %get-tuple-element.7.refs_0_), channel_id=1, source_target_pairs={{0,2},{1,3},{2,0},{3,1},{4,6},{5,7},{6,4},{7,5},{8,10},{9,11},{10,... | collective-permute-start | bytes 147464 | tf_op jit(solution)/shard_map/ppermute | solution.py:247
  6.6 5.0 %collective-permute-start = (bf16[96,256]{1,0:T(8,128)(2,1)S(1)}, bf16[96,256]{1,0:T(8,128)(2,1)S(1)}, u32[]{:S(2)}, u32[]{:S(2)}) collective-permute-start(bf16[96,256]{1,0:T(8,128)(2,1)S(1)} %get-tuple-element.7.refs_0_), channel_id=1, source_target_pairs={{0,1},{1,0},{2,3},{3,2},{4,5},{5,4},{6,7},{7,6},{8,9},{9,8},{10,11... | collective-permute-start | bytes 147464 | tf_op jit(solution)/shard_map/ppermute | solution.py:247
  7.2 9.5 %all-to-all-start = ((bf16[8,8,1024]{2,1,0:T(8,128)(2,1)}), bf16[8,8,1024]{2,1,0:T(8,128)(2,1)S(1)}, u32[]{:S(2)}, u32[]{:S(2)}) async-start(bf16[8,8,1024]{2,1,0:T(8,128)(2,1)} %get-tuple-element.8), calls=%async_computation | async-start | bytes 262144 | tf_op jit(solution)/shard_map/all_to_all | solution.py:276
  11.6 5.1 %copy-start.1 = (f32[4]{0:T(128)S(1)}, f32[4]{0:T(128)}, u32[]{:S(2)}) copy-start(f32[4]{0:T(128)} %gains.1) | copy-start | bytes 52
  11.6 5.1 %copy-start.2 = (f32[4]{0:T(128)S(1)}, f32[4]{0:T(128)}, u32[]{:S(2)}) copy-start(f32[4]{0:T(128)} %strengths.1) | copy-start | bytes 52
  11.6 16.6 %copy-start = (f32[2,1,2,1024]{3,2,1,0:T(2,128)S(1)}, f32[2,1,2,1024]{3,2,1,0:T(2,128)}, u32[]{:S(2)}) copy-start(f32[2,1,2,1024]{3,2,1,0:T(2,128)} %momenta.1) | copy-start | bytes 49156

commit v5 on v4

--- a/solution.py
+++ b/solution.py
@@ -16,6 +16,7 @@
 OFFSET_CELLS = 32
 BANDS = GRID // OFFSET_CELLS
 REACH = STOPS + 1
+INVERSE_TABLES = 6
 f32 = jnp.float32
 bf16 = jnp.bfloat16
 
@@ -42,8 +43,9 @@
     even = 0.5 * (here + there) * count
     odd = 0.5 * (here - there) * count
     mixers = np.stack([even, even.T, odd * sign, -(odd * sign).T])
-    tables = [basis.T, basis, slope.T, basis[order], slope[order]]
-    tables = [*(split_table(table) for table in tables), mixers]
+    forward = [split_table(basis.T), split_table(basis)]
+    inverse = [split_table(table) for table in (slope.T, basis[order], slope[order])]
+    tables = [*forward, mixers, *inverse]
     return np.concatenate([table.astype(ml_dtypes.bfloat16) for table in tables])
 
 
@@ -98,8 +100,13 @@
 def field_kernel(tiles, index, *refs):
     messages = refs[:tiles]
     far, out, near, gathered, densities, arrived = refs[tiles:]
-    fetch = pltpu.make_async_copy(far, near, arrived)
-    fetch.start()
+    early = near.shape[0] - INVERSE_TABLES
+    fetch = [
+        pltpu.make_async_copy(far.at[:early], near.at[:early], arrived.at[0]),
+        pltpu.make_async_copy(far.at[early:], near.at[early:], arrived.at[1]),
+    ]
+    for copy in fetch:
+        copy.start()
     lists = messages[0].shape[0] - GRID // tiles
     columns = GRID // tiles
     for step in range(tiles):
@@ -122,11 +129,11 @@
             density = dot_nt(jnp.concatenate(col_hots, axis=1), jnp.concatenate(row_hots, axis=1))
             densities[:, beam * GRID : (beam + 1) * GRID] = wide(density, 0)
 
-    fetch.wait()
+    fetch[0].wait()
     alpha, beta = (
         dot(near[side], turned[0]) + dot(near[side], turned[1])
         for side, turned in (
-            (side, halves(dot(gathered[...], near[side + 1]))) for side in (10, 12)
+            (side, halves(dot(gathered[...], near[side + 1]))) for side in (4, 6)
         )
     )
     first = dot(long(near[0:2], 1), densities[...])
@@ -143,15 +150,16 @@
             axis=0,
         )
         scaled.append(alpha * spectrum + beta * swapped)
-    scaled = wide(jnp.concatenate(scaled, axis=0), 1)
-    for axis, (inner, outer) in enumerate(((4, 6), (0, 8))):
-        part = dot(scaled, long(near[inner : inner + 2], 0)).astype(bf16)
-        part = jnp.concatenate([part[:GRID], part[GRID:]], axis=1)
-        table = jnp.concatenate([near[outer], near[outer + 1]], axis=1)
-        field = dot(table, jnp.concatenate([part, part], axis=0))
+    fetch[1].wait()
+    left = jnp.concatenate([long(near[10:12], 1), long(near[12:14], 1)], axis=0)
+    part = dot(left, wide(jnp.concatenate(scaled, axis=1), 0)).astype(bf16)
+    for axis, right in enumerate((8, 0)):
+        rows = part[axis * GRID : (axis + 1) * GRID]
+        rows = jnp.concatenate([rows[:, :GRID], rows[:, GRID:]], axis=0)
+        field = dot(rows, near[right]) + dot(rows, near[right + 1])
         for beam in range(2):
             out[beam, axis * GRID : (axis + 1) * GRID, :] = field[
-                :, beam * GRID : (beam + 1) * GRID
+                beam * GRID : (beam + 1) * GRID
             ].astype(bf16)
 
 
@@ -283,7 +291,7 @@
             pltpu.VMEM(tables.shape, bf16),
             pltpu.VMEM((GRID, GRID), bf16),
             pltpu.VMEM((3 * GRID, 2 * GRID), bf16),
-            pltpu.SemaphoreType.DMA,
+            pltpu.SemaphoreType.DMA((2,)),
         ],
         compiler_params=LIMIT,
         cost_estimate=pl.CostEstimate(flops=3000000000, bytes_accessed=1000000, transcendentals=0),

time: 29.2 us -> 29 us (level)
  Pallas kernels: 9.72 us -> 9.33 us
  waiting for transfers between devices: 1.48 us -> 1.87 us
    all_to_all x1, waiting for transfers between devices: 1 us -> 1.39 us  [body(): lax.all_to_all(copies, 'bunch', split_axis=0, concat_axis=0, tiled=True)]
    pallas_call x1, Pallas kernels: 4.03 us -> 3.64 us  [body(): pl.pallas_call(functools.partial(field_kernel, tiles), out_shape=jax.Shap...]
  transfers between devices with their start and end apart: 4 -> 4, of which waited for: 2 -> 2; matrix products, arithmetic and copies ran while one was open for 0% -> 0% of each run, Pallas kernels for 14% -> 13%
where the time goes in v5:
time: 29 us; the launch traced here: 28.7 us
  starting transfers between devices  9.56 us (33%)
  Pallas kernels  9.33 us (32%)
  blocking collectives  7.92 us (27%)
  waiting for transfers between devices  1.87 us (6%)
    all_to_all x1, blocking collectives, body(): lax.all_to_all(kicks, 'bunch', split_axis=0, concat_axis=0, tiled=True)  7.92 us
    ppermute x3, starting transfers between devices, exchanged(): return lax.ppermute(value, axis, pairs)  5.62 us
    all_to_all x1, starting transfers between devices, body(): lax.all_to_all(copies, 'bunch', split_axis=0, concat_axis=0, tiled=True)  3.94 us
    pallas_call x1, Pallas kernels, body(): pl.pallas_call(functools.partial(field_kernel, tiles), out_shape=jax.Shap...  3.64 us
    pallas_call x1, Pallas kernels, body(): pl.pallas_call(functools.partial(kick_kernel, count), out_shape=jax.Shape...  3.46 us
    pallas_call x1, Pallas kernels, body(): pl.pallas_call(pack_kernel, out_shape=(jax.ShapeDtypeStruct((8, particles...  1.59 us
    all_to_all x1, waiting for transfers between devices, body(): lax.all_to_all(copies, 'bunch', split_axis=0, concat_axis=0, tiled=True)  1.39 us
    pallas_call x1, Pallas kernels, body(): pl.pallas_call(functools.partial(final_kernel, count), out_shape=jax.Shap...  0.64 us
  transfers between devices with their start and end apart: 4, of which 2 were waited for; matrix products, arithmetic and copies ran while one was open for 0% of the time, Pallas kernels for 13%

profile of v5, /device:TPU:0, one launch (start us, length us, event | category | flops | bytes accessed | tf_op | source)
XLA Modules:
  0.0 28.7 jit_solution(4937197789735260000)
XLA Ops:
  0.0 1.6 %shard_map.91 = (bf16[8,1024]{1,0:T(8,128)(2,1)}, bf16[8,8,1024]{2,1,0:T(8,128)(2,1)}, bf16[96,256]{1,0:T(8,128)(2,1)S(1)}) custom-call(s32[2,1,2,1024]{3,2,1,0:T(2,128)} %cells.1, bf16[2,1024]{1,0:T(2,128)(2,1)} %bitcast.7, s32[1,2]{1,0:T(1,128)} %bitcast.9, s32[2,2,1,4]{3,2,1,0:T(1,128)} %bitcast.8, f32[64,256]{1,0:T(8,128)} %bitcast.6), custom_call_target="tpu_custom_call" | custom-call | tf_op jit(solution)/shard_map/pallas_call | solution.py:266
  1.6 5.0 %collective-permute-start.2 = (bf16[96,256]{1,0:T(8,128)(2,1)S(1)}, bf16[96,256]{1,0:T(8,128)(2,1)S(1)}, u32[]{:S(2)}, u32[]{:S(2)}) collective-permute-start(bf16[96,256]{1,0:T(8,128)(2,1)S(1)} %get-tuple-element.7.refs_0_), channel_id=1, source_target_pairs={{0,3},{1,2},{2,1},{3,0},{4,7},{5,6},{6,5},{7,4},{8,11},{9,10},{10,... | collective-permute-start | bytes 147464 | tf_op jit(solution)/shard_map/ppermute | solution.py:255
  6.6 0.0 collective-permute-start.1
  6.6 0.6 %collective-permute-start = (bf16[96,256]{1,0:T(8,128)(2,1)S(1)}, bf16[96,256]{1,0:T(8,128)(2,1)S(1)}, u32[]{:S(2)}, u32[]{:S(2)}) collective-permute-start(bf16[96,256]{1,0:T(8,128)(2,1)S(1)} %get-tuple-element.7.refs_0_), channel_id=1, source_target_pairs={{0,1},{1,0},{2,3},{3,2},{4,5},{5,4},{6,7},{7,6},{8,9},{9,8},{10,11... | collective-permute-start | bytes 147464 | tf_op jit(solution)/shard_map/ppermute | solution.py:255
  7.2 3.9 %all-to-all-start = ((bf16[8,8,1024]{2,1,0:T(8,128)(2,1)}), bf16[8,8,1024]{2,1,0:T(8,128)(2,1)S(1)}, u32[]{:S(2)}, u32[]{:S(2)}) async-start(bf16[8,8,1024]{2,1,0:T(8,128)(2,1)} %get-tuple-element.8), calls=%async_computation | async-start | bytes 262144 | tf_op jit(solution)/shard_map/all_to_all | solution.py:284
  11.2 0.0 collective-permute-done.2.refs_3_
  11.2 0.5 %collective-permute-done.1.refs_2_ = bf16[96,256]{1,0:T(8,128)(2,1)S(1)} collective-permute-done((bf16[96,256]{1,0:T(8,128)(2,1)S(1)}, bf16[96,256]{1,0:T(8,128)(2,1)S(1)}, u32[]{:S(2)}, u32[]{:S(2)}) %collective-permute-start.1) | collective-permute-done | bytes 49184 | tf_op jit(solution)/shard_map/ppermute | solution.py:255
  11.6 0.0 collective-permute-done.refs_1_
  11.6 0.0 copy-start.1
  11.6 0.0 copy-start.2
  11.6 0.0 copy-start
  11.6 3.6 %shard_map.92.fields = bf16[2,512,256]{2,1,0:T(8,128)(2,1)S(1)} custom-call(s32[1]{0:T(128)} %bitcast.1.index, bf16[96,256]{1,0:T(8,128)(2,1)S(1)} %get-tuple-element.7.refs_0_, bf16[96,256]{1,0:T(8,128)(2,1)S(1)} %collective-permute-done.refs_1_, bf16[96,256]{1,0:T(8,128)(2,1)S(1)} %collective-permute-done.1.refs_2_, ...), custom_call_target="tpu_custom_call" | custom-call | flops 3000000000 | bytes 1000000 | tf_op jit(solution)/shard_map/pallas_call | solution.py:285
  15.3 1.4 %all-to-all-done.queries = bf16[8,8,1024]{2,1,0:T(8,128)(2,1)S(1)} async-done(((bf16[8,8,1024]{2,1,0:T(8,128)(2,1)}), bf16[8,8,1024]{2,1,0:T(8,128)(2,1)S(1)}, u32[]{:S(2)}, u32[]{:S(2)}) %all-to-all-start) | async-done | bytes 131104 | tf_op jit(solution)/shard_map/all_to_all | solution.py:284
  16.7 0.0 copy-done.1
  16.7 0.0 copy-done.2
  16.7 3.5 %shard_map.93 = f32[8,4,1024]{2,1,0:T(4,128)S(1)} custom-call(s32[1]{0:T(128)} %bitcast.index, f32[4]{0:T(128)S(1)} %copy-done.1, f32[4]{0:T(128)S(1)} %copy-done.2, bf16[2,512,256]{2,1,0:T(8,128)(2,1)S(1)} %shard_map.92.fields, bf16[8,8,1024]{2,1,0:T(8,128)(2,1)S(1)} %all-to-all-done.queries), custom_call_target="tpu_custom_call" | custom-call | tf_op jit(solution)/shard_map/pallas_call | solution.py:299
  20.2 7.9 %all_to_all.10.received = f32[8,4,1024]{2,1,0:T(4,128)S(1)} all-to-all(f32[8,4,1024]{2,1,0:T(4,128)S(1)} %shard_map.93), channel_id=1, replica_groups=mesh['bunch'=8,'tile'=4] {'bunch'}, dimensions={0} | all-to-all | bytes 262144 | tf_op jit(solution)/shard_map/all_to_all | solution.py:306
  28.1 0.0 copy-done
  28.1 0.6 %shard_map.94 = f32[2,1,2,1024]{3,2,1,0:T(2,128)} custom-call(s32[1]{0:T(128)} %bitcast.index, f32[8,4,1024]{2,1,0:T(4,128)S(1)} %all_to_all.10.received, f32[2,1,2,1024]{3,2,1,0:T(2,128)S(1)} %copy-done), custom_call_target="tpu_custom_call" | custom-call | tf_op jit(solution)/shard_map/pallas_call | solution.py:307
Async XLA Ops:
  1.6 9.6 %collective-permute-start.2 = (bf16[96,256]{1,0:T(8,128)(2,1)S(1)}, bf16[96,256]{1,0:T(8,128)(2,1)S(1)}, u32[]{:S(2)}, u32[]{:S(2)}) collective-permute-start(bf16[96,256]{1,0:T(8,128)(2,1)S(1)} %get-tuple-element.7.refs_0_), channel_id=1, source_target_pairs={{0,3},{1,2},{2,1},{3,0},{4,7},{5,6},{6,5},{7,4},{8,11},{9,10},{10,... | collective-permute-start | bytes 147464 | tf_op jit(solution)/shard_map/ppermute | solution.py:255
  6.6 5.0 %collective-permute-start.1 = (bf16[96,256]{1,0:T(8,128)(2,1)S(1)}, bf16[96,256]{1,0:T(8,128)(2,1)S(1)}, u32[]{:S(2)}, u32[]{:S(2)}) collective-permute-start(bf16[96,256]{1,0:T(8,128)(2,1)S(1)} %get-tuple-element.7.refs_0_), channel_id=1, source_target_pairs={{0,2},{1,3},{2,0},{3,1},{4,6},{5,7},{6,4},{7,5},{8,10},{9,11},{10,... | collective-permute-start | bytes 147464 | tf_op jit(solution)/shard_map/ppermute | solution.py:255
  6.6 5.0 %collective-permute-start = (bf16[96,256]{1,0:T(8,128)(2,1)S(1)}, bf16[96,256]{1,0:T(8,128)(2,1)S(1)}, u32[]{:S(2)}, u32[]{:S(2)}) collective-permute-start(bf16[96,256]{1,0:T(8,128)(2,1)S(1)} %get-tuple-element.7.refs_0_), channel_id=1, source_target_pairs={{0,1},{1,0},{2,3},{3,2},{4,5},{5,4},{6,7},{7,6},{8,9},{9,8},{10,11... | collective-permute-start | bytes 147464 | tf_op jit(solution)/shard_map/ppermute | solution.py:255
  7.2 9.5 %all-to-all-start = ((bf16[8,8,1024]{2,1,0:T(8,128)(2,1)}), bf16[8,8,1024]{2,1,0:T(8,128)(2,1)S(1)}, u32[]{:S(2)}, u32[]{:S(2)}) async-start(bf16[8,8,1024]{2,1,0:T(8,128)(2,1)} %get-tuple-element.8), calls=%async_computation | async-start | bytes 262144 | tf_op jit(solution)/shard_map/all_to_all | solution.py:284
  11.6 5.1 %copy-start.1 = (f32[4]{0:T(128)S(1)}, f32[4]{0:T(128)}, u32[]{:S(2)}) copy-start(f32[4]{0:T(128)} %gains.1) | copy-start | bytes 52
  11.6 5.1 %copy-start.2 = (f32[4]{0:T(128)S(1)}, f32[4]{0:T(128)}, u32[]{:S(2)}) copy-start(f32[4]{0:T(128)} %strengths.1) | copy-start | bytes 52
  11.6 16.4 %copy-start = (f32[2,1,2,1024]{3,2,1,0:T(2,128)S(1)}, f32[2,1,2,1024]{3,2,1,0:T(2,128)}, u32[]{:S(2)}) copy-start(f32[2,1,2,1024]{3,2,1,0:T(2,128)} %momenta.1) | copy-start | bytes 49156

commit v6 on v5

--- a/solution.py
+++ b/solution.py
@@ -17,6 +17,7 @@
 BANDS = GRID // OFFSET_CELLS
 REACH = STOPS + 1
 INVERSE_TABLES = 6
+LANES = 128
 f32 = jnp.float32
 bf16 = jnp.bfloat16
 
@@ -71,29 +72,34 @@
     return jnp.concatenate([table[0], table[0], table[1]], axis=axis)
 
 
-def pack_kernel(cells, charges, fill, marks, green, out, copies, message):
+def query_rows(rows, cols, up, down):
+    half = rows.shape[1] // 2
+    marks = [jnp.full((1, LANES), mark, f32) for mark in (up, down, 0.0, 0.0)]
+    places = [rows[:, :half], rows[:, half:], cols[:, :half], cols[:, half:]]
+    return [jnp.concatenate(pair, axis=1) for pair in zip(places, marks)]
+
+
+def pack_kernel(index, cells, charges, fill, marks, green, own, copies, message):
     particles = charges.shape[1]
-    width = particles // 8
+    count = copies.shape[0]
+    here = index[0]
+    lists = 8 * particles // GRID
     for beam in range(2):
-        rows = [
-            charges[beam : beam + 1, :].astype(f32) * fill[0, beam].astype(f32),
-            cells[beam, 0, 0:1, :].astype(f32),
-            cells[beam, 0, 1:2, :].astype(f32),
-        ]
-        group = lax.broadcasted_iota(jnp.int32, (1, particles), 1) // width
-        mark = jnp.zeros((1, particles), f32)
-        for offset in range(1, REACH):
-            mark = jnp.where(group == offset - 1, marks[beam, 0, 0, offset - 1].astype(f32), mark)
-        for offset in range(STOPS - 1):
-            mark = jnp.where(group == STOPS + offset, marks[beam, 1, 0, offset + 1].astype(f32), mark)
-        rows.append(mark)
-        for row, value in enumerate(rows):
-            out[4 * beam + row : 4 * beam + row + 1, :] = value.astype(bf16)
-    for copy in range(copies.shape[0]):
-        copies[copy] = out[...]
-    lists = 8 * particles // GRID
-    for part in range(particles // GRID):
-        message[8 * part : 8 * part + 8, :] = out[:, part * GRID : (part + 1) * GRID]
+        sign = 1 if beam == 0 else -1
+        charge = charges[beam : beam + 1, :].astype(f32) * fill[0, beam].astype(f32)
+        rows = cells[beam, 0, 0:1, :].astype(f32)
+        cols = cells[beam, 0, 1:2, :].astype(f32)
+        for part in range(particles // GRID):
+            lanes = slice(part * GRID, (part + 1) * GRID)
+            for row, value in enumerate((charge, rows, cols)):
+                at = 8 * part + 4 * beam + row
+                message[at : at + 1, :] = value[:, lanes].astype(bf16)
+        for offset in range(REACH):
+            up = marks[beam, 0, 0, offset - 1].astype(f32) if offset else 0.0
+            down = marks[beam, 1, 0, offset + 1].astype(f32) if offset < STOPS - 1 else 0.0
+            target = own if offset == 0 else copies.at[lax.rem(here + sign * offset + count, count)]
+            for row, value in enumerate(query_rows(rows, cols, up, down)):
+                target[4 * beam + row : 4 * beam + row + 1, :] = value.astype(bf16)
     message[lists:, :] = green[...].astype(bf16)
 
 
@@ -163,31 +169,31 @@
             ].astype(bf16)
 
 
-def kick_kernel(count, index, gains, strengths, fields, queries, out):
-    particles = queries.shape[2]
-    width = particles // 8
+def kick_kernel(count, index, gains, strengths, fields, own, queries, home, away):
+    half = queries.shape[-1] - LANES
     here = index[0]
-    block = 2 * width
+    block = 2 * LANES
     cells = lax.broadcasted_iota(jnp.int32, (GRID, block), 0).astype(f32)
     bands = lax.broadcasted_iota(jnp.int32, (BANDS, block), 0).astype(f32)
-    for offset in reversed(range(REACH)):
+    for offset in range(REACH):
         for beam in range(2):
             sign = 1 if beam == 0 else -1
             target = lax.rem(here - sign * offset + count, count)
-            source = queries.at[target]
+            source = queries.at[target] if offset else own
             base = 4 * beam
 
-            def weight_of(stop, group):
-                mark = source[base + 3 : base + 4, group * width : (group + 1) * width].astype(f32)
+            def weight_of(stop, row):
+                mark = source[base + row : base + row + 1, half:].astype(f32)
                 mark = mark * (gains[stop] * strengths[stop])
                 return jnp.concatenate([mark, mark], axis=1)
 
             middle = gains[offset] if offset < STOPS else None
-            up = weight_of(offset - 1, offset - 1) if offset else None
-            down = weight_of(offset + 1, STOPS + offset) if offset < STOPS - 1 else None
-            for start in range(0, particles, block):
-                rows = source[base + 1 : base + 2, start : start + block].astype(f32)
-                cols = source[base + 2 : base + 3, start : start + block].astype(f32)
+            up = weight_of(offset - 1, 0) if offset else None
+            down = weight_of(offset + 1, 1) if offset < STOPS - 1 else None
+            for start in range(0, 2 * half, block):
+                row, lanes = base + start // half, pl.ds(start % half, block)
+                rows = source[row : row + 1, lanes].astype(f32)
+                cols = source[row + 2 : row + 3, lanes].astype(f32)
                 band = jnp.floor(cols * (1.0 / OFFSET_CELLS))
                 inside = jnp.broadcast_to(cols - band * OFFSET_CELLS, (BANDS, block))
                 hot = jnp.where(cells == rows, 1.0, 0.0).astype(bf16)
@@ -205,24 +211,32 @@
                     weight = jnp.where(bands == band - 1, up, weight)
                 if down is not None:
                     weight = jnp.where(bands == band + 1, down, weight)
-                for axis in range(2):
-                    kick = jnp.sum(weight * picked[axis], axis=0, keepdims=True)
-                    out[target, 2 * beam + axis : 2 * beam + axis + 1, start : start + block] = kick
-
-
-def final_kernel(count, index, received, momenta, out):
+                kick = [jnp.sum(weight * value, axis=0, keepdims=True) for value in picked]
+                kick = jnp.concatenate(kick, axis=0)
+                if offset == 0:
+                    home[2 * beam : 2 * beam + 2, start : start + block] = kick
+                elif shared(offset, count):
+                    away[target, 2 * beam : 2 * beam + 2, start : start + block] = kick.astype(bf16)
+                else:
+                    away[target, :, start : start + block] = jnp.concatenate(halves(kick), axis=0)
+
+
+def shared(offset, count):
+    return 2 * offset == count
+
+
+def final_kernel(count, index, received, home, momenta, out):
     here = index[0]
     for beam in range(2):
         sign = 1 if beam == 0 else -1
-        for axis in range(2):
-            total = None
-            for offset in range(REACH):
-                source = lax.rem(here + sign * offset + count, count)
-                part = received[source, 2 * beam + axis : 2 * beam + axis + 1, :]
-                total = part if total is None else total + part
-            out[beam, 0, axis : axis + 1, :] = momenta[beam, 0, axis : axis + 1, :] + total.astype(
-                bf16
-            ).astype(f32)
+        total = home[2 * beam : 2 * beam + 2, :]
+        for offset in range(1, REACH):
+            part = received[lax.rem(here + sign * offset + count, count)].astype(f32)
+            if shared(offset, count):
+                total = total + part[2 * beam : 2 * beam + 2]
+            else:
+                total = total + (part[:2] + part[2:])
+        out[beam, 0] = momenta[beam, 0] + total.astype(bf16).astype(f32)
 
 
 SMEM = pl.BlockSpec(memory_space=pltpu.SMEM)
@@ -263,17 +277,18 @@
     bunch = lax.axis_index("bunch").astype(jnp.int32).reshape(1)
     tile = lax.axis_index("tile").astype(jnp.int32).reshape(1)
     columns = green_spectrum.shape[1]
-    pack, copies, message = pl.pallas_call(
+    own, copies, message = pl.pallas_call(
         pack_kernel,
         out_shape=(
-            jax.ShapeDtypeStruct((8, particles), bf16),
-            jax.ShapeDtypeStruct((count, 8, particles), bf16),
+            jax.ShapeDtypeStruct((8, particles // 2 + LANES), bf16),
+            jax.ShapeDtypeStruct((count, 8, particles // 2 + LANES), bf16),
             jax.ShapeDtypeStruct((8 * particles // GRID + columns, GRID), bf16),
         ),
-        in_specs=[VMEM, VMEM, SMEM, SMEM, VMEM],
+        in_specs=[SMEM, VMEM, VMEM, SMEM, SMEM, VMEM],
         out_specs=(VMEM, VMEM, VMEM),
         compiler_params=SMALL,
     )(
+        bunch,
         kept_far(cell_index),
         kept_far(charges.reshape(2, particles)),
         kept_far(fill_pattern.T),
@@ -296,21 +311,24 @@
         compiler_params=LIMIT,
         cost_estimate=pl.CostEstimate(flops=3000000000, bytes_accessed=1000000, transcendentals=0),
     )(tile, *messages, kept_far(jnp.asarray(tables)))
-    kicks = pl.pallas_call(
+    home, away = pl.pallas_call(
         functools.partial(kick_kernel, count),
-        out_shape=jax.ShapeDtypeStruct((count, 4, particles), f32),
-        in_specs=[SMEM, SMEM, SMEM, VMEM, VMEM],
-        out_specs=VMEM,
+        out_shape=(
+            jax.ShapeDtypeStruct((4, particles), f32),
+            jax.ShapeDtypeStruct((count, 4, particles), bf16),
+        ),
+        in_specs=[SMEM, SMEM, SMEM, VMEM, VMEM, VMEM],
+        out_specs=(VMEM, VMEM),
         compiler_params=LIMIT,
-    )(bunch, stop_gain, parasitic_gain, fields, queries)
-    received = lax.all_to_all(kicks, "bunch", split_axis=0, concat_axis=0, tiled=True)
+    )(bunch, stop_gain, parasitic_gain, fields, own, queries)
+    received = lax.all_to_all(away, "bunch", split_axis=0, concat_axis=0, tiled=True)
     return pl.pallas_call(
         functools.partial(final_kernel, count),
         out_shape=jax.ShapeDtypeStruct(momenta.shape, f32),
-        in_specs=[SMEM, VMEM, VMEM],
+        in_specs=[SMEM, VMEM, VMEM, VMEM],
         out_specs=VMEM,
         compiler_params=SMALL,
-    )(bunch, received, momenta)
+    )(bunch, received, home, momenta)
 
 
 def solution(mesh):

time: 29 us -> 28.3 us (0.976)
  waiting for transfers between devices: 1.87 us -> 1.44 us
    all_to_all x1, waiting for transfers between devices: 1.39 us -> 0.96 us  [body(): lax.all_to_all(copies, 'bunch', split_axis=0, concat_axis=0, tiled=True)]
where the time goes in v6:
time: 28.3 us; the launch traced here: 28 us
  starting transfers between devices  9.56 us (34%)
  Pallas kernels  9.36 us (33%)
  blocking collectives  7.64 us (27%)
  waiting for transfers between devices  1.44 us (5%)
    all_to_all x1, blocking collectives, body(): lax.all_to_all(away, 'bunch', split_axis=0, concat_axis=0, tiled=True)  7.64 us
    ppermute x3, starting transfers between devices, exchanged(): return lax.ppermute(value, axis, pairs)  5.62 us
    all_to_all x1, starting transfers between devices, body(): lax.all_to_all(copies, 'bunch', split_axis=0, concat_axis=0, tiled=True)  3.94 us
    pallas_call x1, Pallas kernels, body(): pl.pallas_call(functools.partial(field_kernel, tiles), out_shape=jax.Shap...  3.64 us
    pallas_call x1, Pallas kernels, body(): pl.pallas_call(functools.partial(kick_kernel, count), out_shape=(jax.Shap...  3.46 us
    pallas_call x1, Pallas kernels, body(): pl.pallas_call(pack_kernel, out_shape=(jax.ShapeDtypeStruct((8, particles...  1.62 us
    all_to_all x1, waiting for transfers between devices, body(): lax.all_to_all(copies, 'bunch', split_axis=0, concat_axis=0, tiled=True)  0.96 us
    pallas_call x1, Pallas kernels, body(): pl.pallas_call(functools.partial(final_kernel, count), out_shape=jax.Shap...  0.64 us
  transfers between devices with their start and end apart: 4, of which 2 were waited for; matrix products, arithmetic and copies ran while one was open for 0% of the time, Pallas kernels for 13%

profile of v6, /device:TPU:0, one launch (start us, length us, event | category | flops | bytes accessed | tf_op | source)
XLA Modules:
  0.0 28.0 jit_solution(10029114232921514715)
XLA Ops:
  0.0 1.6 %shard_map.91 = (bf16[8,640]{1,0:T(8,128)(2,1)S(1)}, bf16[8,8,640]{2,1,0:T(8,128)(2,1)}, bf16[96,256]{1,0:T(8,128)(2,1)S(1)}) custom-call(s32[1]{0:T(128)} %bitcast.index, s32[2,1,2,1024]{3,2,1,0:T(2,128)} %cells.1, bf16[2,1024]{1,0:T(2,128)(2,1)} %bitcast.7, s32[1,2]{1,0:T(1,128)} %bitcast.9, s32[2,2,1,4]{3,2,1,0:T(1,128)} %bitcast.8, f32[64,256]{1,0:T(8,128)} %bitcast.6), custom_call_target="tpu_custom_call" | custom-call | tf_op jit(solution)/shard_map/pallas_call | solution.py:280
  1.6 5.0 %collective-permute-start.2 = (bf16[96,256]{1,0:T(8,128)(2,1)S(1)}, bf16[96,256]{1,0:T(8,128)(2,1)S(1)}, u32[]{:S(2)}, u32[]{:S(2)}) collective-permute-start(bf16[96,256]{1,0:T(8,128)(2,1)S(1)} %get-tuple-element.10.refs_0_), channel_id=1, source_target_pairs={{0,3},{1,2},{2,1},{3,0},{4,7},{5,6},{6,5},{7,4},{8,11},{9,10},{10,... | collective-permute-start | bytes 147464 | tf_op jit(solution)/shard_map/ppermute | solution.py:269
  6.7 0.0 collective-permute-start.1
  6.7 0.6 %collective-permute-start = (bf16[96,256]{1,0:T(8,128)(2,1)S(1)}, bf16[96,256]{1,0:T(8,128)(2,1)S(1)}, u32[]{:S(2)}, u32[]{:S(2)}) collective-permute-start(bf16[96,256]{1,0:T(8,128)(2,1)S(1)} %get-tuple-element.10.refs_0_), channel_id=1, source_target_pairs={{0,1},{1,0},{2,3},{3,2},{4,5},{5,4},{6,7},{7,6},{8,9},{9,8},{10,11... | collective-permute-start | bytes 147464 | tf_op jit(solution)/shard_map/ppermute | solution.py:269
  7.2 3.9 %all-to-all-start = ((bf16[8,8,640]{2,1,0:T(8,128)(2,1)}), bf16[8,8,640]{2,1,0:T(8,128)(2,1)S(1)}, u32[]{:S(2)}, u32[]{:S(2)}) async-start(bf16[8,8,640]{2,1,0:T(8,128)(2,1)} %get-tuple-element.12), calls=%async_computation | async-start | bytes 163840 | tf_op jit(solution)/shard_map/all_to_all | solution.py:299
  11.2 0.0 collective-permute-done.2.refs_3_
  11.2 0.5 %collective-permute-done.1.refs_2_ = bf16[96,256]{1,0:T(8,128)(2,1)S(1)} collective-permute-done((bf16[96,256]{1,0:T(8,128)(2,1)S(1)}, bf16[96,256]{1,0:T(8,128)(2,1)S(1)}, u32[]{:S(2)}, u32[]{:S(2)}) %collective-permute-start.1) | collective-permute-done | bytes 49184 | tf_op jit(solution)/shard_map/ppermute | solution.py:269
  11.7 0.0 collective-permute-done.refs_1_
  11.7 0.0 copy-start.1
  11.7 0.0 copy-start.2
  11.7 0.0 copy-start
  11.7 3.6 %shard_map.92.fields = bf16[2,512,256]{2,1,0:T(8,128)(2,1)S(1)} custom-call(s32[1]{0:T(128)} %bitcast.1.index, bf16[96,256]{1,0:T(8,128)(2,1)S(1)} %get-tuple-element.10.refs_0_, bf16[96,256]{1,0:T(8,128)(2,1)S(1)} %collective-permute-done.refs_1_, bf16[96,256]{1,0:T(8,128)(2,1)S(1)} %collective-permute-done.1.refs_2_, ...), custom_call_target="tpu_custom_call" | custom-call | flops 3000000000 | bytes 1000000 | tf_op jit(solution)/shard_map/pallas_call | solution.py:300
  15.3 1.0 %all-to-all-done.queries = bf16[8,8,640]{2,1,0:T(8,128)(2,1)S(1)} async-done(((bf16[8,8,640]{2,1,0:T(8,128)(2,1)}), bf16[8,8,640]{2,1,0:T(8,128)(2,1)S(1)}, u32[]{:S(2)}, u32[]{:S(2)}) %all-to-all-start) | async-done | bytes 81952 | tf_op jit(solution)/shard_map/all_to_all | solution.py:299
  16.3 0.0 copy-done.1
  16.3 0.0 copy-done.2
  16.3 3.5 %shard_map.93 = (f32[4,1024]{1,0:T(4,128)S(1)}, bf16[8,4,1024]{2,1,0:T(4,128)(2,1)S(1)}) custom-call(s32[1]{0:T(128)} %bitcast.index, f32[4]{0:T(128)S(1)} %copy-done.1, f32[4]{0:T(128)S(1)} %copy-done.2, bf16[2,512,256]{2,1,0:T(8,128)(2,1)S(1)} %shard_map.92.fields, bf16[8,640]{1,0:T(8,128)(2,1)S(1)} %get-tuple-element.11.own, ...), custom_call_target="tpu_custom_call" | custom-call | tf_op jit(solution)/shard_map/pallas_call | solution.py:314
  19.8 7.6 %all_to_all.10.received = bf16[8,4,1024]{2,1,0:T(4,128)(2,1)S(1)} all-to-all(bf16[8,4,1024]{2,1,0:T(4,128)(2,1)S(1)} %get-tuple-element.13), channel_id=1, replica_groups=mesh['bunch'=8,'tile'=4] {'bunch'}, dimensions={0} | all-to-all | bytes 131072 | tf_op jit(solution)/shard_map/all_to_all | solution.py:324
  27.4 0.0 copy-done
  27.4 0.6 %shard_map.94 = f32[2,1,2,1024]{3,2,1,0:T(2,128)} custom-call(s32[1]{0:T(128)} %bitcast.index, bf16[8,4,1024]{2,1,0:T(4,128)(2,1)S(1)} %all_to_all.10.received, f32[4,1024]{1,0:T(4,128)S(1)} %get-tuple-element.14.home, f32[2,1,2,1024]{3,2,1,0:T(2,128)S(1)} %copy-done), custom_call_target="tpu_custom_call" | custom-call | tf_op jit(solution)/shard_map/pallas_call | solution.py:325
Async XLA Ops:
  1.6 9.6 %collective-permute-start.2 = (bf16[96,256]{1,0:T(8,128)(2,1)S(1)}, bf16[96,256]{1,0:T(8,128)(2,1)S(1)}, u32[]{:S(2)}, u32[]{:S(2)}) collective-permute-start(bf16[96,256]{1,0:T(8,128)(2,1)S(1)} %get-tuple-element.10.refs_0_), channel_id=1, source_target_pairs={{0,3},{1,2},{2,1},{3,0},{4,7},{5,6},{6,5},{7,4},{8,11},{9,10},{10,... | collective-permute-start | bytes 147464 | tf_op jit(solution)/shard_map/ppermute | solution.py:269
  6.7 5.0 %collective-permute-start.1 = (bf16[96,256]{1,0:T(8,128)(2,1)S(1)}, bf16[96,256]{1,0:T(8,128)(2,1)S(1)}, u32[]{:S(2)}, u32[]{:S(2)}) collective-permute-start(bf16[96,256]{1,0:T(8,128)(2,1)S(1)} %get-tuple-element.10.refs_0_), channel_id=1, source_target_pairs={{0,2},{1,3},{2,0},{3,1},{4,6},{5,7},{6,4},{7,5},{8,10},{9,11},{10,... | collective-permute-start | bytes 147464 | tf_op jit(solution)/shard_map/ppermute | solution.py:269
  6.7 5.0 %collective-permute-start = (bf16[96,256]{1,0:T(8,128)(2,1)S(1)}, bf16[96,256]{1,0:T(8,128)(2,1)S(1)}, u32[]{:S(2)}, u32[]{:S(2)}) collective-permute-start(bf16[96,256]{1,0:T(8,128)(2,1)S(1)} %get-tuple-element.10.refs_0_), channel_id=1, source_target_pairs={{0,1},{1,0},{2,3},{3,2},{4,5},{5,4},{6,7},{7,6},{8,9},{9,8},{10,11... | collective-permute-start | bytes 147464 | tf_op jit(solution)/shard_map/ppermute | solution.py:269
  7.2 9.0 %all-to-all-start = ((bf16[8,8,640]{2,1,0:T(8,128)(2,1)}), bf16[8,8,640]{2,1,0:T(8,128)(2,1)S(1)}, u32[]{:S(2)}, u32[]{:S(2)}) async-start(bf16[8,8,640]{2,1,0:T(8,128)(2,1)} %get-tuple-element.12), calls=%async_computation | async-start | bytes 163840 | tf_op jit(solution)/shard_map/all_to_all | solution.py:299
  11.7 4.6 %copy-start.1 = (f32[4]{0:T(128)S(1)}, f32[4]{0:T(128)}, u32[]{:S(2)}) copy-start(f32[4]{0:T(128)} %gains.1) | copy-start | bytes 52
  11.7 4.6 %copy-start.2 = (f32[4]{0:T(128)S(1)}, f32[4]{0:T(128)}, u32[]{:S(2)}) copy-start(f32[4]{0:T(128)} %strengths.1) | copy-start | bytes 52
  11.7 15.7 %copy-start = (f32[2,1,2,1024]{3,2,1,0:T(2,128)S(1)}, f32[2,1,2,1024]{3,2,1,0:T(2,128)}, u32[]{:S(2)}) copy-start(f32[2,1,2,1024]{3,2,1,0:T(2,128)} %momenta.1) | copy-start | bytes 49156

commit v7 on v6

--- a/solution.py
+++ b/solution.py
@@ -79,10 +79,10 @@
     return [jnp.concatenate(pair, axis=1) for pair in zip(places, marks)]
 
 
-def pack_kernel(index, cells, charges, fill, marks, green, own, copies, message):
+def pack_kernel(cells, charges, fill, marks, gains, strengths, green, own, copies, message, factors):
     particles = charges.shape[1]
     count = copies.shape[0]
-    here = index[0]
+    here = lax.axis_index("bunch")
     lists = 8 * particles // GRID
     for beam in range(2):
         sign = 1 if beam == 0 else -1
@@ -101,9 +101,14 @@
             for row, value in enumerate(query_rows(rows, cols, up, down)):
                 target[4 * beam + row : 4 * beam + row + 1, :] = value.astype(bf16)
     message[lists:, :] = green[...].astype(bf16)
-
-
-def field_kernel(tiles, index, *refs):
+    for stop in range(STOPS):
+        factors[stop : stop + 1, :] = jnp.full((1, 2 * LANES), gains[stop], f32)
+        product = gains[stop] * strengths[stop]
+        factors[STOPS + stop : STOPS + stop + 1, :] = jnp.full((1, 2 * LANES), product, f32)
+
+
+def field_kernel(tiles, *refs):
+    here = lax.axis_index("tile")
     messages = refs[:tiles]
     far, out, near, gathered, densities, arrived = refs[tiles:]
     early = near.shape[0] - INVERSE_TABLES
@@ -116,10 +121,10 @@
     lists = messages[0].shape[0] - GRID // tiles
     columns = GRID // tiles
     for step in range(tiles):
-        start = pl.multiple_of(relative(index[0], step, tiles) * columns, columns)
+        start = pl.multiple_of(relative(here, step, tiles) * columns, columns)
         gathered[pl.ds(start, columns), :] = messages[step][lists:, :]
 
-    @pl.when(index[0] >= 0)
+    @pl.when(here >= 0)
     def deposit():
         cells = lax.broadcasted_iota(jnp.int32, (GRID, GRID), 0).astype(f32)
         for beam in range(2):
@@ -169,9 +174,9 @@
             ].astype(bf16)
 
 
-def kick_kernel(count, index, gains, strengths, fields, own, queries, home, away):
+def kick_kernel(count, factors, fields, own, queries, home, away):
     half = queries.shape[-1] - LANES
-    here = index[0]
+    here = lax.axis_index("bunch")
     block = 2 * LANES
     cells = lax.broadcasted_iota(jnp.int32, (GRID, block), 0).astype(f32)
     bands = lax.broadcasted_iota(jnp.int32, (BANDS, block), 0).astype(f32)
@@ -184,10 +189,9 @@
 
             def weight_of(stop, row):
                 mark = source[base + row : base + row + 1, half:].astype(f32)
-                mark = mark * (gains[stop] * strengths[stop])
-                return jnp.concatenate([mark, mark], axis=1)
-
-            middle = gains[offset] if offset < STOPS else None
+                return jnp.concatenate([mark, mark], axis=1) * factors[STOPS + stop : STOPS + stop + 1, :]
+
+            middle = factors[offset : offset + 1, :] if offset < STOPS else None
             up = weight_of(offset - 1, 0) if offset else None
             down = weight_of(offset + 1, 1) if offset < STOPS - 1 else None
             for start in range(0, 2 * half, block):
@@ -225,8 +229,8 @@
     return 2 * offset == count
 
 
-def final_kernel(count, index, received, home, momenta, out):
-    here = index[0]
+def final_kernel(count, received, home, momenta, out):
+    here = lax.axis_index("bunch")
     for beam in range(2):
         sign = 1 if beam == 0 else -1
         total = home[2 * beam : 2 * beam + 2, :]
@@ -274,25 +278,25 @@
     tiles = lax.axis_size("tile")
     count = lax.axis_size("bunch")
     tables = make_tables()
-    bunch = lax.axis_index("bunch").astype(jnp.int32).reshape(1)
-    tile = lax.axis_index("tile").astype(jnp.int32).reshape(1)
     columns = green_spectrum.shape[1]
-    own, copies, message = pl.pallas_call(
+    own, copies, message, factors = pl.pallas_call(
         pack_kernel,
         out_shape=(
             jax.ShapeDtypeStruct((8, particles // 2 + LANES), bf16),
             jax.ShapeDtypeStruct((count, 8, particles // 2 + LANES), bf16),
             jax.ShapeDtypeStruct((8 * particles // GRID + columns, GRID), bf16),
+            jax.ShapeDtypeStruct((2 * STOPS, 2 * LANES), f32),
         ),
-        in_specs=[SMEM, VMEM, VMEM, SMEM, SMEM, VMEM],
-        out_specs=(VMEM, VMEM, VMEM),
+        in_specs=[VMEM, VMEM, SMEM, SMEM, SMEM, SMEM, VMEM],
+        out_specs=(VMEM, VMEM, VMEM, VMEM),
         compiler_params=SMALL,
     )(
-        bunch,
         kept_far(cell_index),
         kept_far(charges.reshape(2, particles)),
         kept_far(fill_pattern.T),
         kept_far(jnp.transpose(encounters, (1, 2, 3, 0))),
+        kept_far(stop_gain),
+        kept_far(parasitic_gain),
         kept_far(green_spectrum.T),
     )
     messages = [message] + [exchanged(message, "tile", step) for step in range(1, tiles)]
@@ -300,7 +304,7 @@
     fields = pl.pallas_call(
         functools.partial(field_kernel, tiles),
         out_shape=jax.ShapeDtypeStruct((2, 2 * GRID, GRID), bf16),
-        in_specs=[SMEM] + [VMEM] * tiles + [FAR],
+        in_specs=[VMEM] * tiles + [FAR],
         out_specs=VMEM,
         scratch_shapes=[
             pltpu.VMEM(tables.shape, bf16),
@@ -310,25 +314,25 @@
         ],
         compiler_params=LIMIT,
         cost_estimate=pl.CostEstimate(flops=3000000000, bytes_accessed=1000000, transcendentals=0),
-    )(tile, *messages, kept_far(jnp.asarray(tables)))
+    )(*messages, kept_far(jnp.asarray(tables)))
     home, away = pl.pallas_call(
         functools.partial(kick_kernel, count),
         out_shape=(
             jax.ShapeDtypeStruct((4, particles), f32),
             jax.ShapeDtypeStruct((count, 4, particles), bf16),
         ),
-        in_specs=[SMEM, SMEM, SMEM, VMEM, VMEM, VMEM],
+        in_specs=[VMEM, VMEM, VMEM, VMEM],
         out_specs=(VMEM, VMEM),
         compiler_params=LIMIT,
-    )(bunch, stop_gain, parasitic_gain, fields, own, queries)
+    )(factors, fields, own, queries)
     received = lax.all_to_all(away, "bunch", split_axis=0, concat_axis=0, tiled=True)
     return pl.pallas_call(
         functools.partial(final_kernel, count),
         out_shape=jax.ShapeDtypeStruct(momenta.shape, f32),
-        in_specs=[SMEM, VMEM, VMEM, VMEM],
+        in_specs=[VMEM, VMEM, VMEM],
         out_specs=VMEM,
         compiler_params=SMALL,
-    )(bunch, received, home, momenta)
+    )(received, home, momenta)
 
 
 def solution(mesh):

time: 28.3 us -> 27.7 us (0.979)
  Pallas kernels: 9.36 us -> 8.82 us
    pallas_call x1, Pallas kernels: 3.46 us -> 2.92 us  [body(): pl.pallas_call(functools.partial(kick_kernel, count), out_shape=(jax.Shap...]
where the time goes in v7:
time: 27.7 us; the launch traced here: 27.5 us
  starting transfers between devices  9.56 us (35%)
  Pallas kernels  8.82 us (32%)
  blocking collectives  7.61 us (27%)
  waiting for transfers between devices  1.44 us (5%)
    all_to_all x1, blocking collectives, body(): lax.all_to_all(away, 'bunch', split_axis=0, concat_axis=0, tiled=True)  7.61 us
    ppermute x3, starting transfers between devices, exchanged(): return lax.ppermute(value, axis, pairs)  5.62 us
    all_to_all x1, starting transfers between devices, body(): lax.all_to_all(copies, 'bunch', split_axis=0, concat_axis=0, tiled=True)  3.94 us
    pallas_call x1, Pallas kernels, body(): pl.pallas_call(functools.partial(field_kernel, tiles), out_shape=jax.Shap...  3.64 us
    pallas_call x1, Pallas kernels, body(): pl.pallas_call(functools.partial(kick_kernel, count), out_shape=(jax.Shap...  2.92 us
    pallas_call x1, Pallas kernels, body(): pl.pallas_call(pack_kernel, out_shape=(jax.ShapeDtypeStruct((8, particles...  1.63 us
    all_to_all x1, waiting for transfers between devices, body(): lax.all_to_all(copies, 'bunch', split_axis=0, concat_axis=0, tiled=True)  0.97 us
    pallas_call x1, Pallas kernels, body(): pl.pallas_call(functools.partial(final_kernel, count), out_shape=jax.Shap...  0.64 us
  transfers between devices with their start and end apart: 4, of which 2 were waited for; matrix products, arithmetic and copies ran while one was open for 0% of the time, Pallas kernels for 13%

profile of v7, /device:TPU:0, one launch (start us, length us, event | category | flops | bytes accessed | tf_op | source)
XLA Modules:
  0.0 27.5 jit_solution(9464368693703981482)
XLA Ops:
  0.0 1.6 %shard_map.91 = (bf16[8,640]{1,0:T(8,128)(2,1)S(1)}, bf16[8,8,640]{2,1,0:T(8,128)(2,1)}, bf16[96,256]{1,0:T(8,128)(2,1)S(1)}, f32[8,256]{1,0:T(8,128)S(1)}) custom-call(s32[2,1,2,1024]{3,2,1,0:T(2,128)} %cells.1, bf16[2,1024]{1,0:T(2,128)(2,1)} %bitcast.5, s32[1,2]{1,0:T(1,128)} %bitcast.7, s32[2,2,1,4]{3,2,1,0:T(1,128)} %bitcast.6, f32[4]{0:T(128)} %gains.1, ...), custom_call_target="tpu_custom_call" | custom-call | tf_op jit(solution)/shard_map/pallas_call | solution.py:282
  1.6 5.0 %collective-permute-start.2 = (bf16[96,256]{1,0:T(8,128)(2,1)S(1)}, bf16[96,256]{1,0:T(8,128)(2,1)S(1)}, u32[]{:S(2)}, u32[]{:S(2)}) collective-permute-start(bf16[96,256]{1,0:T(8,128)(2,1)S(1)} %get-tuple-element.12.refs_0_), channel_id=1, source_target_pairs={{0,3},{1,2},{2,1},{3,0},{4,7},{5,6},{6,5},{7,4},{8,11},{9,10},{10,... | collective-permute-start | bytes 147464 | tf_op jit(solution)/shard_map/ppermute | solution.py:273
  6.7 0.0 collective-permute-start.1
  6.7 0.6 %collective-permute-start = (bf16[96,256]{1,0:T(8,128)(2,1)S(1)}, bf16[96,256]{1,0:T(8,128)(2,1)S(1)}, u32[]{:S(2)}, u32[]{:S(2)}) collective-permute-start(bf16[96,256]{1,0:T(8,128)(2,1)S(1)} %get-tuple-element.12.refs_0_), channel_id=1, source_target_pairs={{0,1},{1,0},{2,3},{3,2},{4,5},{5,4},{6,7},{7,6},{8,9},{9,8},{10,11... | collective-permute-start | bytes 147464 | tf_op jit(solution)/shard_map/ppermute | solution.py:273
  7.2 3.9 %all-to-all-start = ((bf16[8,8,640]{2,1,0:T(8,128)(2,1)}), bf16[8,8,640]{2,1,0:T(8,128)(2,1)S(1)}, u32[]{:S(2)}, u32[]{:S(2)}) async-start(bf16[8,8,640]{2,1,0:T(8,128)(2,1)} %get-tuple-element.14), calls=%async_computation | async-start | bytes 163840 | tf_op jit(solution)/shard_map/all_to_all | solution.py:303
  11.2 0.0 copy-start
  11.2 0.0 collective-permute-done.2.refs_3_
  11.2 0.5 %collective-permute-done.1.refs_2_ = bf16[96,256]{1,0:T(8,128)(2,1)S(1)} collective-permute-done((bf16[96,256]{1,0:T(8,128)(2,1)S(1)}, bf16[96,256]{1,0:T(8,128)(2,1)S(1)}, u32[]{:S(2)}, u32[]{:S(2)}) %collective-permute-start.1) | collective-permute-done | bytes 49184 | tf_op jit(solution)/shard_map/ppermute | solution.py:273
  11.7 0.0 collective-permute-done.refs_1_
  11.7 3.6 %shard_map.92.fields = bf16[2,512,256]{2,1,0:T(8,128)(2,1)S(1)} custom-call(bf16[96,256]{1,0:T(8,128)(2,1)S(1)} %get-tuple-element.12.refs_0_, bf16[96,256]{1,0:T(8,128)(2,1)S(1)} %collective-permute-done.refs_1_, bf16[96,256]{1,0:T(8,128)(2,1)S(1)} %collective-permute-done.1.refs_2_, bf16[96,256]{1,0:T(8,128)(2,1)S(1)} %collective-permute-done.2.refs_3_, ...), custom_call_target="tpu_custom_call" | custom-call | flops 3000000000 | bytes 1000000 | tf_op jit(solution)/shard_map/pallas_call | solution.py:304
  15.3 1.0 %all-to-all-done.queries = bf16[8,8,640]{2,1,0:T(8,128)(2,1)S(1)} async-done(((bf16[8,8,640]{2,1,0:T(8,128)(2,1)}), bf16[8,8,640]{2,1,0:T(8,128)(2,1)S(1)}, u32[]{:S(2)}, u32[]{:S(2)}) %all-to-all-start) | async-done | bytes 81952 | tf_op jit(solution)/shard_map/all_to_all | solution.py:303
  16.3 2.9 %shard_map.93 = (f32[4,1024]{1,0:T(4,128)S(1)}, bf16[8,4,1024]{2,1,0:T(4,128)(2,1)S(1)}) custom-call(f32[8,256]{1,0:T(8,128)S(1)} %get-tuple-element.11.factors, bf16[2,512,256]{2,1,0:T(8,128)(2,1)S(1)} %shard_map.92.fields, bf16[8,640]{1,0:T(8,128)(2,1)S(1)} %get-tuple-element.13.own, bf16[8,8,640]{2,1,0:T(8,128)(2,1)S(1)} %all-to-all-done.queries), custom_call_target="tpu_custom_call" | custom-call | tf_op jit(solution)/shard_map/pallas_call | solution.py:318
  19.2 7.6 %all_to_all.10.received = bf16[8,4,1024]{2,1,0:T(4,128)(2,1)S(1)} all-to-all(bf16[8,4,1024]{2,1,0:T(4,128)(2,1)S(1)} %get-tuple-element.15), channel_id=1, replica_groups=mesh['bunch'=8,'tile'=4] {'bunch'}, dimensions={0} | all-to-all | bytes 131072 | tf_op jit(solution)/shard_map/all_to_all | solution.py:328
  26.8 0.0 copy-done
  26.8 0.6 %shard_map.94 = f32[2,1,2,1024]{3,2,1,0:T(2,128)} custom-call(bf16[8,4,1024]{2,1,0:T(4,128)(2,1)S(1)} %all_to_all.10.received, f32[4,1024]{1,0:T(4,128)S(1)} %get-tuple-element.16.home, f32[2,1,2,1024]{3,2,1,0:T(2,128)S(1)} %copy-done), custom_call_target="tpu_custom_call" | custom-call | tf_op jit(solution)/shard_map/pallas_call | solution.py:329
Async XLA Ops:
  1.6 9.6 %collective-permute-start.2 = (bf16[96,256]{1,0:T(8,128)(2,1)S(1)}, bf16[96,256]{1,0:T(8,128)(2,1)S(1)}, u32[]{:S(2)}, u32[]{:S(2)}) collective-permute-start(bf16[96,256]{1,0:T(8,128)(2,1)S(1)} %get-tuple-element.12.refs_0_), channel_id=1, source_target_pairs={{0,3},{1,2},{2,1},{3,0},{4,7},{5,6},{6,5},{7,4},{8,11},{9,10},{10,... | collective-permute-start | bytes 147464 | tf_op jit(solution)/shard_map/ppermute | solution.py:273
  6.7 5.0 %collective-permute-start.1 = (bf16[96,256]{1,0:T(8,128)(2,1)S(1)}, bf16[96,256]{1,0:T(8,128)(2,1)S(1)}, u32[]{:S(2)}, u32[]{:S(2)}) collective-permute-start(bf16[96,256]{1,0:T(8,128)(2,1)S(1)} %get-tuple-element.12.refs_0_), channel_id=1, source_target_pairs={{0,2},{1,3},{2,0},{3,1},{4,6},{5,7},{6,4},{7,5},{8,10},{9,11},{10,... | collective-permute-start | bytes 147464 | tf_op jit(solution)/shard_map/ppermute | solution.py:273
  6.7 5.0 %collective-permute-start = (bf16[96,256]{1,0:T(8,128)(2,1)S(1)}, bf16[96,256]{1,0:T(8,128)(2,1)S(1)}, u32[]{:S(2)}, u32[]{:S(2)}) collective-permute-start(bf16[96,256]{1,0:T(8,128)(2,1)S(1)} %get-tuple-element.12.refs_0_), channel_id=1, source_target_pairs={{0,1},{1,0},{2,3},{3,2},{4,5},{5,4},{6,7},{7,6},{8,9},{9,8},{10,11... | collective-permute-start | bytes 147464 | tf_op jit(solution)/shard_map/ppermute | solution.py:273
  7.2 9.0 %all-to-all-start = ((bf16[8,8,640]{2,1,0:T(8,128)(2,1)}), bf16[8,8,640]{2,1,0:T(8,128)(2,1)S(1)}, u32[]{:S(2)}, u32[]{:S(2)}) async-start(bf16[8,8,640]{2,1,0:T(8,128)(2,1)} %get-tuple-element.14), calls=%async_computation | async-start | bytes 163840 | tf_op jit(solution)/shard_map/all_to_all | solution.py:303
  11.2 15.6 %copy-start = (f32[2,1,2,1024]{3,2,1,0:T(2,128)S(1)}, f32[2,1,2,1024]{3,2,1,0:T(2,128)}, u32[]{:S(2)}) copy-start(f32[2,1,2,1024]{3,2,1,0:T(2,128)} %momenta.1) | copy-start | bytes 49156

commit v8 on v7

--- a/solution.py
+++ b/solution.py
@@ -79,7 +79,21 @@
     return [jnp.concatenate(pair, axis=1) for pair in zip(places, marks)]
 
 
-def pack_kernel(cells, charges, fill, marks, gains, strengths, green, own, copies, message, factors):
+def deposit(messages, lists, beam):
+    cells = lax.broadcasted_iota(jnp.int32, (GRID, GRID), 0).astype(f32)
+    row_hots, col_hots = [], []
+    for message in messages:
+        for part in range(lists // 8):
+            base = 8 * part + 4 * beam
+            charge = message[base : base + 1, :].astype(f32)
+            rows = message[base + 1 : base + 2, :].astype(f32)
+            cols = message[base + 2 : base + 3, :].astype(f32)
+            row_hots.append(jnp.where(cells == rows, 1.0, 0.0).astype(bf16))
+            col_hots.append(jnp.where(cells == cols, charge, 0.0).astype(bf16))
+    return dot_nt(jnp.concatenate(col_hots, axis=1), jnp.concatenate(row_hots, axis=1))
+
+
+def pack_kernel(cells, charges, fill, marks, gains, strengths, green, own, copies, message, factors, far, partial, sent):
     particles = charges.shape[1]
     count = copies.shape[0]
     here = lax.axis_index("bunch")
@@ -97,20 +111,43 @@
         for offset in range(REACH):
             up = marks[beam, 0, 0, offset - 1].astype(f32) if offset else 0.0
             down = marks[beam, 1, 0, offset + 1].astype(f32) if offset < STOPS - 1 else 0.0
-            target = own if offset == 0 else copies.at[lax.rem(here + sign * offset + count, count)]
+            target = own if offset == 0 else copies.at[count - 1 - lax.rem(here + sign * offset + count, count)]
             for row, value in enumerate(query_rows(rows, cols, up, down)):
                 target[4 * beam + row : 4 * beam + row + 1, :] = value.astype(bf16)
+
     message[lists:, :] = green[...].astype(bf16)
     for stop in range(STOPS):
         factors[stop : stop + 1, :] = jnp.full((1, 2 * LANES), gains[stop], f32)
         product = gains[stop] * strengths[stop]
         factors[STOPS + stop : STOPS + stop + 1, :] = jnp.full((1, 2 * LANES), product, f32)
 
+    @pl.when(is_early())
+    def start():
+        pltpu.make_async_copy(copies, far, sent).start()
+
+    @pl.when(is_early())
+    def work():
+        for beam in range(2):
+            partial[:, beam * GRID : (beam + 1) * GRID] = deposit([message], lists, beam)
+        pltpu.make_async_copy(copies, far, sent).wait()
+
+
+def is_early():
+    return lax.axis_index("tile") < lax.axis_size("tile") // 2
+
+
+def late_kernel(copies, far, out, sent):
+    @pl.when(jnp.logical_not(is_early()))
+    def write():
+        copy = pltpu.make_async_copy(copies, out, sent)
+        copy.start()
+        copy.wait()
+
 
 def field_kernel(tiles, *refs):
     here = lax.axis_index("tile")
     messages = refs[:tiles]
-    far, out, near, gathered, densities, arrived = refs[tiles:]
+    partial, far, out, near, gathered, densities, arrived = refs[tiles:]
     early = near.shape[0] - INVERSE_TABLES
     fetch = [
         pltpu.make_async_copy(far.at[:early], near.at[:early], arrived.at[0]),
@@ -120,24 +157,21 @@
         copy.start()
     lists = messages[0].shape[0] - GRID // tiles
     columns = GRID // tiles
-    for step in range(tiles):
+    for step, message in zip(steps_of(tiles), messages):
         start = pl.multiple_of(relative(here, step, tiles) * columns, columns)
-        gathered[pl.ds(start, columns), :] = messages[step][lists:, :]
-
-    @pl.when(here >= 0)
-    def deposit():
-        cells = lax.broadcasted_iota(jnp.int32, (GRID, GRID), 0).astype(f32)
+        gathered[pl.ds(start, columns), :] = message[lists:, :]
+
+    @pl.when(is_early())
+    def add_others():
         for beam in range(2):
-            row_hots, col_hots = [], []
-            for message in messages:
-                for part in range(lists // 8):
-                    base = 8 * part + 4 * beam
-                    charge = message[base : base + 1, :].astype(f32)
-                    rows = message[base + 1 : base + 2, :].astype(f32)
-                    cols = message[base + 2 : base + 3, :].astype(f32)
-                    row_hots.append(jnp.where(cells == rows, 1.0, 0.0).astype(bf16))
-                    col_hots.append(jnp.where(cells == cols, charge, 0.0).astype(bf16))
-            density = dot_nt(jnp.concatenate(col_hots, axis=1), jnp.concatenate(row_hots, axis=1))
+            lanes = slice(beam * GRID, (beam + 1) * GRID)
+            density = partial[:, lanes] + deposit(messages[1:], lists, beam)
+            densities[:, lanes] = wide(density, 0)
+
+    @pl.when(jnp.logical_not(is_early()))
+    def add_all():
+        for beam in range(2):
+            density = deposit(messages, lists, beam)
             densities[:, beam * GRID : (beam + 1) * GRID] = wide(density, 0)
 
     fetch[0].wait()
@@ -183,7 +217,7 @@
     for offset in range(REACH):
         for beam in range(2):
             sign = 1 if beam == 0 else -1
-            target = lax.rem(here - sign * offset + count, count)
+            target = count - 1 - lax.rem(here - sign * offset + count, count)
             source = queries.at[target] if offset else own
             base = 4 * beam
 
@@ -235,7 +269,7 @@
         sign = 1 if beam == 0 else -1
         total = home[2 * beam : 2 * beam + 2, :]
         for offset in range(1, REACH):
-            part = received[lax.rem(here + sign * offset + count, count)].astype(f32)
+            part = received[count - 1 - lax.rem(here + sign * offset + count, count)].astype(f32)
             if shared(offset, count):
                 total = total + part[2 * beam : 2 * beam + 2]
             else:
@@ -252,6 +286,10 @@
 
 def kept_far(value):
     return pltpu.with_memory_space_constraint(value, pltpu.HBM)
+
+
+def steps_of(tiles):
+    return [0, *[1, 3, 2]] if tiles == 4 else list(range(tiles))
 
 
 def is_power_of_two(count):
@@ -279,16 +317,19 @@
     count = lax.axis_size("bunch")
     tables = make_tables()
     columns = green_spectrum.shape[1]
-    own, copies, message, factors = pl.pallas_call(
+    own, staged, message, factors, copies, partial = pl.pallas_call(
         pack_kernel,
         out_shape=(
             jax.ShapeDtypeStruct((8, particles // 2 + LANES), bf16),
             jax.ShapeDtypeStruct((count, 8, particles // 2 + LANES), bf16),
             jax.ShapeDtypeStruct((8 * particles // GRID + columns, GRID), bf16),
             jax.ShapeDtypeStruct((2 * STOPS, 2 * LANES), f32),
+            jax.ShapeDtypeStruct((count, 8, particles // 2 + LANES), bf16),
+            jax.ShapeDtypeStruct((GRID, 2 * GRID), f32),
         ),
         in_specs=[VMEM, VMEM, SMEM, SMEM, SMEM, SMEM, VMEM],
-        out_specs=(VMEM, VMEM, VMEM, VMEM),
+        out_specs=(VMEM, VMEM, VMEM, VMEM, FAR, VMEM),
+        scratch_shapes=[pltpu.SemaphoreType.DMA],
         compiler_params=SMALL,
     )(
         kept_far(cell_index),
@@ -299,12 +340,21 @@
         kept_far(parasitic_gain),
         kept_far(green_spectrum.T),
     )
-    messages = [message] + [exchanged(message, "tile", step) for step in range(1, tiles)]
-    queries = lax.all_to_all(copies, "bunch", split_axis=0, concat_axis=0, tiled=True)
+    copies = pl.pallas_call(
+        late_kernel,
+        out_shape=jax.ShapeDtypeStruct(copies.shape, bf16),
+        in_specs=[VMEM, FAR],
+        out_specs=FAR,
+        scratch_shapes=[pltpu.SemaphoreType.DMA],
+        input_output_aliases={1: 0},
+        compiler_params=SMALL,
+    )(staged, copies)
+    messages = [message] + [exchanged(message, "tile", step) for step in steps_of(tiles)[1:]]
+    queries = lax.all_to_all(copies, "bunch", split_axis=0, concat_axis=0, tiled=True, axis_index_groups=[list(reversed(range(count)))])
     fields = pl.pallas_call(
         functools.partial(field_kernel, tiles),
         out_shape=jax.ShapeDtypeStruct((2, 2 * GRID, GRID), bf16),
-        in_specs=[VMEM] * tiles + [FAR],
+        in_specs=[VMEM] * (tiles + 1) + [FAR],
         out_specs=VMEM,
         scratch_shapes=[
             pltpu.VMEM(tables.shape, bf16),
@@ -314,7 +364,7 @@
         ],
         compiler_params=LIMIT,
         cost_estimate=pl.CostEstimate(flops=3000000000, bytes_accessed=1000000, transcendentals=0),
-    )(*messages, kept_far(jnp.asarray(tables)))
+    )(*messages, partial, kept_far(jnp.asarray(tables)))
     home, away = pl.pallas_call(
         functools.partial(kick_kernel, count),
         out_shape=(
@@ -325,7 +375,7 @@
         out_specs=(VMEM, VMEM),
         compiler_params=LIMIT,
     )(factors, fields, own, queries)
-    received = lax.all_to_all(away, "bunch", split_axis=0, concat_axis=0, tiled=True)
+    received = lax.all_to_all(away, "bunch", split_axis=0, concat_axis=0, tiled=True, axis_index_groups=[list(reversed(range(count)))])
     return pl.pallas_call(
         functools.partial(final_kernel, count),
         out_shape=jax.ShapeDtypeStruct(momenta.shape, f32),

time: 27.7 us -> 25.8 us (0.931)
  waiting for transfers between devices: 1.44 us -> 0.01 us
  blocking collectives: 7.61 us -> 6.5 us
  starting transfers between devices: 9.56 us -> 10.1 us
    all_to_all x1, blocking collectives: 7.61 us -> 6.5 us  [body(): lax.all_to_all(away, 'bunch', split_axis=0, concat_axis=0, tiled=True, ax...]
    all_to_all x1, waiting for transfers between devices: 0.97 us -> 0.01 us  [body(): lax.all_to_all(copies, 'bunch', split_axis=0, concat_axis=0, tiled=True,...]
    all_to_all x1, starting transfers between devices: 3.94 us -> 4.66 us  [body(): lax.all_to_all(copies, 'bunch', split_axis=0, concat_axis=0, tiled=True,...]
    ppermute x3, waiting for transfers between devices: 0.47 us -> 0.01 us  [exchanged(): return lax.ppermute(value, axis, pairs)]
  transfers between devices with their start and end apart: 4 -> 4, of which waited for: 2 -> 0; matrix products, arithmetic and copies ran while one was open for 0% -> 0% of each run, Pallas kernels for 13% -> 14%
where the time goes in v8:
time: 25.8 us; the launch traced here: 25.5 us
  starting transfers between devices  10.1 us (39%)
  Pallas kernels  8.77 us (34%)
  blocking collectives  6.5 us (25%)
    all_to_all x1, blocking collectives, body(): lax.all_to_all(away, 'bunch', split_axis=0, concat_axis=0, tiled=True, ax...  6.5 us
    ppermute x3, starting transfers between devices, exchanged(): return lax.ppermute(value, axis, pairs)  5.45 us
    all_to_all x1, starting transfers between devices, body(): lax.all_to_all(copies, 'bunch', split_axis=0, concat_axis=0, tiled=True,...  4.66 us
    pallas_call x1, Pallas kernels, body(): pl.pallas_call(functools.partial(field_kernel, tiles), out_shape=jax.Shap...  3.56 us
    pallas_call x1, Pallas kernels, body(): pl.pallas_call(functools.partial(kick_kernel, count), out_shape=(jax.Shap...  2.92 us
    pallas_call x1, Pallas kernels, body(): pl.pallas_call(pack_kernel, out_shape=(jax.ShapeDtypeStruct((8, particles...  1.64 us
    pallas_call x1, Pallas kernels, body(): pl.pallas_call(functools.partial(final_kernel, count), out_shape=jax.Shap...  0.64 us
  transfers between devices with their start and end apart: 4, of which 0 were waited for; matrix products, arithmetic and copies ran while one was open for 0% of the time, Pallas kernels for 14%

profile of v8, /device:TPU:0, one launch (start us, length us, event | category | flops | bytes accessed | tf_op | source)
XLA Modules:
  0.0 25.5 jit_solution(187898246319428180)
XLA Ops:
  0.0 1.6 %shard_map.91 = (bf16[8,640]{1,0:T(8,128)(2,1)S(1)}, bf16[8,8,640]{2,1,0:T(8,128)(2,1)S(1)}, bf16[96,256]{1,0:T(8,128)(2,1)S(1)}, f32[8,256]{1,0:T(8,128)S(1)}, ...) custom-call(s32[2,1,2,1024]{3,2,1,0:T(2,128)} %cells.1, bf16[2,1024]{1,0:T(2,128)(2,1)} %bitcast.5, s32[1,2]{1,0:T(1,128)} %bitcast.7, ...), custom_call_target="tpu_custom_call" | custom-call | tf_op jit(solution)/shard_map/pallas_call | solution.py:320
  1.6 3.5 %collective-permute-start.2 = (bf16[96,256]{1,0:T(8,128)(2,1)S(1)}, bf16[96,256]{1,0:T(8,128)(2,1)S(1)}, u32[]{:S(2)}, u32[]{:S(2)}) collective-permute-start(bf16[96,256]{1,0:T(8,128)(2,1)S(1)} %get-tuple-element.14.refs_0_), channel_id=1, source_target_pairs={{0,2},{1,3},{2,0},{3,1},{4,6},{5,7},{6,4},{7,5},{8,10},{9,11},{10,... | collective-permute-start | bytes 147464 | tf_op jit(solution)/shard_map/ppermute | solution.py:311
  5.1 2.0 %collective-permute-start.1 = (bf16[96,256]{1,0:T(8,128)(2,1)S(1)}, bf16[96,256]{1,0:T(8,128)(2,1)S(1)}, u32[]{:S(2)}, u32[]{:S(2)}) collective-permute-start(bf16[96,256]{1,0:T(8,128)(2,1)S(1)} %get-tuple-element.14.refs_0_), channel_id=1, source_target_pairs={{0,3},{1,2},{2,1},{3,0},{4,7},{5,6},{6,5},{7,4},{8,11},{9,10},{10,... | collective-permute-start | bytes 147464 | tf_op jit(solution)/shard_map/ppermute | solution.py:311
  7.1 0.0 collective-permute-start
  7.1 4.7 %all-to-all-start = ((bf16[8,8,640]{2,1,0:T(8,128)(2,1)}), bf16[8,8,640]{2,1,0:T(8,128)(2,1)S(1)}, u32[]{:S(2)}, u32[]{:S(2)}) async-start(bf16[8,8,640]{2,1,0:T(8,128)(2,1)} %shard_map.93), calls=%async_computation | async-start | bytes 163840 | tf_op jit(solution)/shard_map/all_to_all | solution.py:353
  11.8 0.0 collective-permute-done.2.refs_3_
  11.8 0.0 collective-permute-done.1.refs_2_
  11.8 0.0 collective-permute-done.refs_1_
  11.8 0.0 copy-start
  11.8 3.6 %shard_map.92.fields = bf16[2,512,256]{2,1,0:T(8,128)(2,1)S(1)} custom-call(bf16[96,256]{1,0:T(8,128)(2,1)S(1)} %get-tuple-element.14.refs_0_, bf16[96,256]{1,0:T(8,128)(2,1)S(1)} %collective-permute-done.refs_1_, bf16[96,256]{1,0:T(8,128)(2,1)S(1)} %collective-permute-done.1.refs_2_, bf16[96,256]{1,0:T(8,128)(2,1)S(1)} %collective-permute-done.2.refs_3_, ...), custom_call_target="tpu_custom_call" | custom-call | flops 3000000000 | bytes 1000000 | tf_op jit(solution)/shard_map/pallas_call | solution.py:354
  15.4 0.0 all-to-all-done.queries
  15.4 2.9 %shard_map.94 = (f32[4,1024]{1,0:T(4,128)S(1)}, bf16[8,4,1024]{2,1,0:T(4,128)(2,1)S(1)}) custom-call(f32[8,256]{1,0:T(8,128)S(1)} %get-tuple-element.13.factors, bf16[2,512,256]{2,1,0:T(8,128)(2,1)S(1)} %shard_map.92.fields, bf16[8,640]{1,0:T(8,128)(2,1)S(1)} %get-tuple-element.16.own, bf16[8,8,640]{2,1,0:T(8,128)(2,1)S(1)} %all-to-all-done.queries), custom_call_target="tpu_custom_call" | custom-call | tf_op jit(solution)/shard_map/pallas_call | solution.py:368
  18.3 6.5 %all_to_all.10.received = bf16[8,4,1024]{2,1,0:T(4,128)(2,1)S(1)} all-to-all(bf16[8,4,1024]{2,1,0:T(4,128)(2,1)S(1)} %get-tuple-element.19), channel_id=1, replica_groups={{28,24,20,16,12,8,4,0},{29,25,21,17,13,9,5,1},{30,26,22,18,14,10,6,2},{..., dimensions={0} | all-to-all | bytes 131072 | tf_op jit(solution)/shard_map/all_to_all | solution.py:378
  24.8 0.0 copy-done
  24.8 0.6 %shard_map.95 = f32[2,1,2,1024]{3,2,1,0:T(2,128)} custom-call(bf16[8,4,1024]{2,1,0:T(4,128)(2,1)S(1)} %all_to_all.10.received, f32[4,1024]{1,0:T(4,128)S(1)} %get-tuple-element.20.home, f32[2,1,2,1024]{3,2,1,0:T(2,128)S(1)} %copy-done), custom_call_target="tpu_custom_call" | custom-call | tf_op jit(solution)/shard_map/pallas_call | solution.py:379
  (1 shorter events, 0.0 us)
Async XLA Ops:
  1.6 10.1 %collective-permute-start.2 = (bf16[96,256]{1,0:T(8,128)(2,1)S(1)}, bf16[96,256]{1,0:T(8,128)(2,1)S(1)}, u32[]{:S(2)}, u32[]{:S(2)}) collective-permute-start(bf16[96,256]{1,0:T(8,128)(2,1)S(1)} %get-tuple-element.14.refs_0_), channel_id=1, source_target_pairs={{0,2},{1,3},{2,0},{3,1},{4,6},{5,7},{6,4},{7,5},{8,10},{9,11},{10,... | collective-permute-start | bytes 147464 | tf_op jit(solution)/shard_map/ppermute | solution.py:311
  5.1 6.7 %collective-permute-start.1 = (bf16[96,256]{1,0:T(8,128)(2,1)S(1)}, bf16[96,256]{1,0:T(8,128)(2,1)S(1)}, u32[]{:S(2)}, u32[]{:S(2)}) collective-permute-start(bf16[96,256]{1,0:T(8,128)(2,1)S(1)} %get-tuple-element.14.refs_0_), channel_id=1, source_target_pairs={{0,3},{1,2},{2,1},{3,0},{4,7},{5,6},{6,5},{7,4},{8,11},{9,10},{10,... | collective-permute-start | bytes 147464 | tf_op jit(solution)/shard_map/ppermute | solution.py:311
  7.1 4.7 %collective-permute-start = (bf16[96,256]{1,0:T(8,128)(2,1)S(1)}, bf16[96,256]{1,0:T(8,128)(2,1)S(1)}, u32[]{:S(2)}, u32[]{:S(2)}) collective-permute-start(bf16[96,256]{1,0:T(8,128)(2,1)S(1)} %get-tuple-element.14.refs_0_), channel_id=1, source_target_pairs={{0,1},{1,0},{2,3},{3,2},{4,5},{5,4},{6,7},{7,6},{8,9},{9,8},{10,11... | collective-permute-start | bytes 147464 | tf_op jit(solution)/shard_map/ppermute | solution.py:311
  7.1 8.3 %all-to-all-start = ((bf16[8,8,640]{2,1,0:T(8,128)(2,1)}), bf16[8,8,640]{2,1,0:T(8,128)(2,1)S(1)}, u32[]{:S(2)}, u32[]{:S(2)}) async-start(bf16[8,8,640]{2,1,0:T(8,128)(2,1)} %shard_map.93), calls=%async_computation | async-start | bytes 163840 | tf_op jit(solution)/shard_map/all_to_all | solution.py:353
  11.8 13.0 %copy-start = (f32[2,1,2,1024]{3,2,1,0:T(2,128)S(1)}, f32[2,1,2,1024]{3,2,1,0:T(2,128)}, u32[]{:S(2)}) copy-start(f32[2,1,2,1024]{3,2,1,0:T(2,128)} %momenta.1) | copy-start | bytes 49156

commit v9 on v8

--- a/solution.py
+++ b/solution.py
@@ -79,12 +79,12 @@
     return [jnp.concatenate(pair, axis=1) for pair in zip(places, marks)]
 
 
-def deposit(messages, lists, beam):
+def deposit(messages, columns, beam):
     cells = lax.broadcasted_iota(jnp.int32, (GRID, GRID), 0).astype(f32)
     row_hots, col_hots = [], []
     for message in messages:
-        for part in range(lists // 8):
-            base = 8 * part + 4 * beam
+        for part in range((message.shape[0] - columns) // 6):
+            base = columns + 6 * part + 3 * beam
             charge = message[base : base + 1, :].astype(f32)
             rows = message[base + 1 : base + 2, :].astype(f32)
             cols = message[base + 2 : base + 3, :].astype(f32)
@@ -97,7 +97,8 @@
     particles = charges.shape[1]
     count = copies.shape[0]
     here = lax.axis_index("bunch")
-    lists = 8 * particles // GRID
+    columns = green.shape[0]
+    message[:columns, :] = green[...].astype(bf16)
     for beam in range(2):
         sign = 1 if beam == 0 else -1
         charge = charges[beam : beam + 1, :].astype(f32) * fill[0, beam].astype(f32)
@@ -106,7 +107,7 @@
         for part in range(particles // GRID):
             lanes = slice(part * GRID, (part + 1) * GRID)
             for row, value in enumerate((charge, rows, cols)):
-                at = 8 * part + 4 * beam + row
+                at = columns + 6 * part + 3 * beam + row
                 message[at : at + 1, :] = value[:, lanes].astype(bf16)
         for offset in range(REACH):
             up = marks[beam, 0, 0, offset - 1].astype(f32) if offset else 0.0
@@ -115,7 +116,6 @@
             for row, value in enumerate(query_rows(rows, cols, up, down)):
                 target[4 * beam + row : 4 * beam + row + 1, :] = value.astype(bf16)
 
-    message[lists:, :] = green[...].astype(bf16)
     for stop in range(STOPS):
         factors[stop : stop + 1, :] = jnp.full((1, 2 * LANES), gains[stop], f32)
         product = gains[stop] * strengths[stop]
@@ -128,7 +128,7 @@
     @pl.when(is_early())
     def work():
         for beam in range(2):
-            partial[:, beam * GRID : (beam + 1) * GRID] = deposit([message], lists, beam)
+            partial[:, beam * GRID : (beam + 1) * GRID] = deposit([message], columns, beam)
         pltpu.make_async_copy(copies, far, sent).wait()
 
 
@@ -155,23 +155,22 @@
     ]
     for copy in fetch:
         copy.start()
-    lists = messages[0].shape[0] - GRID // tiles
     columns = GRID // tiles
     for step, message in zip(steps_of(tiles), messages):
         start = pl.multiple_of(relative(here, step, tiles) * columns, columns)
-        gathered[pl.ds(start, columns), :] = message[lists:, :]
+        gathered[pl.ds(start, columns), :] = message[:columns, :]
 
     @pl.when(is_early())
     def add_others():
         for beam in range(2):
             lanes = slice(beam * GRID, (beam + 1) * GRID)
-            density = partial[:, lanes] + deposit(messages[1:], lists, beam)
+            density = partial[:, lanes] + deposit(messages[1:], columns, beam)
             densities[:, lanes] = wide(density, 0)
 
     @pl.when(jnp.logical_not(is_early()))
     def add_all():
         for beam in range(2):
-            density = deposit(messages, lists, beam)
+            density = deposit(messages, columns, beam)
             densities[:, beam * GRID : (beam + 1) * GRID] = wide(density, 0)
 
     fetch[0].wait()
@@ -322,7 +321,7 @@
         out_shape=(
             jax.ShapeDtypeStruct((8, particles // 2 + LANES), bf16),
             jax.ShapeDtypeStruct((count, 8, particles // 2 + LANES), bf16),
-            jax.ShapeDtypeStruct((8 * particles // GRID + columns, GRID), bf16),
+            jax.ShapeDtypeStruct((columns + 6 * particles // GRID, GRID), bf16),
             jax.ShapeDtypeStruct((2 * STOPS, 2 * LANES), f32),
             jax.ShapeDtypeStruct((count, 8, particles // 2 + LANES), bf16),
             jax.ShapeDtypeStruct((GRID, 2 * GRID), f32),

time: 25.8 us -> 25.6 us (level)
  no operation moved by 1% of the time
where the time goes in v9:
time: 25.6 us; the launch traced here: 25.3 us
  starting transfers between devices  10.1 us (39%)
  Pallas kernels  8.77 us (34%)
  blocking collectives  6.32 us (25%)
    all_to_all x1, blocking collectives, body(): lax.all_to_all(away, 'bunch', split_axis=0, concat_axis=0, tiled=True, ax...  6.32 us
    ppermute x3, starting transfers between devices, exchanged(): return lax.ppermute(value, axis, pairs)  5.45 us
    all_to_all x1, starting transfers between devices, body(): lax.all_to_all(copies, 'bunch', split_axis=0, concat_axis=0, tiled=True,...  4.66 us
    pallas_call x1, Pallas kernels, body(): pl.pallas_call(functools.partial(field_kernel, tiles), out_shape=jax.Shap...  3.57 us
    pallas_call x1, Pallas kernels, body(): pl.pallas_call(functools.partial(kick_kernel, count), out_shape=(jax.Shap...  2.92 us
    pallas_call x1, Pallas kernels, body(): pl.pallas_call(pack_kernel, out_shape=(jax.ShapeDtypeStruct((8, particles...  1.64 us
    pallas_call x1, Pallas kernels, body(): pl.pallas_call(functools.partial(final_kernel, count), out_shape=jax.Shap...  0.64 us
  transfers between devices with their start and end apart: 4, of which 0 were waited for; matrix products, arithmetic and copies ran while one was open for 0% of the time, Pallas kernels for 14%

profile of v9, /device:TPU:0, one launch (start us, length us, event | category | flops | bytes accessed | tf_op | source)
XLA Modules:
  0.0 25.3 jit_solution(10631237458416971786)
XLA Ops:
  0.0 1.6 %shard_map.91 = (bf16[8,640]{1,0:T(8,128)(2,1)S(1)}, bf16[8,8,640]{2,1,0:T(8,128)(2,1)S(1)}, bf16[88,256]{1,0:T(8,128)(2,1)S(1)}, f32[8,256]{1,0:T(8,128)S(1)}, ...) custom-call(s32[2,1,2,1024]{3,2,1,0:T(2,128)} %cells.1, bf16[2,1024]{1,0:T(2,128)(2,1)} %bitcast.5, s32[1,2]{1,0:T(1,128)} %bitcast.7, ...), custom_call_target="tpu_custom_call" | custom-call | tf_op jit(solution)/shard_map/pallas_call | solution.py:319
  1.6 3.5 %collective-permute-start.2 = (bf16[88,256]{1,0:T(8,128)(2,1)S(1)}, bf16[88,256]{1,0:T(8,128)(2,1)S(1)}, u32[]{:S(2)}, u32[]{:S(2)}) collective-permute-start(bf16[88,256]{1,0:T(8,128)(2,1)S(1)} %get-tuple-element.14.refs_0_), channel_id=1, source_target_pairs={{0,2},{1,3},{2,0},{3,1},{4,6},{5,7},{6,4},{7,5},{8,10},{9,11},{10,... | collective-permute-start | bytes 135176 | tf_op jit(solution)/shard_map/ppermute | solution.py:310
  5.1 2.0 %collective-permute-start.1 = (bf16[88,256]{1,0:T(8,128)(2,1)S(1)}, bf16[88,256]{1,0:T(8,128)(2,1)S(1)}, u32[]{:S(2)}, u32[]{:S(2)}) collective-permute-start(bf16[88,256]{1,0:T(8,128)(2,1)S(1)} %get-tuple-element.14.refs_0_), channel_id=1, source_target_pairs={{0,3},{1,2},{2,1},{3,0},{4,7},{5,6},{6,5},{7,4},{8,11},{9,10},{10,... | collective-permute-start | bytes 135176 | tf_op jit(solution)/shard_map/ppermute | solution.py:310
  7.1 0.0 collective-permute-start
  7.1 4.7 %all-to-all-start = ((bf16[8,8,640]{2,1,0:T(8,128)(2,1)}), bf16[8,8,640]{2,1,0:T(8,128)(2,1)S(1)}, u32[]{:S(2)}, u32[]{:S(2)}) async-start(bf16[8,8,640]{2,1,0:T(8,128)(2,1)} %shard_map.93), calls=%async_computation | async-start | bytes 163840 | tf_op jit(solution)/shard_map/all_to_all | solution.py:352
  11.8 0.0 collective-permute-done.2.refs_3_
  11.8 0.0 collective-permute-done.1.refs_2_
  11.8 0.0 collective-permute-done.refs_1_
  11.8 0.0 copy-start
  11.8 3.6 %shard_map.92.fields = bf16[2,512,256]{2,1,0:T(8,128)(2,1)S(1)} custom-call(bf16[88,256]{1,0:T(8,128)(2,1)S(1)} %get-tuple-element.14.refs_0_, bf16[88,256]{1,0:T(8,128)(2,1)S(1)} %collective-permute-done.refs_1_, bf16[88,256]{1,0:T(8,128)(2,1)S(1)} %collective-permute-done.1.refs_2_, bf16[88,256]{1,0:T(8,128)(2,1)S(1)} %collective-permute-done.2.refs_3_, ...), custom_call_target="tpu_custom_call" | custom-call | flops 3000000000 | bytes 1000000 | tf_op jit(solution)/shard_map/pallas_call | solution.py:353
  15.4 0.0 all-to-all-done.queries
  15.4 2.9 %shard_map.94 = (f32[4,1024]{1,0:T(4,128)S(1)}, bf16[8,4,1024]{2,1,0:T(4,128)(2,1)S(1)}) custom-call(f32[8,256]{1,0:T(8,128)S(1)} %get-tuple-element.13.factors, bf16[2,512,256]{2,1,0:T(8,128)(2,1)S(1)} %shard_map.92.fields, bf16[8,640]{1,0:T(8,128)(2,1)S(1)} %get-tuple-element.16.own, bf16[8,8,640]{2,1,0:T(8,128)(2,1)S(1)} %all-to-all-done.queries), custom_call_target="tpu_custom_call" | custom-call | tf_op jit(solution)/shard_map/pallas_call | solution.py:367
  18.3 6.3 %all_to_all.10.received = bf16[8,4,1024]{2,1,0:T(4,128)(2,1)S(1)} all-to-all(bf16[8,4,1024]{2,1,0:T(4,128)(2,1)S(1)} %get-tuple-element.19), channel_id=1, replica_groups={{28,24,20,16,12,8,4,0},{29,25,21,17,13,9,5,1},{30,26,22,18,14,10,6,2},{..., dimensions={0} | all-to-all | bytes 131072 | tf_op jit(solution)/shard_map/all_to_all | solution.py:377
  24.6 0.0 copy-done
  24.6 0.6 %shard_map.95 = f32[2,1,2,1024]{3,2,1,0:T(2,128)} custom-call(bf16[8,4,1024]{2,1,0:T(4,128)(2,1)S(1)} %all_to_all.10.received, f32[4,1024]{1,0:T(4,128)S(1)} %get-tuple-element.20.home, f32[2,1,2,1024]{3,2,1,0:T(2,128)S(1)} %copy-done), custom_call_target="tpu_custom_call" | custom-call | tf_op jit(solution)/shard_map/pallas_call | solution.py:378
  (1 shorter events, 0.0 us)
Async XLA Ops:
  1.6 10.1 %collective-permute-start.2 = (bf16[88,256]{1,0:T(8,128)(2,1)S(1)}, bf16[88,256]{1,0:T(8,128)(2,1)S(1)}, u32[]{:S(2)}, u32[]{:S(2)}) collective-permute-start(bf16[88,256]{1,0:T(8,128)(2,1)S(1)} %get-tuple-element.14.refs_0_), channel_id=1, source_target_pairs={{0,2},{1,3},{2,0},{3,1},{4,6},{5,7},{6,4},{7,5},{8,10},{9,11},{10,... | collective-permute-start | bytes 135176 | tf_op jit(solution)/shard_map/ppermute | solution.py:310
  5.1 6.7 %collective-permute-start.1 = (bf16[88,256]{1,0:T(8,128)(2,1)S(1)}, bf16[88,256]{1,0:T(8,128)(2,1)S(1)}, u32[]{:S(2)}, u32[]{:S(2)}) collective-permute-start(bf16[88,256]{1,0:T(8,128)(2,1)S(1)} %get-tuple-element.14.refs_0_), channel_id=1, source_target_pairs={{0,3},{1,2},{2,1},{3,0},{4,7},{5,6},{6,5},{7,4},{8,11},{9,10},{10,... | collective-permute-start | bytes 135176 | tf_op jit(solution)/shard_map/ppermute | solution.py:310
  7.1 4.7 %collective-permute-start = (bf16[88,256]{1,0:T(8,128)(2,1)S(1)}, bf16[88,256]{1,0:T(8,128)(2,1)S(1)}, u32[]{:S(2)}, u32[]{:S(2)}) collective-permute-start(bf16[88,256]{1,0:T(8,128)(2,1)S(1)} %get-tuple-element.14.refs_0_), channel_id=1, source_target_pairs={{0,1},{1,0},{2,3},{3,2},{4,5},{5,4},{6,7},{7,6},{8,9},{9,8},{10,11... | collective-permute-start | bytes 135176 | tf_op jit(solution)/shard_map/ppermute | solution.py:310
  7.1 8.3 %all-to-all-start = ((bf16[8,8,640]{2,1,0:T(8,128)(2,1)}), bf16[8,8,640]{2,1,0:T(8,128)(2,1)S(1)}, u32[]{:S(2)}, u32[]{:S(2)}) async-start(bf16[8,8,640]{2,1,0:T(8,128)(2,1)} %shard_map.93), calls=%async_computation | async-start | bytes 163840 | tf_op jit(solution)/shard_map/all_to_all | solution.py:352
  11.8 12.8 %copy-start = (f32[2,1,2,1024]{3,2,1,0:T(2,128)S(1)}, f32[2,1,2,1024]{3,2,1,0:T(2,128)}, u32[]{:S(2)}) copy-start(f32[2,1,2,1024]{3,2,1,0:T(2,128)} %momenta.1) | copy-start | bytes 49156

commit v10 on v9

--- a/solution.py
+++ b/solution.py
@@ -133,7 +133,7 @@
 
 
 def is_early():
-    return lax.axis_index("tile") < lax.axis_size("tile") // 2
+    return lax.axis_index("tile") < 1
 
 
 def late_kernel(copies, far, out, sent):

time: 25.6 us -> 25.2 us (0.984)
  starting transfers between devices: 10.1 us -> 9.71 us
    ppermute x3, starting transfers between devices: 5.45 us -> 5.05 us  [exchanged(): return lax.ppermute(value, axis, pairs)]
where the time goes in v10:
time: 25.2 us; the launch traced here: 24.9 us
  starting transfers between devices  9.71 us (39%)
  Pallas kernels  8.77 us (35%)
  blocking collectives  6.32 us (25%)
    all_to_all x1, blocking collectives, body(): lax.all_to_all(away, 'bunch', split_axis=0, concat_axis=0, tiled=True, ax...  6.32 us
    ppermute x3, starting transfers between devices, exchanged(): return lax.ppermute(value, axis, pairs)  5.05 us
    all_to_all x1, starting transfers between devices, body(): lax.all_to_all(copies, 'bunch', split_axis=0, concat_axis=0, tiled=True,...  4.66 us
    pallas_call x1, Pallas kernels, body(): pl.pallas_call(functools.partial(field_kernel, tiles), out_shape=jax.Shap...  3.56 us
    pallas_call x1, Pallas kernels, body(): pl.pallas_call(functools.partial(kick_kernel, count), out_shape=(jax.Shap...  2.92 us
    pallas_call x1, Pallas kernels, body(): pl.pallas_call(pack_kernel, out_shape=(jax.ShapeDtypeStruct((8, particles...  1.64 us
    pallas_call x1, Pallas kernels, body(): pl.pallas_call(functools.partial(final_kernel, count), out_shape=jax.Shap...  0.64 us
  transfers between devices with their start and end apart: 4, of which 0 were waited for; matrix products, arithmetic and copies ran while one was open for 0% of the time, Pallas kernels for 14%

profile of v10, /device:TPU:0, one launch (start us, length us, event | category | flops | bytes accessed | tf_op | source)
XLA Modules:
  0.0 24.9 jit_solution(8391161177926747288)
XLA Ops:
  0.0 1.6 %shard_map.91 = (bf16[8,640]{1,0:T(8,128)(2,1)S(1)}, bf16[8,8,640]{2,1,0:T(8,128)(2,1)S(1)}, bf16[88,256]{1,0:T(8,128)(2,1)S(1)}, f32[8,256]{1,0:T(8,128)S(1)}, ...) custom-call(s32[2,1,2,1024]{3,2,1,0:T(2,128)} %cells.1, bf16[2,1024]{1,0:T(2,128)(2,1)} %bitcast.5, s32[1,2]{1,0:T(1,128)} %bitcast.7, ...), custom_call_target="tpu_custom_call" | custom-call | tf_op jit(solution)/shard_map/pallas_call | solution.py:319
  1.6 3.5 %collective-permute-start.2 = (bf16[88,256]{1,0:T(8,128)(2,1)S(1)}, bf16[88,256]{1,0:T(8,128)(2,1)S(1)}, u32[]{:S(2)}, u32[]{:S(2)}) collective-permute-start(bf16[88,256]{1,0:T(8,128)(2,1)S(1)} %get-tuple-element.14.refs_0_), channel_id=1, source_target_pairs={{0,2},{1,3},{2,0},{3,1},{4,6},{5,7},{6,4},{7,5},{8,10},{9,11},{10,... | collective-permute-start | bytes 135176 | tf_op jit(solution)/shard_map/ppermute | solution.py:310
  5.1 1.3 %collective-permute-start.1 = (bf16[88,256]{1,0:T(8,128)(2,1)S(1)}, bf16[88,256]{1,0:T(8,128)(2,1)S(1)}, u32[]{:S(2)}, u32[]{:S(2)}) collective-permute-start(bf16[88,256]{1,0:T(8,128)(2,1)S(1)} %get-tuple-element.14.refs_0_), channel_id=1, source_target_pairs={{0,3},{1,2},{2,1},{3,0},{4,7},{5,6},{6,5},{7,4},{8,11},{9,10},{10,... | collective-permute-start | bytes 135176 | tf_op jit(solution)/shard_map/ppermute | solution.py:310
  6.5 0.2 collective-permute-start
  6.7 4.7 %all-to-all-start = ((bf16[8,8,640]{2,1,0:T(8,128)(2,1)}), bf16[8,8,640]{2,1,0:T(8,128)(2,1)S(1)}, u32[]{:S(2)}, u32[]{:S(2)}) async-start(bf16[8,8,640]{2,1,0:T(8,128)(2,1)} %shard_map.93), calls=%async_computation | async-start | bytes 163840 | tf_op jit(solution)/shard_map/all_to_all | solution.py:352
  11.4 0.0 collective-permute-done.2.refs_3_
  11.4 0.0 collective-permute-done.1.refs_2_
  11.4 0.0 collective-permute-done.refs_1_
  11.4 0.0 copy-start
  11.4 3.6 %shard_map.92.fields = bf16[2,512,256]{2,1,0:T(8,128)(2,1)S(1)} custom-call(bf16[88,256]{1,0:T(8,128)(2,1)S(1)} %get-tuple-element.14.refs_0_, bf16[88,256]{1,0:T(8,128)(2,1)S(1)} %collective-permute-done.refs_1_, bf16[88,256]{1,0:T(8,128)(2,1)S(1)} %collective-permute-done.1.refs_2_, bf16[88,256]{1,0:T(8,128)(2,1)S(1)} %collective-permute-done.2.refs_3_, ...), custom_call_target="tpu_custom_call" | custom-call | flops 3000000000 | bytes 1000000 | tf_op jit(solution)/shard_map/pallas_call | solution.py:353
  15.0 0.0 all-to-all-done.queries
  15.0 2.9 %shard_map.94 = (f32[4,1024]{1,0:T(4,128)S(1)}, bf16[8,4,1024]{2,1,0:T(4,128)(2,1)S(1)}) custom-call(f32[8,256]{1,0:T(8,128)S(1)} %get-tuple-element.13.factors, bf16[2,512,256]{2,1,0:T(8,128)(2,1)S(1)} %shard_map.92.fields, bf16[8,640]{1,0:T(8,128)(2,1)S(1)} %get-tuple-element.16.own, bf16[8,8,640]{2,1,0:T(8,128)(2,1)S(1)} %all-to-all-done.queries), custom_call_target="tpu_custom_call" | custom-call | tf_op jit(solution)/shard_map/pallas_call | solution.py:367
  17.9 6.3 %all_to_all.10.received = bf16[8,4,1024]{2,1,0:T(4,128)(2,1)S(1)} all-to-all(bf16[8,4,1024]{2,1,0:T(4,128)(2,1)S(1)} %get-tuple-element.19), channel_id=1, replica_groups={{28,24,20,16,12,8,4,0},{29,25,21,17,13,9,5,1},{30,26,22,18,14,10,6,2},{..., dimensions={0} | all-to-all | bytes 131072 | tf_op jit(solution)/shard_map/all_to_all | solution.py:377
  24.2 0.0 copy-done
  24.2 0.6 %shard_map.95 = f32[2,1,2,1024]{3,2,1,0:T(2,128)} custom-call(bf16[8,4,1024]{2,1,0:T(4,128)(2,1)S(1)} %all_to_all.10.received, f32[4,1024]{1,0:T(4,128)S(1)} %get-tuple-element.20.home, f32[2,1,2,1024]{3,2,1,0:T(2,128)S(1)} %copy-done), custom_call_target="tpu_custom_call" | custom-call | tf_op jit(solution)/shard_map/pallas_call | solution.py:378
  (1 shorter events, 0.0 us)
Async XLA Ops:
  1.6 9.7 %collective-permute-start.2 = (bf16[88,256]{1,0:T(8,128)(2,1)S(1)}, bf16[88,256]{1,0:T(8,128)(2,1)S(1)}, u32[]{:S(2)}, u32[]{:S(2)}) collective-permute-start(bf16[88,256]{1,0:T(8,128)(2,1)S(1)} %get-tuple-element.14.refs_0_), channel_id=1, source_target_pairs={{0,2},{1,3},{2,0},{3,1},{4,6},{5,7},{6,4},{7,5},{8,10},{9,11},{10,... | collective-permute-start | bytes 135176 | tf_op jit(solution)/shard_map/ppermute | solution.py:310
  5.1 6.3 %collective-permute-start.1 = (bf16[88,256]{1,0:T(8,128)(2,1)S(1)}, bf16[88,256]{1,0:T(8,128)(2,1)S(1)}, u32[]{:S(2)}, u32[]{:S(2)}) collective-permute-start(bf16[88,256]{1,0:T(8,128)(2,1)S(1)} %get-tuple-element.14.refs_0_), channel_id=1, source_target_pairs={{0,3},{1,2},{2,1},{3,0},{4,7},{5,6},{6,5},{7,4},{8,11},{9,10},{10,... | collective-permute-start | bytes 135176 | tf_op jit(solution)/shard_map/ppermute | solution.py:310
  6.5 4.9 %collective-permute-start = (bf16[88,256]{1,0:T(8,128)(2,1)S(1)}, bf16[88,256]{1,0:T(8,128)(2,1)S(1)}, u32[]{:S(2)}, u32[]{:S(2)}) collective-permute-start(bf16[88,256]{1,0:T(8,128)(2,1)S(1)} %get-tuple-element.14.refs_0_), channel_id=1, source_target_pairs={{0,1},{1,0},{2,3},{3,2},{4,5},{5,4},{6,7},{7,6},{8,9},{9,8},{10,11... | collective-permute-start | bytes 135176 | tf_op jit(solution)/shard_map/ppermute | solution.py:310
  6.7 8.3 %all-to-all-start = ((bf16[8,8,640]{2,1,0:T(8,128)(2,1)}), bf16[8,8,640]{2,1,0:T(8,128)(2,1)S(1)}, u32[]{:S(2)}, u32[]{:S(2)}) async-start(bf16[8,8,640]{2,1,0:T(8,128)(2,1)} %shard_map.93), calls=%async_computation | async-start | bytes 163840 | tf_op jit(solution)/shard_map/all_to_all | solution.py:352
  11.4 12.8 %copy-start = (f32[2,1,2,1024]{3,2,1,0:T(2,128)S(1)}, f32[2,1,2,1024]{3,2,1,0:T(2,128)}, u32[]{:S(2)}) copy-start(f32[2,1,2,1024]{3,2,1,0:T(2,128)} %momenta.1) | copy-start | bytes 49156

commit v11 on v10

--- a/solution.py
+++ b/solution.py
@@ -216,8 +216,9 @@
     for offset in range(REACH):
         for beam in range(2):
             sign = 1 if beam == 0 else -1
-            target = count - 1 - lax.rem(here - sign * offset + count, count)
-            source = queries.at[target] if offset else own
+            partner = lax.rem(here - sign * offset + count, count)
+            target = back_slot(partner, count)
+            source = queries.at[count - 1 - partner] if offset else own
             base = 4 * beam
 
             def weight_of(stop, row):
@@ -268,7 +269,7 @@
         sign = 1 if beam == 0 else -1
         total = home[2 * beam : 2 * beam + 2, :]
         for offset in range(1, REACH):
-            part = received[count - 1 - lax.rem(here + sign * offset + count, count)].astype(f32)
+            part = received[back_slot(lax.rem(here + sign * offset + count, count), count)].astype(f32)
             if shared(offset, count):
                 total = total + part[2 * beam : 2 * beam + 2]
             else:
@@ -289,6 +290,10 @@
 
 def steps_of(tiles):
     return [0, *[1, 3, 2]] if tiles == 4 else list(range(tiles))
+
+
+def back_slot(device, count):
+    return jnp.where(lax.rem(device, 2) == 1, (count - 1 - device) // 2, count // 2 + (count - 2 - device) // 2)
 
 
 def is_power_of_two(count):
@@ -374,7 +379,10 @@
         out_specs=(VMEM, VMEM),
         compiler_params=LIMIT,
     )(factors, fields, own, queries)
-    received = lax.all_to_all(away, "bunch", split_axis=0, concat_axis=0, tiled=True, axis_index_groups=[list(reversed(range(count)))])
+    order = [*reversed(range(1, count, 2)), *reversed(range(0, count, 2))]
+    received = lax.all_to_all(
+        away, "bunch", split_axis=0, concat_axis=0, tiled=True, axis_index_groups=[order]
+    )
     return pl.pallas_call(
         functools.partial(final_kernel, count),
         out_shape=jax.ShapeDtypeStruct(momenta.shape, f32),

time: 25.2 us -> 25.3 us (level)
  no operation moved by 1% of the time
where the time goes in v11:
time: 25.3 us; the launch traced here: 25 us
  starting transfers between devices  9.71 us (38%)
  Pallas kernels  8.82 us (35%)
  blocking collectives  6.41 us (25%)
    all_to_all x1, blocking collectives, body(): lax.all_to_all(away, 'bunch', split_axis=0, concat_axis=0, tiled=True, ax...  6.41 us
    ppermute x3, starting transfers between devices, exchanged(): return lax.ppermute(value, axis, pairs)  5.05 us
    all_to_all x1, starting transfers between devices, body(): lax.all_to_all(copies, 'bunch', split_axis=0, concat_axis=0, tiled=True,...  4.66 us
    pallas_call x1, Pallas kernels, body(): pl.pallas_call(functools.partial(field_kernel, tiles), out_shape=jax.Shap...  3.56 us
    pallas_call x1, Pallas kernels, body(): pl.pallas_call(functools.partial(kick_kernel, count), out_shape=(jax.Shap...  2.92 us
    pallas_call x1, Pallas kernels, body(): pl.pallas_call(pack_kernel, out_shape=(jax.ShapeDtypeStruct((8, particles...  1.64 us
    pallas_call x1, Pallas kernels, body(): pl.pallas_call(functools.partial(final_kernel, count), out_shape=jax.Shap...  0.69 us
  transfers between devices with their start and end apart: 4, of which 0 were waited for; matrix products, arithmetic and copies ran while one was open for 0% of the time, Pallas kernels for 14%

profile of v11, /device:TPU:0, one launch (start us, length us, event | category | flops | bytes accessed | tf_op | source)
XLA Modules:
  0.0 25.0 jit_solution(7783692398226232841)
XLA Ops:
  0.0 1.6 %shard_map.91 = (bf16[8,640]{1,0:T(8,128)(2,1)S(1)}, bf16[8,8,640]{2,1,0:T(8,128)(2,1)S(1)}, bf16[88,256]{1,0:T(8,128)(2,1)S(1)}, f32[8,256]{1,0:T(8,128)S(1)}, ...) custom-call(s32[2,1,2,1024]{3,2,1,0:T(2,128)} %cells.1, bf16[2,1024]{1,0:T(2,128)(2,1)} %bitcast.5, s32[1,2]{1,0:T(1,128)} %bitcast.7, ...), custom_call_target="tpu_custom_call" | custom-call | tf_op jit(solution)/shard_map/pallas_call | solution.py:324
  1.6 3.5 %collective-permute-start.2 = (bf16[88,256]{1,0:T(8,128)(2,1)S(1)}, bf16[88,256]{1,0:T(8,128)(2,1)S(1)}, u32[]{:S(2)}, u32[]{:S(2)}) collective-permute-start(bf16[88,256]{1,0:T(8,128)(2,1)S(1)} %get-tuple-element.14.refs_0_), channel_id=1, source_target_pairs={{0,2},{1,3},{2,0},{3,1},{4,6},{5,7},{6,4},{7,5},{8,10},{9,11},{10,... | collective-permute-start | bytes 135176 | tf_op jit(solution)/shard_map/ppermute | solution.py:315
  5.1 1.3 %collective-permute-start.1 = (bf16[88,256]{1,0:T(8,128)(2,1)S(1)}, bf16[88,256]{1,0:T(8,128)(2,1)S(1)}, u32[]{:S(2)}, u32[]{:S(2)}) collective-permute-start(bf16[88,256]{1,0:T(8,128)(2,1)S(1)} %get-tuple-element.14.refs_0_), channel_id=1, source_target_pairs={{0,3},{1,2},{2,1},{3,0},{4,7},{5,6},{6,5},{7,4},{8,11},{9,10},{10,... | collective-permute-start | bytes 135176 | tf_op jit(solution)/shard_map/ppermute | solution.py:315
  6.5 0.2 collective-permute-start
  6.7 4.7 %all-to-all-start = ((bf16[8,8,640]{2,1,0:T(8,128)(2,1)}), bf16[8,8,640]{2,1,0:T(8,128)(2,1)S(1)}, u32[]{:S(2)}, u32[]{:S(2)}) async-start(bf16[8,8,640]{2,1,0:T(8,128)(2,1)} %shard_map.93), calls=%async_computation | async-start | bytes 163840 | tf_op jit(solution)/shard_map/all_to_all | solution.py:357
  11.4 0.0 collective-permute-done.2.refs_3_
  11.4 0.0 collective-permute-done.1.refs_2_
  11.4 0.0 collective-permute-done.refs_1_
  11.4 0.0 copy-start
  11.4 3.6 %shard_map.92.fields = bf16[2,512,256]{2,1,0:T(8,128)(2,1)S(1)} custom-call(bf16[88,256]{1,0:T(8,128)(2,1)S(1)} %get-tuple-element.14.refs_0_, bf16[88,256]{1,0:T(8,128)(2,1)S(1)} %collective-permute-done.refs_1_, bf16[88,256]{1,0:T(8,128)(2,1)S(1)} %collective-permute-done.1.refs_2_, bf16[88,256]{1,0:T(8,128)(2,1)S(1)} %collective-permute-done.2.refs_3_, ...), custom_call_target="tpu_custom_call" | custom-call | flops 3000000000 | bytes 1000000 | tf_op jit(solution)/shard_map/pallas_call | solution.py:358
  15.0 0.0 all-to-all-done.queries
  15.0 2.9 %shard_map.94 = (f32[4,1024]{1,0:T(4,128)S(1)}, bf16[8,4,1024]{2,1,0:T(4,128)(2,1)S(1)}) custom-call(f32[8,256]{1,0:T(8,128)S(1)} %get-tuple-element.13.factors, bf16[2,512,256]{2,1,0:T(8,128)(2,1)S(1)} %shard_map.92.fields, bf16[8,640]{1,0:T(8,128)(2,1)S(1)} %get-tuple-element.16.own, bf16[8,8,640]{2,1,0:T(8,128)(2,1)S(1)} %all-to-all-done.queries), custom_call_target="tpu_custom_call" | custom-call | tf_op jit(solution)/shard_map/pallas_call | solution.py:372
  17.9 6.4 %all_to_all.10.received = bf16[8,4,1024]{2,1,0:T(4,128)(2,1)S(1)} all-to-all(bf16[8,4,1024]{2,1,0:T(4,128)(2,1)S(1)} %get-tuple-element.19), channel_id=1, replica_groups={{28,20,12,4,24,16,8,0},{29,21,13,5,25,17,9,1},{30,22,14,6,26,18,10,2},{..., dimensions={0} | all-to-all | bytes 131072 | tf_op jit(solution)/shard_map/all_to_all | solution.py:383
  24.3 0.0 copy-done
  24.3 0.7 %shard_map.95 = f32[2,1,2,1024]{3,2,1,0:T(2,128)} custom-call(bf16[8,4,1024]{2,1,0:T(4,128)(2,1)S(1)} %all_to_all.10.received, f32[4,1024]{1,0:T(4,128)S(1)} %get-tuple-element.20.home, f32[2,1,2,1024]{3,2,1,0:T(2,128)S(1)} %copy-done), custom_call_target="tpu_custom_call" | custom-call | tf_op jit(solution)/shard_map/pallas_call | solution.py:386
  (1 shorter events, 0.0 us)
Async XLA Ops:
  1.6 9.7 %collective-permute-start.2 = (bf16[88,256]{1,0:T(8,128)(2,1)S(1)}, bf16[88,256]{1,0:T(8,128)(2,1)S(1)}, u32[]{:S(2)}, u32[]{:S(2)}) collective-permute-start(bf16[88,256]{1,0:T(8,128)(2,1)S(1)} %get-tuple-element.14.refs_0_), channel_id=1, source_target_pairs={{0,2},{1,3},{2,0},{3,1},{4,6},{5,7},{6,4},{7,5},{8,10},{9,11},{10,... | collective-permute-start | bytes 135176 | tf_op jit(solution)/shard_map/ppermute | solution.py:315
  5.1 6.3 %collective-permute-start.1 = (bf16[88,256]{1,0:T(8,128)(2,1)S(1)}, bf16[88,256]{1,0:T(8,128)(2,1)S(1)}, u32[]{:S(2)}, u32[]{:S(2)}) collective-permute-start(bf16[88,256]{1,0:T(8,128)(2,1)S(1)} %get-tuple-element.14.refs_0_), channel_id=1, source_target_pairs={{0,3},{1,2},{2,1},{3,0},{4,7},{5,6},{6,5},{7,4},{8,11},{9,10},{10,... | collective-permute-start | bytes 135176 | tf_op jit(solution)/shard_map/ppermute | solution.py:315
  6.5 4.9 %collective-permute-start = (bf16[88,256]{1,0:T(8,128)(2,1)S(1)}, bf16[88,256]{1,0:T(8,128)(2,1)S(1)}, u32[]{:S(2)}, u32[]{:S(2)}) collective-permute-start(bf16[88,256]{1,0:T(8,128)(2,1)S(1)} %get-tuple-element.14.refs_0_), channel_id=1, source_target_pairs={{0,1},{1,0},{2,3},{3,2},{4,5},{5,4},{6,7},{7,6},{8,9},{9,8},{10,11... | collective-permute-start | bytes 135176 | tf_op jit(solution)/shard_map/ppermute | solution.py:315
  6.7 8.3 %all-to-all-start = ((bf16[8,8,640]{2,1,0:T(8,128)(2,1)}), bf16[8,8,640]{2,1,0:T(8,128)(2,1)S(1)}, u32[]{:S(2)}, u32[]{:S(2)}) async-start(bf16[8,8,640]{2,1,0:T(8,128)(2,1)} %shard_map.93), calls=%async_computation | async-start | bytes 163840 | tf_op jit(solution)/shard_map/all_to_all | solution.py:357
  11.4 12.9 %copy-start = (f32[2,1,2,1024]{3,2,1,0:T(2,128)S(1)}, f32[2,1,2,1024]{3,2,1,0:T(2,128)}, u32[]{:S(2)}) copy-start(f32[2,1,2,1024]{3,2,1,0:T(2,128)} %momenta.1) | copy-start | bytes 49156

commit v12 on v10

--- a/solution.py
+++ b/solution.py
@@ -16,6 +16,7 @@
 OFFSET_CELLS = 32
 BANDS = GRID // OFFSET_CELLS
 REACH = STOPS + 1
+FORWARD_TABLES = 4
 INVERSE_TABLES = 6
 LANES = 128
 f32 = jnp.float32
@@ -148,10 +149,10 @@
     here = lax.axis_index("tile")
     messages = refs[:tiles]
     partial, far, out, near, gathered, densities, arrived = refs[tiles:]
-    early = near.shape[0] - INVERSE_TABLES
+    cuts = (0, FORWARD_TABLES, near.shape[0] - INVERSE_TABLES, near.shape[0])
     fetch = [
-        pltpu.make_async_copy(far.at[:early], near.at[:early], arrived.at[0]),
-        pltpu.make_async_copy(far.at[early:], near.at[early:], arrived.at[1]),
+        pltpu.make_async_copy(far.at[start:end], near.at[start:end], arrived.at[which])
+        for which, (start, end) in enumerate(zip(cuts, cuts[1:]))
     ]
     for copy in fetch:
         copy.start()
@@ -174,14 +175,15 @@
             densities[:, beam * GRID : (beam + 1) * GRID] = wide(density, 0)
 
     fetch[0].wait()
+    first = dot(long(near[0:2], 1), densities[...])
+    first = jnp.concatenate([first[:, :GRID], first[:, GRID:]], axis=0)
+    fetch[1].wait()
     alpha, beta = (
         dot(near[side], turned[0]) + dot(near[side], turned[1])
         for side, turned in (
             (side, halves(dot(gathered[...], near[side + 1]))) for side in (4, 6)
         )
     )
-    first = dot(long(near[0:2], 1), densities[...])
-    first = jnp.concatenate([first[:, :GRID], first[:, GRID:]], axis=0)
     spectra = dot(wide(first, 1), long(near[2:4], 0))
     scaled = []
     for beam in range(2):
@@ -194,7 +196,7 @@
             axis=0,
         )
         scaled.append(alpha * spectrum + beta * swapped)
-    fetch[1].wait()
+    fetch[2].wait()
     left = jnp.concatenate([long(near[10:12], 1), long(near[12:14], 1)], axis=0)
     part = dot(left, wide(jnp.concatenate(scaled, axis=1), 0)).astype(bf16)
     for axis, right in enumerate((8, 0)):
@@ -359,7 +361,7 @@
             pltpu.VMEM(tables.shape, bf16),
             pltpu.VMEM((GRID, GRID), bf16),
             pltpu.VMEM((3 * GRID, 2 * GRID), bf16),
-            pltpu.SemaphoreType.DMA((2,)),
+            pltpu.SemaphoreType.DMA((3,)),
         ],
         compiler_params=LIMIT,
         cost_estimate=pl.CostEstimate(flops=3000000000, bytes_accessed=1000000, transcendentals=0),

time: 25.2 us -> 25.1 us (level)
  no operation moved by 1% of the time
where the time goes in v12:
time: 25.1 us; the launch traced here: 24.8 us
  starting transfers between devices  9.71 us (39%)
  Pallas kernels  8.72 us (35%)
  blocking collectives  6.32 us (25%)
    all_to_all x1, blocking collectives, body(): lax.all_to_all(away, 'bunch', split_axis=0, concat_axis=0, tiled=True, ax...  6.32 us
    ppermute x3, starting transfers between devices, exchanged(): return lax.ppermute(value, axis, pairs)  5.05 us
    all_to_all x1, starting transfers between devices, body(): lax.all_to_all(copies, 'bunch', split_axis=0, concat_axis=0, tiled=True,...  4.66 us
    pallas_call x1, Pallas kernels, body(): pl.pallas_call(functools.partial(field_kernel, tiles), out_shape=jax.Shap...  3.52 us
    pallas_call x1, Pallas kernels, body(): pl.pallas_call(functools.partial(kick_kernel, count), out_shape=(jax.Shap...  2.92 us
    pallas_call x1, Pallas kernels, body(): pl.pallas_call(pack_kernel, out_shape=(jax.ShapeDtypeStruct((8, particles...  1.64 us
    pallas_call x1, Pallas kernels, body(): pl.pallas_call(functools.partial(final_kernel, count), out_shape=jax.Shap...  0.64 us
  transfers between devices with their start and end apart: 4, of which 0 were waited for; matrix products, arithmetic and copies ran while one was open for 0% of the time, Pallas kernels for 14%

profile of v12, /device:TPU:0, one launch (start us, length us, event | category | flops | bytes accessed | tf_op | source)
XLA Modules:
  0.0 24.8 jit_solution(13959906837328406873)
XLA Ops:
  0.0 1.6 %shard_map.91 = (bf16[8,640]{1,0:T(8,128)(2,1)S(1)}, bf16[8,8,640]{2,1,0:T(8,128)(2,1)S(1)}, bf16[88,256]{1,0:T(8,128)(2,1)S(1)}, f32[8,256]{1,0:T(8,128)S(1)}, ...) custom-call(s32[2,1,2,1024]{3,2,1,0:T(2,128)} %cells.1, bf16[2,1024]{1,0:T(2,128)(2,1)} %bitcast.5, s32[1,2]{1,0:T(1,128)} %bitcast.7, ...), custom_call_target="tpu_custom_call" | custom-call | tf_op jit(solution)/shard_map/pallas_call | solution.py:321
  1.6 3.5 %collective-permute-start.2 = (bf16[88,256]{1,0:T(8,128)(2,1)S(1)}, bf16[88,256]{1,0:T(8,128)(2,1)S(1)}, u32[]{:S(2)}, u32[]{:S(2)}) collective-permute-start(bf16[88,256]{1,0:T(8,128)(2,1)S(1)} %get-tuple-element.14.refs_0_), channel_id=1, source_target_pairs={{0,2},{1,3},{2,0},{3,1},{4,6},{5,7},{6,4},{7,5},{8,10},{9,11},{10,... | collective-permute-start | bytes 135176 | tf_op jit(solution)/shard_map/ppermute | solution.py:312
  5.1 1.3 %collective-permute-start.1 = (bf16[88,256]{1,0:T(8,128)(2,1)S(1)}, bf16[88,256]{1,0:T(8,128)(2,1)S(1)}, u32[]{:S(2)}, u32[]{:S(2)}) collective-permute-start(bf16[88,256]{1,0:T(8,128)(2,1)S(1)} %get-tuple-element.14.refs_0_), channel_id=1, source_target_pairs={{0,3},{1,2},{2,1},{3,0},{4,7},{5,6},{6,5},{7,4},{8,11},{9,10},{10,... | collective-permute-start | bytes 135176 | tf_op jit(solution)/shard_map/ppermute | solution.py:312
  6.5 0.2 collective-permute-start
  6.7 4.7 %all-to-all-start = ((bf16[8,8,640]{2,1,0:T(8,128)(2,1)}), bf16[8,8,640]{2,1,0:T(8,128)(2,1)S(1)}, u32[]{:S(2)}, u32[]{:S(2)}) async-start(bf16[8,8,640]{2,1,0:T(8,128)(2,1)} %shard_map.93), calls=%async_computation | async-start | bytes 163840 | tf_op jit(solution)/shard_map/all_to_all | solution.py:354
  11.4 0.0 collective-permute-done.2.refs_3_
  11.4 0.0 collective-permute-done.1.refs_2_
  11.4 0.0 collective-permute-done.refs_1_
  11.4 0.0 copy-start
  11.4 3.5 %shard_map.92.fields = bf16[2,512,256]{2,1,0:T(8,128)(2,1)S(1)} custom-call(bf16[88,256]{1,0:T(8,128)(2,1)S(1)} %get-tuple-element.14.refs_0_, bf16[88,256]{1,0:T(8,128)(2,1)S(1)} %collective-permute-done.refs_1_, bf16[88,256]{1,0:T(8,128)(2,1)S(1)} %collective-permute-done.1.refs_2_, bf16[88,256]{1,0:T(8,128)(2,1)S(1)} %collective-permute-done.2.refs_3_, ...), custom_call_target="tpu_custom_call" | custom-call | flops 3000000000 | bytes 1000000 | tf_op jit(solution)/shard_map/pallas_call | solution.py:355
  14.9 0.0 all-to-all-done.queries
  14.9 2.9 %shard_map.94 = (f32[4,1024]{1,0:T(4,128)S(1)}, bf16[8,4,1024]{2,1,0:T(4,128)(2,1)S(1)}) custom-call(f32[8,256]{1,0:T(8,128)S(1)} %get-tuple-element.13.factors, bf16[2,512,256]{2,1,0:T(8,128)(2,1)S(1)} %shard_map.92.fields, bf16[8,640]{1,0:T(8,128)(2,1)S(1)} %get-tuple-element.16.own, bf16[8,8,640]{2,1,0:T(8,128)(2,1)S(1)} %all-to-all-done.queries), custom_call_target="tpu_custom_call" | custom-call | tf_op jit(solution)/shard_map/pallas_call | solution.py:369
  17.9 6.3 %all_to_all.10.received = bf16[8,4,1024]{2,1,0:T(4,128)(2,1)S(1)} all-to-all(bf16[8,4,1024]{2,1,0:T(4,128)(2,1)S(1)} %get-tuple-element.19), channel_id=1, replica_groups={{28,24,20,16,12,8,4,0},{29,25,21,17,13,9,5,1},{30,26,22,18,14,10,6,2},{..., dimensions={0} | all-to-all | bytes 131072 | tf_op jit(solution)/shard_map/all_to_all | solution.py:379
  24.2 0.0 copy-done
  24.2 0.6 %shard_map.95 = f32[2,1,2,1024]{3,2,1,0:T(2,128)} custom-call(bf16[8,4,1024]{2,1,0:T(4,128)(2,1)S(1)} %all_to_all.10.received, f32[4,1024]{1,0:T(4,128)S(1)} %get-tuple-element.20.home, f32[2,1,2,1024]{3,2,1,0:T(2,128)S(1)} %copy-done), custom_call_target="tpu_custom_call" | custom-call | tf_op jit(solution)/shard_map/pallas_call | solution.py:380
  (1 shorter events, 0.0 us)
Async XLA Ops:
  1.6 9.7 %collective-permute-start.2 = (bf16[88,256]{1,0:T(8,128)(2,1)S(1)}, bf16[88,256]{1,0:T(8,128)(2,1)S(1)}, u32[]{:S(2)}, u32[]{:S(2)}) collective-permute-start(bf16[88,256]{1,0:T(8,128)(2,1)S(1)} %get-tuple-element.14.refs_0_), channel_id=1, source_target_pairs={{0,2},{1,3},{2,0},{3,1},{4,6},{5,7},{6,4},{7,5},{8,10},{9,11},{10,... | collective-permute-start | bytes 135176 | tf_op jit(solution)/shard_map/ppermute | solution.py:312
  5.1 6.3 %collective-permute-start.1 = (bf16[88,256]{1,0:T(8,128)(2,1)S(1)}, bf16[88,256]{1,0:T(8,128)(2,1)S(1)}, u32[]{:S(2)}, u32[]{:S(2)}) collective-permute-start(bf16[88,256]{1,0:T(8,128)(2,1)S(1)} %get-tuple-element.14.refs_0_), channel_id=1, source_target_pairs={{0,3},{1,2},{2,1},{3,0},{4,7},{5,6},{6,5},{7,4},{8,11},{9,10},{10,... | collective-permute-start | bytes 135176 | tf_op jit(solution)/shard_map/ppermute | solution.py:312
  6.5 4.9 %collective-permute-start = (bf16[88,256]{1,0:T(8,128)(2,1)S(1)}, bf16[88,256]{1,0:T(8,128)(2,1)S(1)}, u32[]{:S(2)}, u32[]{:S(2)}) collective-permute-start(bf16[88,256]{1,0:T(8,128)(2,1)S(1)} %get-tuple-element.14.refs_0_), channel_id=1, source_target_pairs={{0,1},{1,0},{2,3},{3,2},{4,5},{5,4},{6,7},{7,6},{8,9},{9,8},{10,11... | collective-permute-start | bytes 135176 | tf_op jit(solution)/shard_map/ppermute | solution.py:312
  6.7 8.2 %all-to-all-start = ((bf16[8,8,640]{2,1,0:T(8,128)(2,1)}), bf16[8,8,640]{2,1,0:T(8,128)(2,1)S(1)}, u32[]{:S(2)}, u32[]{:S(2)}) async-start(bf16[8,8,640]{2,1,0:T(8,128)(2,1)} %shard_map.93), calls=%async_computation | async-start | bytes 163840 | tf_op jit(solution)/shard_map/all_to_all | solution.py:354
  11.4 12.8 %copy-start = (f32[2,1,2,1024]{3,2,1,0:T(2,128)S(1)}, f32[2,1,2,1024]{3,2,1,0:T(2,128)}, u32[]{:S(2)}) copy-start(f32[2,1,2,1024]{3,2,1,0:T(2,128)} %momenta.1) | copy-start | bytes 49156
